TPU v7x, 128 devices: a whole 4x4x4 slice. The times are simulated.
128 devices in a mesh: req: 32 (over y, x, core), tp: 4 (over z).
Axes of the slice: x: 4, y: 4, z: 4, core: 2. Of those that a mesh axis runs over, the one named last changes fastest.
Arguments:
- hidden: bfloat16 [32, 8192], P(None, 'req')
- attn_gain: bfloat16 [2, 8192], P(None, 'req'), may hold values from 0.5 to 1.5
- q_weight: bfloat16 [2, 8192, 4096], P(None, 'req', 'tp'), may hold values from -0.0625 to 0.0625
- o_weight: bfloat16 [2, 4096, 8192], P(None, 'tp', 'req'), may hold values from -0.09375 to 0.09375
- ffn_gain: bfloat16 [2, 8192], P(None, 'req'), may hold values from 0.5 to 1.5
- gate_weight: bfloat16 [2, 8192, 14336], P(None, 'req', 'tp'), may hold values from -0.0625 to 0.0625
- up_weight: bfloat16 [2, 8192, 14336], P(None, 'req', 'tp'), may hold values from -0.0625 to 0.0625
- down_weight: bfloat16 [2, 14336, 8192], P(None, 'tp', 'req'), may hold values from -0.046875 to 0.046875
- kv_pool: bfloat16 [2, 1024, 4, 2, 128, 128], P(None, 'req', 'tp')
- block_home: int32 [32, 32], P('req'), may hold values from 0 to 1023, as said below
- chosen: int32 [2, 32, 4, 24], P(None, 'req', 'tp'), may hold values from 0 to 31, as said below
- chosen_count: int32 [2, 32, 4], P(None, 'req', 'tp'), may hold values from 6 to 24
Outputs:
- new_hidden: bfloat16 [32, 8192], P(None, 'req')
Inputs may be any that keep to these rules, and one draw needn't show every extreme that they name: `block_home`: pool slot p lies on store device p // 32 of req; every slot belongs to exactly one block of one request, and every request has exactly 1 block on each store device. `chosen`: entries of a list are distinct. The used entries of a list are the one block of some store devices and some blocks of one more; entries from chosen_count on are ignored.
All inputs are finite; a program needn't handle non-finite values.
Results may differ from a plain program's by a relative error of at most 0.038.
Values may be sent and summed in bfloat16 or wider, within the bound.
No kernel may reach another device: no remote copies, remote signals or barrier semaphores. Data moves between devices by JAX's collectives and lax.ppermute only.
A program may use at most 64 MiB of HBM per device.

v0:
```python
import math

import jax
import jax.numpy as jnp
from jax import lax
from jax.sharding import PartitionSpec as P

D = 8192
LAYERS = 2


MASK_FILL = -1e30
EPSILON = 1e-05


def rotary(queries, position):
    head_size = queries.shape[-1]
    half_size = head_size // 2
    freq_idx = jnp.arange(half_size).astype(queries.dtype)
    angles = position * jnp.exp(freq_idx * (-2.0 * math.log(500000.0) / head_size))
    cosine = jnp.cos(angles)
    sine_part = jnp.sin(angles)
    lower_half = queries[..., :half_size]
    upper_half = queries[..., half_size:]
    return jnp.concatenate(
        [
            lower_half * cosine - upper_half * sine_part,
            upper_half * cosine + lower_half * sine_part,
        ],
        axis=-1,
    )


def local_squares(current):
    widened = current.astype(jnp.float32)
    return jnp.sum(widened * widened, axis=1)


def apply_gain(current, gain):
    return (current.astype(jnp.float32) * gain.astype(jnp.float32)).astype(jnp.bfloat16)


def inverse_of(squares):
    return lax.rsqrt(squares / D + EPSILON)


def summed_inverse(current):
    return inverse_of(lax.psum(local_squares(current), "req"))


def sum_over_heads(partial_sum):
    return lax.psum(partial_sum, "tp")


def block_stats(queries, blocks, valid):
    scores = jnp.einsum(
        "sigeh,sigqbh->sigeqb", queries, blocks[:, :, :, :, 0], preferred_element_type=jnp.float32
    )
    block_max = jnp.max(scores, axis=5)
    exp_terms = jnp.exp(scores - block_max[..., None])
    block_sum = jnp.sum(exp_terms, axis=5)
    block_acc = jnp.einsum(
        "sigeqb,sigqbh->sigeqh",
        exp_terms.astype(jnp.bfloat16),
        blocks[:, :, :, :, 1],
        preferred_element_type=jnp.float32,
    )
    block_max = jnp.where(valid[:, :, :, None, :], block_max, MASK_FILL)
    return (block_max, block_sum, block_acc)


def combine(block_max, block_sum, block_acc, axes):
    overall = jnp.max(block_max, axis=axes, keepdims=True)
    rescale = jnp.exp(block_max - overall)
    numerator = jnp.sum(rescale[..., None] * block_acc, axis=axes)
    denominator = jnp.sum(rescale * block_sum, axis=axes)
    return (jnp.squeeze(overall, axes), denominator, numerator)


def shards(
    hidden,
    attn_gain,
    q_weight,
    o_weight,
    ffn_gain,
    gate_weight,
    up_weight,
    down_weight,
    kv_pool,
    block_home,
    chosen,
    chosen_count,
):
    n_req = lax.axis_size("req")
    req_dev = chosen.shape[1]
    heads_dev = chosen.shape[2]
    most_sel = chosen.shape[3]
    pool_dev = kv_pool.shape[1]
    head_size = kv_pool.shape[5]
    per_store = block_home.shape[1] // n_req
    position = float(block_home.shape[1] * kv_pool.shape[4] - 1)
    own_start = lax.axis_index("req") * req_dev
    row_index = jnp.arange(req_dev)[:, None, None]
    entries = jnp.arange(most_sel)
    store_ids = jnp.arange(n_req)[:, None, None, None, None]
    slot_ids = jnp.arange(per_store)[None, None, None, :, None]
    head_index = jnp.arange(heads_dev)[None, None, :, None]
    current = hidden
    for layer_no in range(LAYERS):
        scaled = apply_gain(current, attn_gain[layer_no])
        inv_all = summed_inverse(current)
        rows_in = scaled
        product = jnp.dot(rows_in, q_weight[layer_no], preferred_element_type=jnp.float32)
        summed = lax.psum_scatter(product, "req", scatter_dimension=0, tiled=True)
        inv_own = lax.dynamic_slice_in_dim(inv_all, own_start, req_dev, 0)
        queries = (summed * inv_own[:, None]).reshape(req_dev, heads_dev, -1, head_size)
        queries = (rotary(queries, position) * head_size ** (-0.5)).astype(jnp.bfloat16)
        pool_ids = block_home[row_index, chosen[layer_no]]
        home_store = pool_ids // pool_dev
        home_slot = pool_ids % pool_dev
        used_mask = entries[None, None, :] < chosen_count[layer_no][:, :, None]
        earlier = (
            (home_store[..., :, None] == home_store[..., None, :])
            & used_mask[..., None, :]
            & (entries[None, :] < entries[:, None])
        )
        rank = jnp.sum(earlier.astype(jnp.int32), axis=-1)
        match = (
            (home_store[None, :, :, None, :] == store_ids)
            & (rank[None, :, :, None, :] == slot_ids)
            & used_mask[None, :, :, None, :]
        )
        wanted = jnp.sum(jnp.where(match, home_slot[None, :, :, None, :] + 1, 0), axis=4) - 1
        received_ids = lax.all_to_all(wanted, "req", split_axis=0, concat_axis=0, tiled=True)
        served = kv_pool[layer_no][jnp.maximum(received_ids, 0), head_index]
        fetched = lax.all_to_all(served, "req", split_axis=0, concat_axis=0, tiled=True)
        spread = jnp.broadcast_to(queries[None], (n_req,) + queries.shape)
        stats = block_stats(spread, fetched, wanted >= 0)
        overall, denominator, numerator = combine(stats[0], stats[1], stats[2], (0, 4))
        context = (numerator / denominator[..., None]).astype(jnp.bfloat16).reshape(req_dev, -1)
        attn_part = jnp.dot(
            lax.all_gather(context, "req", axis=0, tiled=True),
            o_weight[layer_no],
            preferred_element_type=jnp.float32,
        )
        attended = (current.astype(jnp.float32) + sum_over_heads(attn_part)).astype(jnp.bfloat16)
        scaled = apply_gain(attended, ffn_gain[layer_no])
        inv_all = summed_inverse(attended)
        gate = jnp.dot(scaled, gate_weight[layer_no], preferred_element_type=jnp.float32)
        up_part = jnp.dot(scaled, up_weight[layer_no], preferred_element_type=jnp.float32)
        payload = (gate, up_part)
        totals = lax.psum((payload[0], payload[1]), "req")
        gate = totals[0] * inv_all[:, None]
        up_part = totals[1] * inv_all[:, None]
        activated = (jax.nn.silu(gate) * up_part).astype(jnp.bfloat16)
        ffn_part = jnp.dot(activated, down_weight[layer_no], preferred_element_type=jnp.float32)
        current = (attended.astype(jnp.float32) + sum_over_heads(ffn_part)).astype(jnp.bfloat16)
    return current


def solution(mesh):
    return jax.shard_map(
        shards,
        mesh=mesh,
        in_specs=(
            P(None, "req"),
            P(None, "req"),
            P(None, "req", "tp"),
            P(None, "tp", "req"),
            P(None, "req"),
            P(None, "req", "tp"),
            P(None, "req", "tp"),
            P(None, "tp", "req"),
            P(None, "req", "tp", None, None, None),
            P("req", None),
            P(None, "req", "tp", None),
            P(None, "req", "tp"),
        ),
        out_specs=P(None, "req"),
        check_vma=False,
    )
```

profile of v0, /device:TPU:0, one launch (start us, length us, event | category | flops | bytes accessed | tf_op | source)
XLA Modules:
  0.0 630.1 jit_solution(11722193057288461711)
XLA Ops:
  11.0 7.4 %all-to-all-start = ((s32[32,1,1,1]{3,2,1,0:T(1,128)}), s32[32,1,1,1]{3,2,1,0:T(1,128)S(1)}, u32[]{:S(2)}, u32[]{:S(2)}) async-start(s32[32,1,1,1]{3,2,1,0:T(1,128)} %copy.38), calls=%async_computation | async-start | bytes 32768 | tf_op jit(solution)/shard_map/all_to_all | solution.py:134
  18.4 4.1 slice_bitcast_fusion.1
  25.8 6.6 %all-to-all-start.2 = ((s32[32,1,1,1]{3,2,1,0:T(1,128)}), s32[32,1,1,1]{3,2,1,0:T(1,128)S(1)}, u32[]{:S(2)}, u32[]{:S(2)}) async-start(s32[32,1,1,1]{3,2,1,0:T(1,128)} %copy.43), calls=%async_computation.2 | async-start | bytes 32768 | tf_op jit(solution)/shard_map/all_to_all | solution.py:134
  33.0 3.7 gather_fusion.1
  36.7 2.9 all-to-all-done.2
  39.6 4.9 all-to-all-start.1
  46.2 82.1 %psum.84 = f32[32]{0:T(128)S(1)} all-reduce(f32[32]{0:T(128)S(1)} %fusion.53), channel_id=1, replica_groups=mesh['req'=32,'tp'=4] {'req'}, use_global_device_ids=true, to_apply=%region_4.5 | all-reduce | flops 32 | bytes 256 | tf_op jit(solution)/shard_map/psum | solution.py:48
  131.8 24.4 %all-reduce.13.cloned.1.call-done = f32[32,1024]{1,0:T(8,128)} async-done(((f32[32,1024]{1,0:T(8,128)}), f32[32,1024]{1,0:T(8,128)}) %all-reduce.13.cloned.1.call-update) | async-done | bytes 131088
  158.5 5.4 all-to-all-start.3
  168.2 38.5 %all-gather = bf16[32,1,1024]{2,1,0:T(2,128)(2,1)S(1)} all-gather(bf16[1,1,1024]{2,1,0:T(2,128)(2,1)S(1)} %convert_bitcast_fusion.1), channel_id=1, replica_groups=mesh['req'=32,'tp'=4] {'req'}, dimensions={0}, use_global_device_ids=true | all-gather | bytes 67584 | tf_op jit(solution)/shard_map/all_gather | solution.py:142
  206.9 17.3 %psum.85 = f32[32,256]{1,0:T(8,128)S(1)} all-reduce(f32[32,256]{1,0:T(8,128)S(1)} %fusion.28), channel_id=1, replica_groups=mesh['req'=32,'tp'=4] {'tp'}, use_global_device_ids=true, to_apply=%region_10.11 | all-reduce | flops 8192 | bytes 65536 | tf_op jit(solution)/shard_map/psum | solution.py:52
  224.3 2.7 fusion.8
  229.7 62.7 %psum.87 = f32[32]{0:T(128)S(1)} all-reduce(f32[32]{0:T(128)S(1)} %get-tuple-element.15), channel_id=1, replica_groups=mesh['req'=32,'tp'=4] {'req'}, use_global_device_ids=true, to_apply=%region_13.14 | all-reduce | flops 32 | bytes 256 | tf_op jit(solution)/shard_map/psum | solution.py:48
  292.5 39.3 %all-reduce.19.cloned.1.call-done = (f32[32,3584]{1,0:T(8,128)}, f32[32,3584]{1,0:T(8,128)}) async-done(((f32[32,3584]{1,0:T(8,128)}, f32[32,3584]{1,0:T(8,128)}), (f32[32,3584]{1,0:T(8,128)}, f32[32,3584]{1,0:T(8,128)})) %all-reduce.19.cloned.1.call-update) | async-done | bytes 917520 | tf_op jit(solution)/shard_map/psum | solution.py:152
  334.1 17.3 %psum.89 = f32[32,256]{1,0:T(8,128)S(1)} all-reduce(f32[32,256]{1,0:T(8,128)S(1)} %fusion.6), channel_id=1, replica_groups=mesh['req'=32,'tp'=4] {'tp'}, use_global_device_ids=true, to_apply=%region_15.16 | all-reduce | flops 8192 | bytes 65536 | tf_op jit(solution)/shard_map/psum | solution.py:52
  352.4 62.7 %psum.90 = f32[32]{0:T(128)S(1)} all-reduce(f32[32]{0:T(128)S(1)} %get-tuple-element.13), channel_id=1, replica_groups=mesh['req'=32,'tp'=4] {'req'}, use_global_device_ids=true, to_apply=%region_20.21 | all-reduce | flops 32 | bytes 256 | tf_op jit(solution)/shard_map/psum | solution.py:48
  415.7 34.1 %all-reduce.15.cloned.1.call-done = f32[32,1024]{1,0:T(8,128)} async-done(((f32[32,1024]{1,0:T(8,128)}), f32[32,1024]{1,0:T(8,128)}) %all-reduce.15.cloned.1.call-update) | async-done | bytes 131088
  453.6 24.9 %all-gather.1 = bf16[32,1,1024]{2,1,0:T(2,128)(2,1)S(1)} all-gather(bf16[1,1,1024]{2,1,0:T(2,128)(2,1)S(1)} %convert_bitcast_fusion), channel_id=1, replica_groups=mesh['req'=32,'tp'=4] {'req'}, dimensions={0}, use_global_device_ids=true | all-gather | bytes 67584 | tf_op jit(solution)/shard_map/all_gather | solution.py:142
  479.7 17.3 %psum.91 = f32[32,256]{1,0:T(8,128)S(1)} all-reduce(f32[32,256]{1,0:T(8,128)S(1)} %fusion.24), channel_id=1, replica_groups=mesh['req'=32,'tp'=4] {'tp'}, use_global_device_ids=true, to_apply=%region_26.27 | all-reduce | flops 8192 | bytes 65536 | tf_op jit(solution)/shard_map/psum | solution.py:52
  497.1 2.7 fusion.2
  499.8 2.7 fusion.4
  502.5 62.7 %psum.93 = f32[32]{0:T(128)S(1)} all-reduce(f32[32]{0:T(128)S(1)} %get-tuple-element.9), channel_id=1, replica_groups=mesh['req'=32,'tp'=4] {'req'}, use_global_device_ids=true, to_apply=%region_29.30 | all-reduce | flops 32 | bytes 256 | tf_op jit(solution)/shard_map/psum | solution.py:48
  565.2 38.2 %all-reduce.17.cloned.1.call-done = (f32[32,3584]{1,0:T(8,128)}, f32[32,3584]{1,0:T(8,128)}) async-done(((f32[32,3584]{1,0:T(8,128)}, f32[32,3584]{1,0:T(8,128)}), (f32[32,3584]{1,0:T(8,128)}, f32[32,3584]{1,0:T(8,128)})) %all-reduce.17.cloned.1.call-update) | async-done | bytes 917520 | tf_op jit(solution)/shard_map/psum | solution.py:152
  605.6 17.3 %psum.95 = f32[32,256]{1,0:T(8,128)S(1)} all-reduce(f32[32,256]{1,0:T(8,128)S(1)} %fusion), channel_id=1, replica_groups=mesh['req'=32,'tp'=4] {'tp'}, use_global_device_ids=true, to_apply=%region_31.32 | all-reduce | flops 8192 | bytes 65536 | tf_op jit(solution)/shard_map/psum | solution.py:52
  (97 shorter events, 34.8 us)
Async XLA Ops:
  6.5 2.1 copy-start
  11.0 14.8 %all-to-all-start = ((s32[32,1,1,1]{3,2,1,0:T(1,128)}), s32[32,1,1,1]{3,2,1,0:T(1,128)S(1)}, u32[]{:S(2)}, u32[]{:S(2)}) async-start(s32[32,1,1,1]{3,2,1,0:T(1,128)} %copy.38), calls=%async_computation | async-start | bytes 32768 | tf_op jit(solution)/shard_map/all_to_all | solution.py:134
  18.4 5.7 copy-start.3
  25.8 13.8 %all-to-all-start.2 = ((s32[32,1,1,1]{3,2,1,0:T(1,128)}), s32[32,1,1,1]{3,2,1,0:T(1,128)S(1)}, u32[]{:S(2)}, u32[]{:S(2)}) async-start(s32[32,1,1,1]{3,2,1,0:T(1,128)} %copy.43), calls=%async_computation.2 | async-start | bytes 32768 | tf_op jit(solution)/shard_map/all_to_all | solution.py:134
  39.6 5.0 copy-start.1
  39.6 5.0 copy-start.2
  39.6 5.9 copy-start.6
  39.6 89.4 %copy-start.4 = (bf16[2,256]{1,0:T(2,128)(2,1)S(1)}, bf16[2,256]{1,0:T(2,128)(2,1)}, u32[]{:S(2)}) copy-start(bf16[2,256]{1,0:T(2,128)(2,1)} %param.16) | copy-start | bytes 3076
  39.6 118.9 %all-to-all-start.1 = ((bf16[32,1,1,1,2,128,128]{6,5,4,3,2,1,0:T(8,128)(2,1)}), bf16[32,1,1,1,2,128,128]{6,5,4,3,2,1,0:T(8,128)(2,1)}, u32[]{:S(2)}, u32[]{:S(2)}) async-start(bf16[32,1,1,1,2,128,128]{6,5,4,3,2,1,0:T(8,128)(2,1)} %bitcast.16), calls=%async_computation.1 | async-start | bytes 4194304 | tf_op jit(solution)/shard_map/all_to_all | solution.py:136
  44.5 111.7 %all-reduce.13.cloned.1.call-start = ((), (), s32[]{:S(2)}) async-start(), calls=%async_computation.4 | async-start | bytes 262144
  158.5 293.4 %all-to-all-start.3 = ((bf16[32,1,1,1,2,128,128]{6,5,4,3,2,1,0:T(8,128)(2,1)}), bf16[32,1,1,1,2,128,128]{6,5,4,3,2,1,0:T(8,128)(2,1)S(1)}, u32[]{:S(2)}, u32[]{:S(2)}) async-start(bf16[32,1,1,1,2,128,128]{6,5,4,3,2,1,0:T(8,128)(2,1)} %bitcast.45), calls=%async_computation.3 | async-start | bytes 4194304 | tf_op jit(solution)/shard_map/all_to_all | solution.py:136
  163.9 167.9 %all-reduce.19.cloned.1.call-start = ((), (), s32[]{:S(2)}) async-start(), calls=%async_computation.7 | async-start | bytes 1835008 | tf_op jit(solution)/shard_map/psum | solution.py:152
  163.9 42.7 %copy-start.5 = (bf16[2,1024,256]{2,1,0:T(8,128)(2,1)S(1)}, bf16[2,1024,256]{2,1,0:T(8,128)(2,1)}, u32[]{:S(2)}) copy-start(bf16[2,1024,256]{2,1,0:T(8,128)(2,1)} %param.15) | copy-start | bytes 3145732
  229.7 220.1 %all-reduce.15.cloned.1.call-start = ((), (), s32[]{:S(2)}) async-start(), calls=%async_computation.5 | async-start | bytes 262144
  352.3 251.1 %all-reduce.17.cloned.1.call-start = ((), (), s32[]{:S(2)}) async-start(), calls=%async_computation.6 | async-start | bytes 1835008 | tf_op jit(solution)/shard_map/psum | solution.py:152
Sparse Core Ops, SparseCore 0:
  48.6 107.6 all-reduce.12
  229.8 101.9 all-reduce.18
  352.4 97.3 all-reduce.14
  502.6 100.7 all-reduce.16
where the time goes:
time: 632 us; the launch traced here: 630 us
  blocking collectives  403 us (64%)
  waiting for transfers between devices  140 us (22%)
  starting transfers between devices  24.5 us (4%)
  matrix products  23.3 us (4%)
  local copies, waits for them, and re-layouts  16.2 us (3%)
  between operations  13.4 us (2%)
  other arithmetic  10.3 us (2%)
    psum x4, blocking collectives, summed_inverse(): return inverse_of(lax.psum(local_squares(current), 'req'))  270 us
    psum x2, waiting for transfers between devices, shards(): totals = lax.psum((payload[0], payload[1]), 'req')  77.5 us
    psum x4, blocking collectives, sum_over_heads(): return lax.psum(partial_sum, 'tp')  69 us
    all_gather x2, blocking collectives, shards(): lax.all_gather(context, 'req', axis=0, tiled=True)  63.4 us
    unnamed x6, waiting for transfers between devices  58.6 us
    all_to_all x2, starting transfers between devices, shards(): lax.all_to_all(wanted, 'req', split_axis=0, concat_axis=0, tiled=True)  14 us
  transfers between devices with their start and end apart: 8, of which 6 were waited for; matrix products, arithmetic and copies ran while one was open for 5% of the time, Pallas kernels for 0%

commit v1 on v0

v1 whole, which is shorter than its diff:
```python
import math

import jax
import jax.numpy as jnp
from jax import lax
from jax.sharding import PartitionSpec as P

D = 8192
LAYERS = 2

MASK_FILL = -1e30
EPSILON = 1e-05


def rotary(queries, position):
    head_size = queries.shape[-1]
    half_size = head_size // 2
    freq_idx = jnp.arange(half_size).astype(queries.dtype)
    angles = position * jnp.exp(freq_idx * (-2.0 * math.log(500000.0) / head_size))
    cosine = jnp.cos(angles)
    sine_part = jnp.sin(angles)
    lower_half = queries[..., :half_size]
    upper_half = queries[..., half_size:]
    return jnp.concatenate(
        [
            lower_half * cosine - upper_half * sine_part,
            upper_half * cosine + lower_half * sine_part,
        ],
        axis=-1,
    )


def apply_gain(current, gain):
    return (current.astype(jnp.float32) * gain.astype(jnp.float32)).astype(jnp.bfloat16)


def split_squares(current):
    widened = current.astype(jnp.float32)
    squares = jnp.sum(widened * widened, axis=1)
    high = squares.astype(jnp.bfloat16)
    low = (squares - high.astype(jnp.float32)).astype(jnp.bfloat16)
    return high, low


def exchange(array):
    return lax.all_to_all(array, "req", split_axis=0, concat_axis=0, tiled=True)


def with_squares(partial_sums, current, lanes, rows):
    requests, width = partial_sums.shape
    body = partial_sums.astype(jnp.bfloat16).reshape(requests, width // lanes, lanes)
    high, low = split_squares(current)
    spare = rows - width // lanes
    tail = jnp.zeros((requests, spare, lanes), jnp.bfloat16)
    tail = tail.at[:, 0, :].set(high[:, None]).at[:, 1, :].set(low[:, None])
    return jnp.concatenate([body, tail], axis=1)


def reduce_request(partial_sums, current, rows):
    width = partial_sums.shape[1]
    received = exchange(with_squares(partial_sums, current, 128, rows))
    totals = jnp.sum(received.astype(jnp.float32), axis=0)
    used = width // 128
    squares = totals[used, 0] + totals[used + 1, 0]
    return totals[:used], lax.rsqrt(squares / D + EPSILON)


def gather_requests(own):
    n_req = lax.axis_size("req")
    return exchange(jnp.broadcast_to(own[None], (n_req,) + own.shape))


def sum_over_heads(partial_sum):
    n_tp = lax.axis_size("tp")
    total = partial_sum
    for shift in (2, 1, 3):
        pairs = [(i, (i + shift) % n_tp) for i in range(n_tp)]
        total = total + lax.ppermute(partial_sum, "tp", pairs)
    return total


def shards(
    hidden,
    attn_gain,
    q_weight,
    o_weight,
    ffn_gain,
    gate_weight,
    up_weight,
    down_weight,
    kv_pool,
    block_home,
    chosen,
    chosen_count,
):
    n_req = lax.axis_size("req")
    most_sel = chosen.shape[3]
    pool_dev = kv_pool.shape[1]
    head_size = kv_pool.shape[5]
    position = float(block_home.shape[1] * kv_pool.shape[4] - 1)
    store_ids = jnp.arange(n_req)
    homes = block_home[0]
    at_store = homes[None, :] // pool_dev == store_ids[:, None]
    slots = jnp.sum(jnp.where(at_store, homes[None, :] % pool_dev, 0), axis=1)
    wanted = exchange(slots.reshape(n_req, 1, 1).astype(jnp.int32)).reshape(n_req)
    fetched = [
        exchange(jnp.take(kv_pool[layer_no, :, 0], wanted, axis=0)) for layer_no in range(LAYERS)
    ]
    valid = []
    for layer_no in range(LAYERS):
        stores = homes[chosen[layer_no, 0, 0]] // pool_dev
        used = jnp.arange(most_sel) < chosen_count[layer_no, 0, 0]
        valid.append(jnp.any((stores[None, :] == store_ids[:, None]) & used[None, :], axis=1))
    current = hidden
    for layer_no in range(LAYERS):
        scaled = apply_gain(current, attn_gain[layer_no])
        product = jnp.dot(scaled, q_weight[layer_no], preferred_element_type=jnp.float32)
        totals, inv = reduce_request(product, current, 16)
        queries = (rotary(totals * inv, position) * head_size ** (-0.5)).astype(jnp.bfloat16)
        blocks = fetched[layer_no]
        scores = jnp.einsum("eh,sbh->seb", queries, blocks[:, 0], preferred_element_type=jnp.float32)
        block_max = jnp.max(scores, axis=2)
        terms = jnp.exp(scores - block_max[..., None])
        block_sum = jnp.sum(terms, axis=2)
        block_acc = jnp.einsum(
            "seb,sbh->seh", terms.astype(jnp.bfloat16), blocks[:, 1], preferred_element_type=jnp.float32
        )
        block_max = jnp.where(valid[layer_no][:, None], block_max, MASK_FILL)
        rescale = jnp.exp(block_max - jnp.max(block_max, axis=0, keepdims=True))
        numerator = jnp.sum(rescale[..., None] * block_acc, axis=0)
        denominator = jnp.sum(rescale * block_sum, axis=0)
        context = (numerator / denominator[..., None]).astype(jnp.bfloat16)
        contexts = gather_requests(context).reshape(n_req, -1)
        attn_part = jnp.dot(contexts, o_weight[layer_no], preferred_element_type=jnp.float32)
        attended = (current.astype(jnp.float32) + sum_over_heads(attn_part)).astype(jnp.bfloat16)
        scaled = apply_gain(attended, ffn_gain[layer_no])
        gate = jnp.dot(scaled, gate_weight[layer_no], preferred_element_type=jnp.float32)
        up_part = jnp.dot(scaled, up_weight[layer_no], preferred_element_type=jnp.float32)
        totals, inv = reduce_request(jnp.concatenate([gate, up_part], axis=1), attended, 64)
        half = totals.shape[0] // 2
        activated = (jax.nn.silu(totals[:half] * inv) * (totals[half:] * inv)).astype(jnp.bfloat16)
        rows = gather_requests(activated).reshape(n_req, -1)
        ffn_part = jnp.dot(rows, down_weight[layer_no], preferred_element_type=jnp.float32)
        current = (attended.astype(jnp.float32) + sum_over_heads(ffn_part)).astype(jnp.bfloat16)
    return current


def solution(mesh):
    return jax.shard_map(
        shards,
        mesh=mesh,
        in_specs=(
            P(None, "req"),
            P(None, "req"),
            P(None, "req", "tp"),
            P(None, "tp", "req"),
            P(None, "req"),
            P(None, "req", "tp"),
            P(None, "req", "tp"),
            P(None, "tp", "req"),
            P(None, "req", "tp", None, None, None),
            P("req", None),
            P(None, "req", "tp", None),
            P(None, "req", "tp"),
        ),
        out_specs=P(None, "req"),
        check_vma=False,
    )
```

time: 632 us -> 263 us (0.42)
  blocking collectives: 403 us -> 77.9 us
  waiting for transfers between devices: 140 us -> 61.9 us
  starting transfers between devices: 24.5 us -> 50.5 us
  local copies, waits for them, and re-layouts: 16.2 us -> 38.4 us
  matrix products: 23.3 us -> 15 us
  between operations: 13.4 us -> 5.72 us
    psum x8 -> x0, blocking collectives: 339 us -> none  [the longest x4 270 us: summed_inverse(): return inverse_of(lax.psum(local_squares(current), 'req'))]
    all_to_all x0 -> x6, blocking collectives: none -> 77.9 us  [exchange(): return lax.all_to_all(array, 'req', split_axis=0, concat_axis=0, tiled=True)]
    psum x2 -> x0, waiting for transfers between devices: 77.5 us -> none  [shards(): totals = lax.psum((payload[0], payload[1]), 'req')]
    all_gather x2 -> x0, blocking collectives: 63.4 us -> none  [shards(): lax.all_gather(context, 'req', axis=0, tiled=True)]
    unnamed x6 -> x0, waiting for transfers between devices: 58.6 us -> none
    all_to_all x4 -> x5, waiting for transfers between devices: 3.72 us -> 54.2 us  [exchange(): return lax.all_to_all(array, 'req', split_axis=0, concat_axis=0, tiled=True)]
    dot_general x0 -> x6, local copies, waits for them, and re-layouts: none -> 21.5 us  [the longest x3 11.8 us: shards(): jnp.dot(scaled, gate_weight[layer_no], preferred_element_type=jnp.float32)]
    ppermute x0 -> x12, starting transfers between devices: none -> 19.4 us  [sum_over_heads(): total = total + lax.ppermute(partial_sum, 'tp', pairs)]
  transfers between devices with their start and end apart: 8 -> 17, of which waited for: 6 -> 7; matrix products, arithmetic and copies ran while one was open for 5% -> 17% of each run, Pallas kernels for 0% -> 0%
where the time goes in v1:
time: 263 us; the launch traced here: 262 us
  blocking collectives  77.9 us (30%)
  waiting for transfers between devices  61.9 us (24%)
  starting transfers between devices  50.5 us (19%)
  local copies, waits for them, and re-layouts  38.4 us (15%)
  matrix products  15 us (6%)
  other arithmetic  12.5 us (5%)
  between operations  5.72 us (2%)
    all_to_all x6, blocking collectives, exchange(): return lax.all_to_all(array, 'req', split_axis=0, concat_axis=0, tiled=True)  77.9 us
    all_to_all x5, waiting for transfers between devices, exchange(): return lax.all_to_all(array, 'req', split_axis=0, concat_axis=0, tiled=True)  54.2 us
    all_to_all x5, starting transfers between devices, exchange(): return lax.all_to_all(array, 'req', split_axis=0, concat_axis=0, tiled=True)  31.1 us
    ppermute x12, starting transfers between devices, sum_over_heads(): total = total + lax.ppermute(partial_sum, 'tp', pairs)  19.4 us
    dot_general x3, local copies, waits for them, and re-layouts, shards(): jnp.dot(scaled, gate_weight[layer_no], preferred_element_type=jnp.float32)  11.8 us
    dot_general x3, local copies, waits for them, and re-layouts, shards(): jnp.dot(scaled, up_weight[layer_no], preferred_element_type=jnp.float32)  9.63 us
    ppermute x12, waiting for transfers between devices, sum_over_heads(): total = total + lax.ppermute(partial_sum, 'tp', pairs)  7.68 us
    gather x2, local copies, waits for them, and re-layouts, shards(): jnp.take(kv_pool[layer_no, :, 0], wanted, axis=0)  5.88 us
  transfers between devices with their start and end apart: 17, of which 7 were waited for; matrix products, arithmetic and copies ran while one was open for 17% of the time, Pallas kernels for 0%

profile of v1, /device:TPU:0, one launch (start us, length us, event | category | flops | bytes accessed | tf_op | source)
XLA Modules:
  0.0 261.9 jit_solution(4211070998871965554)
XLA Ops:
  1.5 7.4 %all-to-all-start = ((s32[32,1,1]{2,1,0:T(1,128)}), s32[32,1,1]{2,1,0:T(1,128)S(1)}, u32[]{:S(2)}, u32[]{:S(2)}) async-start(s32[32,1,1]{2,1,0:T(1,128)} %copy.51), calls=%async_computation | async-start | bytes 32768 | tf_op jit(solution)/shard_map/all_to_all | solution.py:46
  11.9 4.0 %slice_bitcast_fusion.1 = (bf16[32,2,128,128]{3,2,1,0:T(8,128)(2,1)S(1)}, bf16[32,2,128,128]{3,2,1,0:T(8,128)(2,1)}) fusion(bf16[2,32,1,2,128,128]{5,4,3,1,2,0:T(8,128)(2,1)} %bitcast.146), kind=kLoop, calls=%fused_computation.5 | loop fusion | bytes 8388608 | tf_op jit(solution)/shard_map/squeeze | solution.py:107
  18.9 7.4 %all-to-all-start.2 = ((bf16[32,16,128]{2,1,0:T(8,128)(2,1)}), bf16[32,16,128]{2,1,0:T(8,128)(2,1)S(1)}, u32[]{:S(2)}, u32[]{:S(2)}) async-start(bf16[32,16,128]{2,1,0:T(8,128)(2,1)} %pad_maximum_fusion.2), calls=%async_computation.2 | async-start | bytes 262144 | tf_op jit(solution)/shard_map/all_to_all | solution.py:46
  27.0 3.8 %gather_fusion.3 = bf16[32,2,128,128]{3,2,1,0:T(8,128)(2,1)} fusion(bf16[32,2,128,128]{3,2,1,0:T(8,128)(2,1)} %get-tuple-element.113, s32[1024]{0:T(1024)S(1)} %pad_clamp_fusion.1), kind=kCustom, calls=%fused_computation.1.clone | custom fusion | bytes 4194432 | tf_op jit(solution)/shard_map/jit(_take)/gather | solution.py:107
  32.8 4.6 %broadcast_select_fusion.1 = (bf16[32,2,128,128]{3,2,1,0:T(8,128)(2,1)}, bf16[32,2,128,128]{3,2,1,0:T(8,128)(2,1)}) fusion(bf16[32,2,128,128]{3,2,1,0:T(8,128)(2,1)} %gather_fusion.2, pred[32]{0:T(512)(128)(4,1)S(1)} %compare_and_fusion, bf16[32,2,128,128]{3,2,1,0:T(8,128)(2,1)} %gather_fusion.3), kind=kLoop, calls=%fused_computation.7 | loop fusion | flops 2097152 | bytes 8388640 | tf_op jit(solution)/shard_map/jit(_take)/select_n | solution.py:107
  37.5 7.5 %all-to-all-start.1 = ((bf16[32,2,128,128]{3,2,1,0:T(8,128)(2,1)}), bf16[32,2,128,128]{3,2,1,0:T(8,128)(2,1)}, u32[]{:S(2)}, u32[]{:S(2)}) async-start(bf16[32,2,128,128]{3,2,1,0:T(8,128)(2,1)} %get-tuple-element.146), calls=%async_computation.1 | async-start | bytes 4194304 | tf_op jit(solution)/shard_map/all_to_all | solution.py:46
  45.1 3.5 %slice_bitcast_fusion.2 = (bf16[3584,256]{0,1:T(8,128)(2,1)S(1)}, bf16[3584,256]{0,1:T(8,128)(2,1)}) fusion(bf16[2,256,3584]{2,1,0:T(8,128)(2,1)} %param.36), kind=kLoop, calls=%fused_computation.13 | loop fusion | bytes 7340032 | tf_op jit(solution)/shard_map/dot_general | solution.py:138
  50.6 24.4 %all-to-all-done.1 = bf16[32,2,128,128]{3,2,1,0:T(8,128)(2,1)} async-done(((bf16[32,2,128,128]{3,2,1,0:T(8,128)(2,1)}), bf16[32,2,128,128]{3,2,1,0:T(8,128)(2,1)}, u32[]{:S(2)}, u32[]{:S(2)}) %all-to-all-start.1) | async-done | bytes 2097184 | tf_op jit(solution)/shard_map/all_to_all | solution.py:46
  79.5 3.8 %all-to-all-start.3 = ((bf16[32,8,128]{2,1,0:T(8,128)(2,1)}), bf16[32,8,128]{2,1,0:T(8,128)(2,1)S(1)}, u32[]{:S(2)}, u32[]{:S(2)}) async-start(bf16[32,8,128]{2,1,0:T(8,128)(2,1)} %broadcast_in_dim.54), calls=%async_computation.3 | async-start | bytes 131072 | tf_op jit(solution)/shard_map/all_to_all | solution.py:46
  83.3 4.2 %slice_bitcast_fusion.3 = (bf16[3584,256]{0,1:T(8,128)(2,1)}, bf16[3584,256]{0,1:T(8,128)(2,1)}) fusion(bf16[2,256,3584]{2,1,0:T(8,128)(2,1)} %param.35), kind=kLoop, calls=%fused_computation.14 | loop fusion | bytes 7340032 | tf_op jit(solution)/shard_map/dot_general | solution.py:137
  87.5 3.3 %all-to-all-done.3 = bf16[32,8,128]{2,1,0:T(8,128)(2,1)S(1)} async-done(((bf16[32,8,128]{2,1,0:T(8,128)(2,1)}), bf16[32,8,128]{2,1,0:T(8,128)(2,1)S(1)}, u32[]{:S(2)}, u32[]{:S(2)}) %all-to-all-start.3) | async-done | bytes 65568 | tf_op jit(solution)/shard_map/all_to_all | solution.py:46
  91.0 3.9 %collective-permute-start = (f32[32,256]{1,0:T(8,128)S(1)}, f32[32,256]{1,0:T(8,128)S(1)}, u32[]{:S(2)}, u32[]{:S(2)}) collective-permute-start(f32[32,256]{1,0:T(8,128)S(1)} %fusion.13), channel_id=1, source_target_pairs={{0,2},{1,3},{2,0},{3,1},{4,6},{5,7},{6,4},{7,5},{8,10},{9,11},{10,... | collective-permute-start | bytes 98312 | tf_op jit(solution)/shard_map/ppermute | solution.py:78
  98.1 3.8 %copy.56 = bf16[3584,256]{1,0:T(8,128)(2,1)} copy(bf16[3584,256]{0,1:T(8,128)(2,1)} %get-tuple-element.117) | data formatting | bytes 3670016 | tf_op jit(solution)/shard_map/dot_general | solution.py:138
  101.9 3.8 %copy.55 = bf16[3584,256]{1,0:T(8,128)(2,1)} copy(bf16[3584,256]{0,1:T(8,128)(2,1)} %get-tuple-element.115) | data formatting | bytes 3670016 | tf_op jit(solution)/shard_map/dot_general | solution.py:137
  109.3 15.9 %all_to_all.55 = bf16[32,64,128]{2,1,0:T(8,128)(2,1)S(1)} all-to-all(bf16[32,64,128]{2,1,0:T(8,128)(2,1)S(1)} %copy.57), channel_id=1, replica_groups=mesh['req'=32,'tp'=4] {'req'}, dimensions={0} | all-to-all | bytes 1048576 | tf_op jit(solution)/shard_map/all_to_all | solution.py:46
  127.2 12.4 %all_to_all.56 = bf16[32,28,128]{2,1,0:T(8,128)(2,1)S(1)} all-to-all(bf16[32,28,128]{2,1,0:T(8,128)(2,1)S(1)} %broadcast_in_dim.55), channel_id=1, replica_groups=mesh['req'=32,'tp'=4] {'req'}, dimensions={0} | all-to-all | bytes 458752 | tf_op jit(solution)/shard_map/all_to_all | solution.py:46
  146.3 11.3 %all_to_all.57 = bf16[32,16,128]{2,1,0:T(8,128)(2,1)S(1)} all-to-all(bf16[32,16,128]{2,1,0:T(8,128)(2,1)S(1)} %pad_maximum_fusion.3), channel_id=1, replica_groups=mesh['req'=32,'tp'=4] {'req'}, dimensions={0} | all-to-all | bytes 262144 | tf_op jit(solution)/shard_map/all_to_all | solution.py:46
  157.7 4.9 %all-to-all-start.6 = ((bf16[32,2,128,128]{3,2,1,0:T(8,128)(2,1)}), bf16[32,2,128,128]{3,2,1,0:T(8,128)(2,1)}, u32[]{:S(2)}, u32[]{:S(2)}) async-start(bf16[32,2,128,128]{3,2,1,0:T(8,128)(2,1)} %get-tuple-element.147), calls=%async_computation.6 | async-start | bytes 4194304 | tf_op jit(solution)/shard_map/all_to_all | solution.py:46
  166.0 26.6 %all-to-all-done.6 = bf16[32,2,128,128]{3,2,1,0:T(8,128)(2,1)} async-done(((bf16[32,2,128,128]{3,2,1,0:T(8,128)(2,1)}), bf16[32,2,128,128]{3,2,1,0:T(8,128)(2,1)}, u32[]{:S(2)}, u32[]{:S(2)}) %all-to-all-start.6) | async-done | bytes 2097184 | tf_op jit(solution)/shard_map/all_to_all | solution.py:46
  196.4 10.4 %all_to_all.58 = bf16[32,8,128]{2,1,0:T(8,128)(2,1)S(1)} all-to-all(bf16[32,8,128]{2,1,0:T(8,128)(2,1)S(1)} %broadcast_in_dim.57), channel_id=1, replica_groups=mesh['req'=32,'tp'=4] {'req'}, dimensions={0} | all-to-all | bytes 131072 | tf_op jit(solution)/shard_map/all_to_all | solution.py:46
  212.7 3.8 %copy.61 = bf16[3584,256]{1,0:T(8,128)(2,1)} copy(bf16[3584,256]{0,1:T(8,128)(2,1)} %get-tuple-element.114) | data formatting | bytes 3670016 | tf_op jit(solution)/shard_map/dot_general | solution.py:137
  222.3 15.4 %all_to_all.59 = bf16[32,64,128]{2,1,0:T(8,128)(2,1)S(1)} all-to-all(bf16[32,64,128]{2,1,0:T(8,128)(2,1)S(1)} %copy.63), channel_id=1, replica_groups=mesh['req'=32,'tp'=4] {'req'}, dimensions={0} | all-to-all | bytes 1048576 | tf_op jit(solution)/shard_map/all_to_all | solution.py:46
  239.8 12.4 %all_to_all.60 = bf16[32,28,128]{2,1,0:T(8,128)(2,1)S(1)} all-to-all(bf16[32,28,128]{2,1,0:T(8,128)(2,1)S(1)} %broadcast_in_dim.58), channel_id=1, replica_groups=mesh['req'=32,'tp'=4] {'req'}, dimensions={0} | all-to-all | bytes 458752 | tf_op jit(solution)/shard_map/all_to_all | solution.py:46
  257.7 3.5 %collective-permute-done.9 = f32[32,256]{1,0:T(8,128)S(1)} collective-permute-done((f32[32,256]{1,0:T(8,128)S(1)}, f32[32,256]{1,0:T(8,128)S(1)}, u32[]{:S(2)}, u32[]{:S(2)}) %collective-permute-start.9) | collective-permute-done | bytes 32800 | tf_op jit(solution)/shard_map/ppermute | solution.py:78
  (140 shorter events, 54.0 us)
Async XLA Ops:
  1.5 17.4 %all-to-all-start = ((s32[32,1,1]{2,1,0:T(1,128)}), s32[32,1,1]{2,1,0:T(1,128)S(1)}, u32[]{:S(2)}, u32[]{:S(2)}) async-start(s32[32,1,1]{2,1,0:T(1,128)} %copy.51), calls=%async_computation | async-start | bytes 32768 | tf_op jit(solution)/shard_map/all_to_all | solution.py:46
  11.8 4.0 %copy-start.7 = (s32[2,1,1,24]{3,2,1,0:T(1,128)S(1)}, s32[2,1,1,24]{3,2,1,0:T(1,128)}, u32[]{:S(2)}) copy-start(s32[2,1,1,24]{3,2,1,0:T(1,128)} %param.40) | copy-start | bytes 580
  11.8 6.3 %copy-start = (s32[1,32]{1,0:T(1,128)S(1)}, s32[1,32]{1,0:T(1,128)}, u32[]{:S(2)}) copy-start(s32[1,32]{1,0:T(1,128)} %param.39) | copy-start | bytes 388
  18.9 18.6 %all-to-all-start.2 = ((bf16[32,16,128]{2,1,0:T(8,128)(2,1)}), bf16[32,16,128]{2,1,0:T(8,128)(2,1)S(1)}, u32[]{:S(2)}, u32[]{:S(2)}) async-start(bf16[32,16,128]{2,1,0:T(8,128)(2,1)} %pad_maximum_fusion.2), calls=%async_computation.2 | async-start | bytes 262144 | tf_op jit(solution)/shard_map/all_to_all | solution.py:46
  37.5 37.5 %all-to-all-start.1 = ((bf16[32,2,128,128]{3,2,1,0:T(8,128)(2,1)}), bf16[32,2,128,128]{3,2,1,0:T(8,128)(2,1)}, u32[]{:S(2)}, u32[]{:S(2)}) async-start(bf16[32,2,128,128]{3,2,1,0:T(8,128)(2,1)} %get-tuple-element.146), calls=%async_computation.1 | async-start | bytes 4194304 | tf_op jit(solution)/shard_map/all_to_all | solution.py:46
  79.5 11.3 %all-to-all-start.3 = ((bf16[32,8,128]{2,1,0:T(8,128)(2,1)}), bf16[32,8,128]{2,1,0:T(8,128)(2,1)S(1)}, u32[]{:S(2)}, u32[]{:S(2)}) async-start(bf16[32,8,128]{2,1,0:T(8,128)(2,1)} %broadcast_in_dim.54), calls=%async_computation.3 | async-start | bytes 131072 | tf_op jit(solution)/shard_map/all_to_all | solution.py:46
  83.3 7.5 %copy-start.10 = (bf16[2,1024,256]{2,1,0:T(8,128)(2,1)S(1)}, bf16[2,1024,256]{2,1,0:T(8,128)(2,1)}, u32[]{:S(2)}) copy-start(bf16[2,1024,256]{2,1,0:T(8,128)(2,1)} %param.33) | copy-start | bytes 3145732
  83.3 14.8 %copy-start.5 = (bf16[2,256]{1,0:T(2,128)(2,1)S(1)}, bf16[2,256]{1,0:T(2,128)(2,1)}, u32[]{:S(2)}) copy-start(bf16[2,256]{1,0:T(2,128)(2,1)} %param.34) | copy-start | bytes 3076
  91.0 14.8 %collective-permute-start = (f32[32,256]{1,0:T(8,128)S(1)}, f32[32,256]{1,0:T(8,128)S(1)}, u32[]{:S(2)}, u32[]{:S(2)}) collective-permute-start(f32[32,256]{1,0:T(8,128)S(1)} %fusion.13), channel_id=1, source_target_pairs={{0,2},{1,3},{2,0},{3,1},{4,6},{5,7},{6,4},{7,5},{8,10},{9,11},{10,... | collective-permute-start | bytes 98312 | tf_op jit(solution)/shard_map/ppermute | solution.py:78
  94.9 10.9 %collective-permute-start.1 = (f32[32,256]{1,0:T(8,128)S(1)}, f32[32,256]{1,0:T(8,128)S(1)}, u32[]{:S(2)}, u32[]{:S(2)}) collective-permute-start(f32[32,256]{1,0:T(8,128)S(1)} %fusion.13), channel_id=1, source_target_pairs={{0,1},{1,2},{2,3},{3,0},{4,5},{5,6},{6,7},{7,4},{8,9},{9,10},{10,1... | collective-permute-start | bytes 98312 | tf_op jit(solution)/shard_map/ppermute | solution.py:78
  95.9 9.9 %collective-permute-start.2 = (f32[32,256]{1,0:T(8,128)S(1)}, f32[32,256]{1,0:T(8,128)S(1)}, u32[]{:S(2)}, u32[]{:S(2)}) collective-permute-start(f32[32,256]{1,0:T(8,128)S(1)} %fusion.13), channel_id=1, source_target_pairs={{0,3},{1,0},{2,1},{3,2},{4,7},{5,4},{6,5},{7,6},{8,11},{9,8},{10,9... | collective-permute-start | bytes 98312 | tf_op jit(solution)/shard_map/ppermute | solution.py:78
  109.0 30.6 %copy-start.8 = (bf16[2,3584,256]{2,1,0:T(8,128)(2,1)S(1)}, bf16[2,3584,256]{2,1,0:T(8,128)(2,1)}, u32[]{:S(2)}) copy-start(bf16[2,3584,256]{2,1,0:T(8,128)(2,1)} %param.37) | copy-start | bytes 11010052
  125.2 20.6 %copy-start.3 = (bf16[2,256,1024]{2,1,0:T(8,128)(2,1)S(1)}, bf16[2,256,1024]{2,1,0:T(8,128)(2,1)}, u32[]{:S(2)}) copy-start(bf16[2,256,1024]{2,1,0:T(8,128)(2,1)} %param.32) | copy-start | bytes 3145732
  139.9 5.5 %collective-permute-start.3 = (f32[32,256]{1,0:T(8,128)S(1)}, f32[32,256]{1,0:T(8,128)S(1)}, u32[]{:S(2)}, u32[]{:S(2)}) collective-permute-start(f32[32,256]{1,0:T(8,128)S(1)} %fusion.2), channel_id=1, source_target_pairs={{0,2},{1,3},{2,0},{3,1},{4,6},{5,7},{6,4},{7,5},{8,10},{9,11},{10,... | collective-permute-start | bytes 98312 | tf_op jit(solution)/shard_map/ppermute | solution.py:78
  140.0 5.6 %collective-permute-start.4 = (f32[32,256]{1,0:T(8,128)S(1)}, f32[32,256]{1,0:T(8,128)S(1)}, u32[]{:S(2)}, u32[]{:S(2)}) collective-permute-start(f32[32,256]{1,0:T(8,128)S(1)} %fusion.2), channel_id=1, source_target_pairs={{0,1},{1,2},{2,3},{3,0},{4,5},{5,6},{6,7},{7,4},{8,9},{9,10},{10,1... | collective-permute-start | bytes 98312 | tf_op jit(solution)/shard_map/ppermute | solution.py:78
  140.9 4.7 %collective-permute-start.5 = (f32[32,256]{1,0:T(8,128)S(1)}, f32[32,256]{1,0:T(8,128)S(1)}, u32[]{:S(2)}, u32[]{:S(2)}) collective-permute-start(f32[32,256]{1,0:T(8,128)S(1)} %fusion.2), channel_id=1, source_target_pairs={{0,3},{1,0},{2,1},{3,2},{4,7},{5,4},{6,5},{7,6},{8,11},{9,8},{10,9... | collective-permute-start | bytes 98312 | tf_op jit(solution)/shard_map/ppermute | solution.py:78
  157.7 34.9 %all-to-all-start.6 = ((bf16[32,2,128,128]{3,2,1,0:T(8,128)(2,1)}), bf16[32,2,128,128]{3,2,1,0:T(8,128)(2,1)}, u32[]{:S(2)}, u32[]{:S(2)}) async-start(bf16[32,2,128,128]{3,2,1,0:T(8,128)(2,1)} %get-tuple-element.147), calls=%async_computation.6 | async-start | bytes 4194304 | tf_op jit(solution)/shard_map/all_to_all | solution.py:46
  207.1 11.7 %collective-permute-start.6 = (f32[32,256]{1,0:T(8,128)S(1)}, f32[32,256]{1,0:T(8,128)S(1)}, u32[]{:S(2)}, u32[]{:S(2)}) collective-permute-start(f32[32,256]{1,0:T(8,128)S(1)} %fusion.10), channel_id=1, source_target_pairs={{0,2},{1,3},{2,0},{3,1},{4,6},{5,7},{6,4},{7,5},{8,10},{9,11},{10,... | collective-permute-start | bytes 98312 | tf_op jit(solution)/shard_map/ppermute | solution.py:78
  209.4 9.3 %collective-permute-start.7 = (f32[32,256]{1,0:T(8,128)S(1)}, f32[32,256]{1,0:T(8,128)S(1)}, u32[]{:S(2)}, u32[]{:S(2)}) collective-permute-start(f32[32,256]{1,0:T(8,128)S(1)} %fusion.10), channel_id=1, source_target_pairs={{0,1},{1,2},{2,3},{3,0},{4,5},{5,6},{6,7},{7,4},{8,9},{9,10},{10,1... | collective-permute-start | bytes 98312 | tf_op jit(solution)/shard_map/ppermute | solution.py:78
  210.9 7.9 %collective-permute-start.8 = (f32[32,256]{1,0:T(8,128)S(1)}, f32[32,256]{1,0:T(8,128)S(1)}, u32[]{:S(2)}, u32[]{:S(2)}) collective-permute-start(f32[32,256]{1,0:T(8,128)S(1)} %fusion.10), channel_id=1, source_target_pairs={{0,3},{1,0},{2,1},{3,2},{4,7},{5,4},{6,5},{7,6},{8,11},{9,8},{10,9... | collective-permute-start | bytes 98312 | tf_op jit(solution)/shard_map/ppermute | solution.py:78
  222.0 30.2 %copy-start.9 = (bf16[2,3584,256]{2,1,0:T(8,128)(2,1)S(1)}, bf16[2,3584,256]{2,1,0:T(8,128)(2,1)}, u32[]{:S(2)}) copy-start(bf16[2,3584,256]{2,1,0:T(8,128)(2,1)} %param.37) | copy-start | bytes 11010052
  252.5 5.2 %collective-permute-start.10 = (f32[32,256]{1,0:T(8,128)S(1)}, f32[32,256]{1,0:T(8,128)S(1)}, u32[]{:S(2)}, u32[]{:S(2)}) collective-permute-start(f32[32,256]{1,0:T(8,128)S(1)} %fusion), channel_id=1, source_target_pairs={{0,1},{1,2},{2,3},{3,0},{4,5},{5,6},{6,7},{7,4},{8,9},{9,10},{10,1... | collective-permute-start | bytes 98312 | tf_op jit(solution)/shard_map/ppermute | solution.py:78
  252.8 4.9 %collective-permute-start.11 = (f32[32,256]{1,0:T(8,128)S(1)}, f32[32,256]{1,0:T(8,128)S(1)}, u32[]{:S(2)}, u32[]{:S(2)}) collective-permute-start(f32[32,256]{1,0:T(8,128)S(1)} %fusion), channel_id=1, source_target_pairs={{0,3},{1,0},{2,1},{3,2},{4,7},{5,4},{6,5},{7,6},{8,11},{9,8},{10,9... | collective-permute-start | bytes 98312 | tf_op jit(solution)/shard_map/ppermute | solution.py:78
  255.8 5.4 %collective-permute-start.9 = (f32[32,256]{1,0:T(8,128)S(1)}, f32[32,256]{1,0:T(8,128)S(1)}, u32[]{:S(2)}, u32[]{:S(2)}) collective-permute-start(f32[32,256]{1,0:T(8,128)S(1)} %fusion), channel_id=1, source_target_pairs={{0,2},{1,3},{2,0},{3,1},{4,6},{5,7},{6,4},{7,5},{8,10},{9,11},{10,... | collective-permute-start | bytes 98312 | tf_op jit(solution)/shard_map/ppermute | solution.py:78
  (4 other events, 12.7 us)

commit v2 on v1

v2 whole, which is shorter than its diff:
```python
import functools
import math

import jax
import jax.numpy as jnp
import numpy as np
from jax import lax
from jax.experimental import pallas as pl
from jax.experimental.pallas import tpu as pltpu
from jax.sharding import PartitionSpec as P

D = 8192
LAYERS = 2
LANES = 128

MASK_FILL = -1e30
EPSILON = 1e-05

VMEM = pl.BlockSpec(memory_space=pltpu.VMEM)
SMEM = pl.BlockSpec(memory_space=pltpu.SMEM)
ANY = pl.BlockSpec(memory_space=pl.ANY)
F32 = jnp.float32
BF16 = jnp.bfloat16


def rotary_tables(position, head_size):
    freq_idx = np.arange(head_size // 2)
    angles = position * np.exp(freq_idx * (-2.0 * math.log(500000.0) / head_size))
    cosine, sine_part = np.cos(angles), np.sin(angles)
    scale = head_size**-0.5
    tables = np.stack([np.concatenate([cosine, cosine]), np.concatenate([-sine_part, sine_part])])
    return jnp.asarray(tables * scale, F32)


def call(kernel, out_shape, in_specs, scratch=(), limit=16, out_specs=None, flops=0, nbytes=0):
    return pl.pallas_call(
        kernel,
        out_shape=out_shape,
        in_specs=in_specs,
        out_specs=out_specs if out_specs is not None else jax.tree.map(lambda _: VMEM, out_shape),
        scratch_shapes=list(scratch),
        compiler_params=pltpu.CompilerParams(vmem_limit_bytes=limit * 1024 * 1024),
        cost_estimate=pl.CostEstimate(flops=flops, bytes_accessed=nbytes, transcendentals=0),
    )


def store_squares(packed, current, stride, row):
    requests = current.shape[0]
    squares = jnp.sum(current * current, axis=1, keepdims=True)
    high = squares.astype(BF16).astype(F32)
    packed[pl.ds(row, requests, stride=stride), :] = jnp.broadcast_to(high, (requests, LANES))
    packed[pl.ds(row + 1, requests, stride=stride), :] = jnp.broadcast_to(
        squares - high, (requests, LANES)
    )


def store_blocks(packed, product, stride, row):
    requests, width = product.shape
    for k in range(width // LANES):
        packed[pl.ds(row + k, requests, stride=stride), :] = product[:, k * LANES : (k + 1) * LANES]


def store_zeros(packed, requests, stride, rows):
    for row in rows:
        packed[pl.ds(row, requests, stride=stride), :] = jnp.zeros((requests, LANES), F32)


def queries_of(current, gain_ref, layer_no, weight, packed, payload_ref):
    requests = current.shape[0]
    heads = weight.shape[1] // LANES
    stride = packed.shape[0] // requests
    scaled = (current * gain_ref[pl.ds(layer_no, 1), :].astype(F32)).astype(BF16)
    product = jnp.dot(scaled, weight[...], preferred_element_type=F32)
    store_blocks(packed, product, stride, 0)
    store_squares(packed, current, stride, heads)
    store_zeros(packed, requests, stride, range(heads + 2, stride))
    payload_ref[...] = packed[...].astype(BF16)


def first_query_kernel(layer_no, x_ref, gain_ref, weight_ref, payload_ref, weight, packed, sem):
    copy = pltpu.make_async_copy(weight_ref.at[layer_no], weight, sem)
    copy.start()
    current = x_ref[...].astype(F32)
    copy.wait()
    queries_of(current, gain_ref, layer_no, weight, packed, payload_ref)


def query_kernel(
    layer_no, x_ref, own, part_a, part_b, part_c, gain_ref, weight_ref, out_ref, payload_ref, weight, packed, sem
):
    copy = pltpu.make_async_copy(weight_ref.at[layer_no], weight, sem)
    copy.start()
    total = x_ref[...].astype(F32) + ((own[...] + part_a[...]) + (part_b[...] + part_c[...]))
    out_ref[...] = total.astype(BF16)
    current = out_ref[...].astype(F32)
    copy.wait()
    queries_of(current, gain_ref, layer_no, weight, packed, payload_ref)


def attention_kernel(received_ref, tables_ref, bias_ref, kv_ref, out_ref):
    stores = kv_ref.shape[0]
    rows = received_ref.shape[0] // stores
    heads = out_ref.shape[0] // stores
    totals = jnp.sum(received_ref[...].astype(F32).reshape(stores, rows, LANES), axis=0)
    squares = totals[heads : heads + 1, :] + totals[heads + 1 : heads + 2, :]
    queries = totals[:heads] * lax.rsqrt(squares / D + EPSILON)
    queries = queries * tables_ref[0:1, :] + pltpu.roll(queries, LANES // 2, 1) * tables_ref[1:2, :]
    keys = kv_ref[:, 0].reshape(-1, LANES)
    values = kv_ref[:, 1].reshape(-1, LANES)
    scores = lax.dot_general(
        queries.astype(BF16), keys, (((1,), (1,)), ((), ())), preferred_element_type=F32
    )
    scores = jnp.where(bias_ref[...] < 0.0, MASK_FILL, scores)
    terms = jnp.exp(scores - jnp.max(scores, axis=1, keepdims=True))
    total = jnp.sum(terms, axis=1, keepdims=True)
    context = jnp.dot(terms.astype(BF16), values, preferred_element_type=F32) / total
    out_ref[...] = jnp.broadcast_to(context[None], (stores, heads, LANES)).reshape(-1, LANES).astype(BF16)


def rows_of(packed, requests, blocks):
    stride = packed.shape[0] // requests
    return jnp.concatenate(
        [packed[pl.ds(k, requests, stride=stride), :].astype(BF16) for k in range(blocks)], axis=1
    )


def project_kernel(layer_no, requests, received_ref, weight_ref, out_ref, weight, packed, sem):
    copy = pltpu.make_async_copy(weight_ref.at[layer_no], weight, sem)
    copy.start()
    packed[...] = received_ref[...].astype(F32)
    rows = rows_of(packed, requests, weight.shape[0] // LANES)
    copy.wait()
    out_ref[...] = jnp.dot(rows, weight[...], preferred_element_type=F32)


def gate_up_kernel(
    layer_no,
    x_ref,
    own,
    part_a,
    part_b,
    part_c,
    gain_ref,
    gate_ref,
    up_ref,
    out_ref,
    payload_ref,
    gate,
    up,
    packed,
    sems,
):
    gate_copy = pltpu.make_async_copy(gate_ref.at[layer_no], gate, sems.at[0])
    up_copy = pltpu.make_async_copy(up_ref.at[layer_no], up, sems.at[1])
    gate_copy.start()
    up_copy.start()
    requests = x_ref.shape[0]
    stride = packed.shape[0] // requests
    half = stride // 2
    blocks = gate.shape[1] // LANES
    total = x_ref[...].astype(F32) + ((own[...] + part_a[...]) + (part_b[...] + part_c[...]))
    out_ref[...] = total.astype(BF16)
    current = out_ref[...].astype(F32)
    scaled = (current * gain_ref[pl.ds(layer_no, 1), :].astype(F32)).astype(BF16)
    store_squares(packed, current, stride, blocks)
    store_zeros(packed, requests, stride, range(blocks + 2, half))
    store_zeros(packed, requests, stride, range(half + blocks, stride))
    gate_copy.wait()
    store_blocks(packed, jnp.dot(scaled, gate[...], preferred_element_type=F32), stride, 0)
    up_copy.wait()
    store_blocks(packed, jnp.dot(scaled, up[...], preferred_element_type=F32), stride, half)
    payload_ref[...] = packed[...].astype(BF16)


def activation_kernel(blocks, received_ref, out_ref):
    half = 32
    rows = 2 * half
    sources = received_ref.shape[0] // rows
    totals = jnp.sum(received_ref[...].astype(F32).reshape(sources, rows, LANES), axis=0)
    squares = totals[blocks : blocks + 1, :] + totals[blocks + 1 : blocks + 2, :]
    inv = lax.rsqrt(squares / D + EPSILON)
    gate = totals[:half] * inv
    act = gate / (1.0 + jnp.exp(-gate)) * (totals[half:] * inv)
    out_ref[...] = jnp.broadcast_to(act[None], (sources, half, LANES)).reshape(-1, LANES).astype(BF16)


def serve_kernel(layer_no, wanted_ref, pool_ref, out_ref, sem):
    requests = out_ref.shape[0]

    def start(r, carry):
        pltpu.make_async_copy(pool_ref.at[layer_no, wanted_ref[r], 0], out_ref.at[r], sem).start()
        return carry

    lax.fori_loop(0, requests, start, 0)
    pltpu.make_async_copy(pool_ref.at[layer_no, :, 0], out_ref, sem).wait()


def exchange(array, n_req):
    shape = array.shape
    blocks = array.reshape((n_req, shape[0] // n_req) + shape[1:])
    return lax.all_to_all(blocks, "req", split_axis=0, concat_axis=0, tiled=True).reshape(shape)


def tp_parts(partial_sum):
    n_tp = lax.axis_size("tp")
    return [
        lax.ppermute(partial_sum, "tp", [(i, (i + shift) % n_tp) for i in range(n_tp)])
        for shift in (2, 1, 3)
    ]


def shards(
    hidden,
    attn_gain,
    q_weight,
    o_weight,
    ffn_gain,
    gate_weight,
    up_weight,
    down_weight,
    kv_pool,
    block_home,
    chosen,
    chosen_count,
):
    n_req = lax.axis_size("req")
    requests, width = hidden.shape
    most_sel = chosen.shape[3]
    pool_dev = kv_pool.shape[1]
    block_tokens, head_size = kv_pool.shape[4:]
    heads = q_weight.shape[2] // head_size
    hidden_units = gate_weight.shape[2]
    q_rows = 16
    f_rows = 32
    blocks = hidden_units // LANES
    position = float(block_home.shape[1] * block_tokens - 1)
    tables = rotary_tables(position, head_size)
    dma = pltpu.SemaphoreType.DMA

    store_ids = jnp.arange(n_req)
    homes = block_home[0]
    at_store = homes[None, :] // pool_dev == store_ids[:, None]
    slots = jnp.sum(jnp.where(at_store, homes[None, :] % pool_dev, 0), axis=1)
    wanted = exchange(slots.astype(jnp.int32).reshape(n_req, 1), n_req).reshape(n_req)
    fetched, biases = [], []
    for layer_no in range(LAYERS):
        served = call(
            functools.partial(serve_kernel, layer_no),
            jax.ShapeDtypeStruct((n_req, 2, block_tokens, head_size), BF16),
            [SMEM, ANY],
            [dma],
            out_specs=ANY,
        )(wanted, kv_pool)
        fetched.append(exchange(served, n_req))
        stores = jnp.sum(
            jnp.where(chosen[layer_no, 0, 0][:, None] == store_ids[None, :], homes[None, :] // pool_dev, 0),
            axis=1,
        )
        used = jnp.arange(most_sel) < chosen_count[layer_no, 0, 0]
        valid = jnp.any((stores[None, :] == store_ids[:, None]) & used[None, :], axis=1)
        bias = jnp.where(valid, 0.0, -1.0).astype(F32)
        biases.append(jnp.broadcast_to(bias[:, None], (n_req, block_tokens)).reshape(1, -1))

    current = hidden
    parts = None
    for layer_no in range(LAYERS):
        payload_shape = jax.ShapeDtypeStruct((requests * q_rows, LANES), BF16)
        scratch = [
            pltpu.VMEM(q_weight.shape[1:], BF16),
            pltpu.VMEM((requests * q_rows, LANES), F32),
            dma,
        ]
        if parts is None:
            payload = call(
                functools.partial(first_query_kernel, layer_no),
                payload_shape,
                [VMEM, VMEM, ANY],
                scratch,
            )(current, attn_gain, q_weight)
        else:
            current, payload = call(
                functools.partial(query_kernel, layer_no),
                [jax.ShapeDtypeStruct(current.shape, BF16), payload_shape],
                [VMEM] * 6 + [ANY],
                scratch,
            )(current, *parts, attn_gain, q_weight)
        received = exchange(payload, n_req)
        context = call(
            attention_kernel,
            jax.ShapeDtypeStruct((n_req * heads, LANES), BF16),
            [VMEM] * 4,
        )(received, tables, biases[layer_no], fetched[layer_no])
        contexts = exchange(context, n_req)
        own = call(
            functools.partial(project_kernel, layer_no, requests),
            jax.ShapeDtypeStruct((requests, width), F32),
            [VMEM, ANY],
            [pltpu.VMEM(o_weight.shape[1:], BF16), pltpu.VMEM(contexts.shape, F32), dma],
        )(contexts, o_weight)
        attended, payload = call(
            functools.partial(gate_up_kernel, layer_no),
            [
                jax.ShapeDtypeStruct(current.shape, BF16),
                jax.ShapeDtypeStruct((requests * 2 * f_rows, LANES), BF16),
            ],
            [VMEM] * 6 + [ANY] * 2,
            [
                pltpu.VMEM(gate_weight.shape[1:], BF16),
                pltpu.VMEM(up_weight.shape[1:], BF16),
                pltpu.VMEM((requests * 2 * f_rows, LANES), F32),
                dma((2,)),
            ],
        )(current, own, *tp_parts(own), ffn_gain, gate_weight, up_weight)
        received = exchange(payload, n_req)
        act = call(
            functools.partial(activation_kernel, blocks),
            jax.ShapeDtypeStruct((n_req * f_rows, LANES), BF16),
            [VMEM],
        )(received)
        acts = exchange(act, n_req)
        own = call(
            functools.partial(project_kernel, layer_no, requests),
            jax.ShapeDtypeStruct((requests, width), F32),
            [VMEM, ANY],
            [pltpu.VMEM(down_weight.shape[1:], BF16), pltpu.VMEM(acts.shape, F32), dma],
        )(acts, down_weight)
        current, parts = attended, [own] + tp_parts(own)
    total = (parts[0] + parts[1]) + (parts[2] + parts[3])
    return (current.astype(F32) + total).astype(BF16)


def solution(mesh):
    return jax.shard_map(
        shards,
        mesh=mesh,
        in_specs=(
            P(None, "req"),
            P(None, "req"),
            P(None, "req", "tp"),
            P(None, "tp", "req"),
            P(None, "req"),
            P(None, "req", "tp"),
            P(None, "req", "tp"),
            P(None, "tp", "req"),
            P(None, "req", "tp", None, None, None),
            P("req", None),
            P(None, "req", "tp", None),
            P(None, "req", "tp"),
        ),
        out_specs=P(None, "req"),
        check_vma=False,
    )
```

time: 263 us -> 229 us (0.87)
  local copies, waits for them, and re-layouts: 38.4 us -> 19.9 us
  waiting for transfers between devices: 61.9 us -> 78.9 us
  matrix products: 15 us -> 0 us
  blocking collectives: 77.9 us -> 64.1 us
  Pallas kernels: 0 us -> 13.4 us
  other arithmetic: 12.5 us -> 3.67 us
  between operations: 5.72 us -> 0.32 us
  starting transfers between devices: 50.5 us -> 47.8 us
    dot_general x6 -> x0, local copies, waits for them, and re-layouts: 21.5 us -> none  [the longest x3 11.8 us: shards(): jnp.dot(scaled, gate_weight[layer_no], preferred_element_type=jnp.float32)]
    unnamed x24 -> x40, local copies, waits for them, and re-layouts: 0.11 us -> 18.4 us
    dot_general x14 -> x0, matrix products: 15 us -> none  [the longest x2 3.44 us: shards(): jnp.einsum('eh,sbh->seb', queries, blocks[:, 0], preferred_element_type=j...]
    all_to_all x6 -> x5, blocking collectives: 77.9 us -> 64.1 us  [exchange(): lax.all_to_all(blocks, 'req', split_axis=0, concat_axis=0, tiled=True)]
    pallas_call x0 -> x14, Pallas kernels: none -> 13.4 us  [the longest x2 3.81 us: shards(): call(functools.partial(serve_kernel, layer_no), jax.ShapeDtypeStruct((n_r...]
    all_to_all x5 -> x6, waiting for transfers between devices: 54.2 us -> 65 us  [exchange(): lax.all_to_all(blocks, 'req', split_axis=0, concat_axis=0, tiled=True)]
    gather x4 -> x0, local copies, waits for them, and re-layouts: 7.27 us -> none  [the longest x2 5.88 us: shards(): jnp.take(kv_pool[layer_no, :, 0], wanted, axis=0)]
    ppermute x12, waiting for transfers between devices: 7.68 us -> 13.9 us  [tp_parts(): lax.ppermute(partial_sum, 'tp', [(i, (i + shift) % n_tp) for i in range(n...]
  transfers between devices with their start and end apart: 17 -> 18, of which waited for: 7 -> 15; matrix products, arithmetic and copies ran while one was open for 17% -> 1% of each run, Pallas kernels for 0% -> 3%
where the time goes in v2:
time: 229 us; the launch traced here: 228 us
  waiting for transfers between devices  78.9 us (34%)
  blocking collectives  64.1 us (28%)
  starting transfers between devices  47.8 us (21%)
  local copies, waits for them, and re-layouts  19.9 us (9%)
  Pallas kernels  13.4 us (6%)
  other arithmetic  3.67 us (2%)
    all_to_all x6, waiting for transfers between devices, exchange(): lax.all_to_all(blocks, 'req', split_axis=0, concat_axis=0, tiled=True)  65 us
    all_to_all x5, blocking collectives, exchange(): lax.all_to_all(blocks, 'req', split_axis=0, concat_axis=0, tiled=True)  64.1 us
    all_to_all x6, starting transfers between devices, exchange(): lax.all_to_all(blocks, 'req', split_axis=0, concat_axis=0, tiled=True)  27.7 us
    ppermute x12, starting transfers between devices, tp_parts(): lax.ppermute(partial_sum, 'tp', [(i, (i + shift) % n_tp) for i in range(n...  20.1 us
    unnamed x40, local copies, waits for them, and re-layouts  18.4 us
    ppermute x12, waiting for transfers between devices, tp_parts(): lax.ppermute(partial_sum, 'tp', [(i, (i + shift) % n_tp) for i in range(n...  13.9 us
  transfers between devices with their start and end apart: 18, of which 15 were waited for; matrix products, arithmetic and copies ran while one was open for 1% of the time, Pallas kernels for 3%

profile of v2, /device:TPU:0, one launch (start us, length us, event | category | flops | bytes accessed | tf_op | source)
XLA Modules:
  0.0 228.0 jit_solution(16724813112123314032)
XLA Ops:
  1.5 7.4 %all-to-all-start.1 = ((s32[32,1,1]{2,1,0:T(1,128)}), s32[32,1,1]{2,1,0:T(1,128)S(1)}, u32[]{:S(2)}, u32[]{:S(2)}) async-start(s32[32,1,1]{2,1,0:T(1,128)} %copy.20), calls=%async_computation.1 | async-start | bytes 32768 | tf_op jit(solution)/shard_map/all_to_all | solution.py:201
  12.5 3.7 %all-to-all-done.1 = s32[32,1,1]{2,1,0:T(1,128)S(1)} async-done(((s32[32,1,1]{2,1,0:T(1,128)}), s32[32,1,1]{2,1,0:T(1,128)S(1)}, u32[]{:S(2)}, u32[]{:S(2)}) %all-to-all-start.1) | async-done | bytes 160 | tf_op jit(solution)/shard_map/all_to_all | solution.py:201
  16.2 3.8 %all-to-all-start = ((bf16[32,16,128]{2,1,0:T(8,128)(2,1)}), bf16[32,16,128]{2,1,0:T(8,128)(2,1)S(1)}, u32[]{:S(2)}, u32[]{:S(2)}) async-start(bf16[32,16,128]{2,1,0:T(8,128)(2,1)} %bitcast), calls=%async_computation | async-start | bytes 262144 | tf_op jit(solution)/shard_map/all_to_all | solution.py:201
  20.7 2.2 copy-done
  24.8 3.0 %all-to-all-done = bf16[32,16,128]{2,1,0:T(8,128)(2,1)S(1)} async-done(((bf16[32,16,128]{2,1,0:T(8,128)(2,1)}), bf16[32,16,128]{2,1,0:T(8,128)(2,1)S(1)}, u32[]{:S(2)}, u32[]{:S(2)}) %all-to-all-start) | async-done | bytes 131104 | tf_op jit(solution)/shard_map/all_to_all | solution.py:201
  27.8 4.6 %all-to-all-start.2 = ((bf16[32,1,2,128,128]{4,3,2,1,0:T(8,128)(2,1)}), bf16[32,1,2,128,128]{4,3,2,1,0:T(8,128)(2,1)S(1)}, u32[]{:S(2)}, u32[]{:S(2)}) async-start(bf16[32,1,2,128,128]{4,3,2,1,0:T(8,128)(2,1)} %bitcast.9), calls=%async_computation.2 | async-start | bytes 4194304 | tf_op jit(solution)/shard_map/all_to_all | solution.py:201
  34.7 27.7 %all-to-all-done.2 = bf16[32,1,2,128,128]{4,3,2,1,0:T(8,128)(2,1)S(1)} async-done(((bf16[32,1,2,128,128]{4,3,2,1,0:T(8,128)(2,1)}), bf16[32,1,2,128,128]{4,3,2,1,0:T(8,128)(2,1)S(1)}, u32[]{:S(2)}, u32[]{:S(2)}) %all-to-all-start.2) | async-done | bytes 2097184 | tf_op jit(solution)/shard_map/all_to_all | solution.py:201
  63.2 10.4 %all_to_all.55 = bf16[32,8,128]{2,1,0:T(8,128)(2,1)S(1)} all-to-all(bf16[32,8,128]{2,1,0:T(8,128)(2,1)S(1)} %bitcast.49), channel_id=1, replica_groups=mesh['req'=32,'tp'=4] {'req'}, dimensions={0} | all-to-all | bytes 131072 | tf_op jit(solution)/shard_map/all_to_all | solution.py:201
  74.0 4.0 %collective-permute-start = (f32[32,256]{1,0:T(8,128)S(1)}, f32[32,256]{1,0:T(8,128)S(1)}, u32[]{:S(2)}, u32[]{:S(2)}) collective-permute-start(f32[32,256]{1,0:T(8,128)S(1)} %shard_map.130.own), channel_id=1, source_target_pairs={{0,2},{1,3},{2,0},{3,1},{4,6},{5,7},{6,4},{7,5},{8,10},{9,11},{10,... | collective-permute-start | bytes 98312 | tf_op jit(solution)/shard_map/ppermute | solution.py:207
  79.0 2.2 collective-permute-start.2
  88.6 15.2 %all_to_all.56 = bf16[32,64,128]{2,1,0:T(8,128)(2,1)S(1)} all-to-all(bf16[32,64,128]{2,1,0:T(8,128)(2,1)S(1)} %bitcast.47), channel_id=1, replica_groups=mesh['req'=32,'tp'=4] {'req'}, dimensions={0} | all-to-all | bytes 1048576 | tf_op jit(solution)/shard_map/all_to_all | solution.py:201
  104.6 3.9 %all-to-all-start.5 = ((bf16[32,32,128]{2,1,0:T(8,128)(2,1)}), bf16[32,32,128]{2,1,0:T(8,128)(2,1)S(1)}, u32[]{:S(2)}, u32[]{:S(2)}) async-start(bf16[32,32,128]{2,1,0:T(8,128)(2,1)} %bitcast.15), calls=%async_computation.5 | async-start | bytes 524288 | tf_op jit(solution)/shard_map/all_to_all | solution.py:201
  112.6 4.8 %all-to-all-done.5 = bf16[32,32,128]{2,1,0:T(8,128)(2,1)S(1)} async-done(((bf16[32,32,128]{2,1,0:T(8,128)(2,1)}), bf16[32,32,128]{2,1,0:T(8,128)(2,1)S(1)}, u32[]{:S(2)}, u32[]{:S(2)}) %all-to-all-start.5) | async-done | bytes 262176 | tf_op jit(solution)/shard_map/all_to_all | solution.py:201
  117.4 4.1 %all-to-all-start.7 = ((bf16[32,1,2,128,128]{4,3,2,1,0:T(8,128)(2,1)}), bf16[32,1,2,128,128]{4,3,2,1,0:T(8,128)(2,1)S(1)}, u32[]{:S(2)}, u32[]{:S(2)}) async-start(bf16[32,1,2,128,128]{4,3,2,1,0:T(8,128)(2,1)} %bitcast.23), calls=%async_computation.7 | async-start | bytes 4194304 | tf_op jit(solution)/shard_map/all_to_all | solution.py:201
  126.0 2.6 %collective-permute-start.4 = (f32[32,256]{1,0:T(8,128)S(1)}, f32[32,256]{1,0:T(8,128)S(1)}, u32[]{:S(2)}, u32[]{:S(2)}) collective-permute-start(f32[32,256]{1,0:T(8,128)S(1)} %shard_map.133.own), channel_id=1, source_target_pairs={{0,1},{1,2},{2,3},{3,0},{4,5},{5,6},{6,7},{7,4},{8,9},{9,10},{10,1... | collective-permute-start | bytes 98312 | tf_op jit(solution)/shard_map/ppermute | solution.py:207
  133.5 18.0 %all-to-all-done.7 = bf16[32,1,2,128,128]{4,3,2,1,0:T(8,128)(2,1)S(1)} async-done(((bf16[32,1,2,128,128]{4,3,2,1,0:T(8,128)(2,1)}), bf16[32,1,2,128,128]{4,3,2,1,0:T(8,128)(2,1)S(1)}, u32[]{:S(2)}, u32[]{:S(2)}) %all-to-all-start.7) | async-done | bytes 2097184 | tf_op jit(solution)/shard_map/all_to_all | solution.py:201
  151.5 3.8 %all-to-all-start.6 = ((bf16[32,16,128]{2,1,0:T(8,128)(2,1)}), bf16[32,16,128]{2,1,0:T(8,128)(2,1)S(1)}, u32[]{:S(2)}, u32[]{:S(2)}) async-start(bf16[32,16,128]{2,1,0:T(8,128)(2,1)} %bitcast.17), calls=%async_computation.6 | async-start | bytes 262144 | tf_op jit(solution)/shard_map/all_to_all | solution.py:201
  155.4 7.8 %all-to-all-done.6 = bf16[32,16,128]{2,1,0:T(8,128)(2,1)S(1)} async-done(((bf16[32,16,128]{2,1,0:T(8,128)(2,1)}), bf16[32,16,128]{2,1,0:T(8,128)(2,1)S(1)}, u32[]{:S(2)}, u32[]{:S(2)}) %all-to-all-start.6) | async-done | bytes 131104 | tf_op jit(solution)/shard_map/all_to_all | solution.py:201
  164.0 11.0 %all_to_all.57 = bf16[32,8,128]{2,1,0:T(8,128)(2,1)S(1)} all-to-all(bf16[32,8,128]{2,1,0:T(8,128)(2,1)S(1)} %bitcast.48), channel_id=1, replica_groups=mesh['req'=32,'tp'=4] {'req'}, dimensions={0} | all-to-all | bytes 131072 | tf_op jit(solution)/shard_map/all_to_all | solution.py:201
  178.0 2.6 %collective-permute-start.7 = (f32[32,256]{1,0:T(8,128)S(1)}, f32[32,256]{1,0:T(8,128)S(1)}, u32[]{:S(2)}, u32[]{:S(2)}) collective-permute-start(f32[32,256]{1,0:T(8,128)S(1)} %shard_map.137.own), channel_id=1, source_target_pairs={{0,1},{1,2},{2,3},{3,0},{4,5},{5,6},{6,7},{7,4},{8,9},{9,10},{10,1... | collective-permute-start | bytes 98312 | tf_op jit(solution)/shard_map/ppermute | solution.py:207
  190.1 15.2 %all_to_all.58 = bf16[32,64,128]{2,1,0:T(8,128)(2,1)S(1)} all-to-all(bf16[32,64,128]{2,1,0:T(8,128)(2,1)S(1)} %bitcast.46), channel_id=1, replica_groups=mesh['req'=32,'tp'=4] {'req'}, dimensions={0} | all-to-all | bytes 1048576 | tf_op jit(solution)/shard_map/all_to_all | solution.py:201
  205.4 12.4 %all_to_all.59 = bf16[32,32,128]{2,1,0:T(8,128)(2,1)S(1)} all-to-all(bf16[32,32,128]{2,1,0:T(8,128)(2,1)S(1)} %bitcast.41), channel_id=1, replica_groups=mesh['req'=32,'tp'=4] {'req'}, dimensions={0} | all-to-all | bytes 524288 | tf_op jit(solution)/shard_map/all_to_all | solution.py:201
  218.7 3.2 %collective-permute-start.11 = (f32[32,256]{1,0:T(8,128)S(1)}, f32[32,256]{1,0:T(8,128)S(1)}, u32[]{:S(2)}, u32[]{:S(2)}) collective-permute-start(f32[32,256]{1,0:T(8,128)S(1)} %shard_map.140), channel_id=1, source_target_pairs={{0,3},{1,0},{2,1},{3,2},{4,7},{5,4},{6,5},{7,6},{8,11},{9,8},{10,9... | collective-permute-start | bytes 98312 | tf_op jit(solution)/shard_map/ppermute | solution.py:207
  223.8 3.5 %collective-permute-done.9 = f32[32,256]{1,0:T(8,128)S(1)} collective-permute-done((f32[32,256]{1,0:T(8,128)S(1)}, f32[32,256]{1,0:T(8,128)S(1)}, u32[]{:S(2)}, u32[]{:S(2)}) %collective-permute-start.9) | collective-permute-done | bytes 32800 | tf_op jit(solution)/shard_map/ppermute | solution.py:207
  (86 shorter events, 50.5 us)
Async XLA Ops:
  1.5 14.7 %all-to-all-start.1 = ((s32[32,1,1]{2,1,0:T(1,128)}), s32[32,1,1]{2,1,0:T(1,128)S(1)}, u32[]{:S(2)}, u32[]{:S(2)}) async-start(s32[32,1,1]{2,1,0:T(1,128)} %copy.20), calls=%async_computation.1 | async-start | bytes 32768 | tf_op jit(solution)/shard_map/all_to_all | solution.py:201
  16.2 11.6 %all-to-all-start = ((bf16[32,16,128]{2,1,0:T(8,128)(2,1)}), bf16[32,16,128]{2,1,0:T(8,128)(2,1)S(1)}, u32[]{:S(2)}, u32[]{:S(2)}) async-start(bf16[32,16,128]{2,1,0:T(8,128)(2,1)} %bitcast), calls=%async_computation | async-start | bytes 262144 | tf_op jit(solution)/shard_map/all_to_all | solution.py:201
  24.8 37.7 %copy-start.14 = (f32[2,128]{1,0:T(2,128)S(1)}, f32[2,128]{1,0:T(2,128)}, u32[]{:S(2)}) copy-start(f32[2,128]{1,0:T(2,128)} %constant.41.clone.tables_ref) | copy-start | bytes 3076
  24.8 48.9 %copy-start.10 = (bf16[2,1024,256]{2,1,0:T(8,128)(2,1)S(1)}, bf16[2,1024,256]{2,1,0:T(8,128)(2,1)}, u32[]{:S(2)}) copy-start(bf16[2,1024,256]{2,1,0:T(8,128)(2,1)} %weight_ref.10) | copy-start | bytes 3145732
  27.8 55.3 %copy-start.13 = (bf16[32,256]{1,0:T(8,128)(2,1)S(1)}, bf16[32,256]{1,0:T(8,128)(2,1)}, u32[]{:S(2)}) copy-start(bf16[32,256]{1,0:T(8,128)(2,1)} %x_ref.3) | copy-start | bytes 49156
  27.8 55.3 %copy-start.17 = (bf16[2,256]{1,0:T(2,128)(2,1)S(1)}, bf16[2,256]{1,0:T(2,128)(2,1)}, u32[]{:S(2)}) copy-start(bf16[2,256]{1,0:T(2,128)(2,1)} %gain_ref.7) | copy-start | bytes 3076
  27.8 34.6 %all-to-all-start.2 = ((bf16[32,1,2,128,128]{4,3,2,1,0:T(8,128)(2,1)}), bf16[32,1,2,128,128]{4,3,2,1,0:T(8,128)(2,1)S(1)}, u32[]{:S(2)}, u32[]{:S(2)}) async-start(bf16[32,1,2,128,128]{4,3,2,1,0:T(8,128)(2,1)} %bitcast.9), calls=%async_computation.2 | async-start | bytes 4194304 | tf_op jit(solution)/shard_map/all_to_all | solution.py:201
  74.0 7.2 %collective-permute-start = (f32[32,256]{1,0:T(8,128)S(1)}, f32[32,256]{1,0:T(8,128)S(1)}, u32[]{:S(2)}, u32[]{:S(2)}) collective-permute-start(f32[32,256]{1,0:T(8,128)S(1)} %shard_map.130.own), channel_id=1, source_target_pairs={{0,2},{1,3},{2,0},{3,1},{4,6},{5,7},{6,4},{7,5},{8,10},{9,11},{10,... | collective-permute-start | bytes 98312 | tf_op jit(solution)/shard_map/ppermute | solution.py:207
  77.9 5.1 %collective-permute-start.1 = (f32[32,256]{1,0:T(8,128)S(1)}, f32[32,256]{1,0:T(8,128)S(1)}, u32[]{:S(2)}, u32[]{:S(2)}) collective-permute-start(f32[32,256]{1,0:T(8,128)S(1)} %shard_map.130.own), channel_id=1, source_target_pairs={{0,1},{1,2},{2,3},{3,0},{4,5},{5,6},{6,7},{7,4},{8,9},{9,10},{10,1... | collective-permute-start | bytes 98312 | tf_op jit(solution)/shard_map/ppermute | solution.py:207
  79.0 4.1 %collective-permute-start.2 = (f32[32,256]{1,0:T(8,128)S(1)}, f32[32,256]{1,0:T(8,128)S(1)}, u32[]{:S(2)}, u32[]{:S(2)}) collective-permute-start(f32[32,256]{1,0:T(8,128)S(1)} %shard_map.130.own), channel_id=1, source_target_pairs={{0,3},{1,0},{2,1},{3,2},{4,7},{5,4},{6,5},{7,6},{8,11},{9,8},{10,9... | collective-permute-start | bytes 98312 | tf_op jit(solution)/shard_map/ppermute | solution.py:207
  104.6 12.8 %all-to-all-start.5 = ((bf16[32,32,128]{2,1,0:T(8,128)(2,1)}), bf16[32,32,128]{2,1,0:T(8,128)(2,1)S(1)}, u32[]{:S(2)}, u32[]{:S(2)}) async-start(bf16[32,32,128]{2,1,0:T(8,128)(2,1)} %bitcast.15), calls=%async_computation.5 | async-start | bytes 524288 | tf_op jit(solution)/shard_map/all_to_all | solution.py:201
  117.4 15.1 %copy-start.16 = (bf16[2,256]{1,0:T(2,128)(2,1)S(1)}, bf16[2,256]{1,0:T(2,128)(2,1)}, u32[]{:S(2)}) copy-start(bf16[2,256]{1,0:T(2,128)(2,1)} %gain_ref.6) | copy-start | bytes 3076
  117.4 34.1 %all-to-all-start.7 = ((bf16[32,1,2,128,128]{4,3,2,1,0:T(8,128)(2,1)}), bf16[32,1,2,128,128]{4,3,2,1,0:T(8,128)(2,1)S(1)}, u32[]{:S(2)}, u32[]{:S(2)}) async-start(bf16[32,1,2,128,128]{4,3,2,1,0:T(8,128)(2,1)} %bitcast.23), calls=%async_computation.7 | async-start | bytes 4194304 | tf_op jit(solution)/shard_map/all_to_all | solution.py:201
  124.4 5.5 %collective-permute-start.3 = (f32[32,256]{1,0:T(8,128)S(1)}, f32[32,256]{1,0:T(8,128)S(1)}, u32[]{:S(2)}, u32[]{:S(2)}) collective-permute-start(f32[32,256]{1,0:T(8,128)S(1)} %shard_map.133.own), channel_id=1, source_target_pairs={{0,2},{1,3},{2,0},{3,1},{4,6},{5,7},{6,4},{7,5},{8,10},{9,11},{10,... | collective-permute-start | bytes 98312 | tf_op jit(solution)/shard_map/ppermute | solution.py:207
  126.0 5.1 %collective-permute-start.4 = (f32[32,256]{1,0:T(8,128)S(1)}, f32[32,256]{1,0:T(8,128)S(1)}, u32[]{:S(2)}, u32[]{:S(2)}) collective-permute-start(f32[32,256]{1,0:T(8,128)S(1)} %shard_map.133.own), channel_id=1, source_target_pairs={{0,1},{1,2},{2,3},{3,0},{4,5},{5,6},{6,7},{7,4},{8,9},{9,10},{10,1... | collective-permute-start | bytes 98312 | tf_op jit(solution)/shard_map/ppermute | solution.py:207
  128.6 3.9 %collective-permute-start.5 = (f32[32,256]{1,0:T(8,128)S(1)}, f32[32,256]{1,0:T(8,128)S(1)}, u32[]{:S(2)}, u32[]{:S(2)}) collective-permute-start(f32[32,256]{1,0:T(8,128)S(1)} %shard_map.133.own), channel_id=1, source_target_pairs={{0,3},{1,0},{2,1},{3,2},{4,7},{5,4},{6,5},{7,6},{8,11},{9,8},{10,9... | collective-permute-start | bytes 98312 | tf_op jit(solution)/shard_map/ppermute | solution.py:207
  151.5 11.6 %all-to-all-start.6 = ((bf16[32,16,128]{2,1,0:T(8,128)(2,1)}), bf16[32,16,128]{2,1,0:T(8,128)(2,1)S(1)}, u32[]{:S(2)}, u32[]{:S(2)}) async-start(bf16[32,16,128]{2,1,0:T(8,128)(2,1)} %bitcast.17), calls=%async_computation.6 | async-start | bytes 262144 | tf_op jit(solution)/shard_map/all_to_all | solution.py:201
  176.5 5.5 %collective-permute-start.6 = (f32[32,256]{1,0:T(8,128)S(1)}, f32[32,256]{1,0:T(8,128)S(1)}, u32[]{:S(2)}, u32[]{:S(2)}) collective-permute-start(f32[32,256]{1,0:T(8,128)S(1)} %shard_map.137.own), channel_id=1, source_target_pairs={{0,2},{1,3},{2,0},{3,1},{4,6},{5,7},{6,4},{7,5},{8,10},{9,11},{10,... | collective-permute-start | bytes 98312 | tf_op jit(solution)/shard_map/ppermute | solution.py:207
  178.0 5.1 %collective-permute-start.7 = (f32[32,256]{1,0:T(8,128)S(1)}, f32[32,256]{1,0:T(8,128)S(1)}, u32[]{:S(2)}, u32[]{:S(2)}) collective-permute-start(f32[32,256]{1,0:T(8,128)S(1)} %shard_map.137.own), channel_id=1, source_target_pairs={{0,1},{1,2},{2,3},{3,0},{4,5},{5,6},{6,7},{7,4},{8,9},{9,10},{10,1... | collective-permute-start | bytes 98312 | tf_op jit(solution)/shard_map/ppermute | solution.py:207
  180.7 3.9 %collective-permute-start.8 = (f32[32,256]{1,0:T(8,128)S(1)}, f32[32,256]{1,0:T(8,128)S(1)}, u32[]{:S(2)}, u32[]{:S(2)}) collective-permute-start(f32[32,256]{1,0:T(8,128)S(1)} %shard_map.137.own), channel_id=1, source_target_pairs={{0,3},{1,0},{2,1},{3,2},{4,7},{5,4},{6,5},{7,6},{8,11},{9,8},{10,9... | collective-permute-start | bytes 98312 | tf_op jit(solution)/shard_map/ppermute | solution.py:207
  188.7 29.1 %copy-start.7 = (bf16[2,3584,256]{2,1,0:T(8,128)(2,1)S(1)}, bf16[2,3584,256]{2,1,0:T(8,128)(2,1)}, u32[]{:S(2)}) copy-start(bf16[2,3584,256]{2,1,0:T(8,128)(2,1)} %weight_ref.11) | copy-start | bytes 11010052
  218.6 5.2 %collective-permute-start.10 = (f32[32,256]{1,0:T(8,128)S(1)}, f32[32,256]{1,0:T(8,128)S(1)}, u32[]{:S(2)}, u32[]{:S(2)}) collective-permute-start(f32[32,256]{1,0:T(8,128)S(1)} %shard_map.140), channel_id=1, source_target_pairs={{0,1},{1,2},{2,3},{3,0},{4,5},{5,6},{6,7},{7,4},{8,9},{9,10},{10,1... | collective-permute-start | bytes 98312 | tf_op jit(solution)/shard_map/ppermute | solution.py:207
  218.7 5.1 %collective-permute-start.11 = (f32[32,256]{1,0:T(8,128)S(1)}, f32[32,256]{1,0:T(8,128)S(1)}, u32[]{:S(2)}, u32[]{:S(2)}) collective-permute-start(f32[32,256]{1,0:T(8,128)S(1)} %shard_map.140), channel_id=1, source_target_pairs={{0,3},{1,0},{2,1},{3,2},{4,7},{5,4},{6,5},{7,6},{8,11},{9,8},{10,9... | collective-permute-start | bytes 98312 | tf_op jit(solution)/shard_map/ppermute | solution.py:207
  221.9 5.4 %collective-permute-start.9 = (f32[32,256]{1,0:T(8,128)S(1)}, f32[32,256]{1,0:T(8,128)S(1)}, u32[]{:S(2)}, u32[]{:S(2)}) collective-permute-start(f32[32,256]{1,0:T(8,128)S(1)} %shard_map.140), channel_id=1, source_target_pairs={{0,2},{1,3},{2,0},{3,1},{4,6},{5,7},{6,4},{7,5},{8,10},{9,11},{10,... | collective-permute-start | bytes 98312 | tf_op jit(solution)/shard_map/ppermute | solution.py:207
  (14 other events, 50.7 us)

commit v3 on v2

--- a/solution.py
+++ b/solution.py
@@ -18,7 +18,7 @@
 
 VMEM = pl.BlockSpec(memory_space=pltpu.VMEM)
 SMEM = pl.BlockSpec(memory_space=pltpu.SMEM)
-ANY = pl.BlockSpec(memory_space=pl.ANY)
+HBM = pl.BlockSpec(memory_space=pltpu.HBM)
 F32 = jnp.float32
 BF16 = jnp.bfloat16
 
@@ -65,56 +65,142 @@
         packed[pl.ds(row, requests, stride=stride), :] = jnp.zeros((requests, LANES), F32)
 
 
-def queries_of(current, gain_ref, layer_no, weight, packed, payload_ref):
+def queries_of(current, gain, weight, packed, payload_ref, slots=None):
     requests = current.shape[0]
     heads = weight.shape[1] // LANES
     stride = packed.shape[0] // requests
-    scaled = (current * gain_ref[pl.ds(layer_no, 1), :].astype(F32)).astype(BF16)
+    scaled = (current * gain).astype(BF16)
     product = jnp.dot(scaled, weight[...], preferred_element_type=F32)
     store_blocks(packed, product, stride, 0)
     store_squares(packed, current, stride, heads)
-    store_zeros(packed, requests, stride, range(heads + 2, stride))
+    first = heads + 2
+    if slots is not None:
+        packed[pl.ds(first, requests, stride=stride), :] = slots
+        first += 1
+    store_zeros(packed, requests, stride, range(first, stride))
     payload_ref[...] = packed[...].astype(BF16)
 
 
-def first_query_kernel(layer_no, x_ref, gain_ref, weight_ref, payload_ref, weight, packed, sem):
-    copy = pltpu.make_async_copy(weight_ref.at[layer_no], weight, sem)
-    copy.start()
-    current = x_ref[...].astype(F32)
-    copy.wait()
-    queries_of(current, gain_ref, layer_no, weight, packed, payload_ref)
+def first_query_kernel(pool_dev, x_hbm, gain_hbm, weight_hbm, homes_hbm, payload_ref, x, gain, weight, homes, packed, sems):
+    copies = [
+        pltpu.make_async_copy(weight_hbm.at[0], weight, sems.at[0]),
+        pltpu.make_async_copy(x_hbm, x, sems.at[1]),
+        pltpu.make_async_copy(gain_hbm, gain, sems.at[2]),
+        pltpu.make_async_copy(homes_hbm, homes, sems.at[3]),
+    ]
+    for copy in copies:
+        copy.start()
+    copies[3].wait()
+    requests = x.shape[0]
+    n_blocks = homes.shape[1]
+    places = jnp.broadcast_to(homes[...], (requests, n_blocks))
+    store_ids = lax.broadcasted_iota(jnp.int32, (requests, n_blocks), 0)
+    here = lax.div(places, pool_dev) == store_ids
+    slots = jnp.sum(jnp.where(here, lax.rem(places, pool_dev), 0).astype(F32), axis=1, keepdims=True)
+    slots = jnp.broadcast_to(slots, (requests, LANES))
+    copies[1].wait()
+    copies[2].wait()
+    copies[0].wait()
+    queries_of(x[...].astype(F32), gain[0:1, :].astype(F32), weight, packed, payload_ref, slots)
 
 
 def query_kernel(
-    layer_no, x_ref, own, part_a, part_b, part_c, gain_ref, weight_ref, out_ref, payload_ref, weight, packed, sem
+    layer_no, x_ref, own, part_a, part_b, part_c, gain_ref, weight_hbm, out_ref, payload_ref, weight, packed, sem
 ):
-    copy = pltpu.make_async_copy(weight_ref.at[layer_no], weight, sem)
+    copy = pltpu.make_async_copy(weight_hbm.at[layer_no], weight, sem)
     copy.start()
     total = x_ref[...].astype(F32) + ((own[...] + part_a[...]) + (part_b[...] + part_c[...]))
     out_ref[...] = total.astype(BF16)
     current = out_ref[...].astype(F32)
     copy.wait()
-    queries_of(current, gain_ref, layer_no, weight, packed, payload_ref)
-
-
-def attention_kernel(received_ref, tables_ref, bias_ref, kv_ref, out_ref):
-    stores = kv_ref.shape[0]
-    rows = received_ref.shape[0] // stores
-    heads = out_ref.shape[0] // stores
-    totals = jnp.sum(received_ref[...].astype(F32).reshape(stores, rows, LANES), axis=0)
+    gain = gain_ref[layer_no : layer_no + 1, :].astype(F32)
+    queries_of(current, gain, weight, packed, payload_ref)
+
+
+def rotate_kernel(sources, received_ref, tables_ref, out_ref):
+    rows = received_ref.shape[0] // sources
+    heads = out_ref.shape[0] // sources
+    totals = jnp.sum(received_ref[...].astype(F32).reshape(sources, rows, LANES), axis=0)
     squares = totals[heads : heads + 1, :] + totals[heads + 1 : heads + 2, :]
     queries = totals[:heads] * lax.rsqrt(squares / D + EPSILON)
     queries = queries * tables_ref[0:1, :] + pltpu.roll(queries, LANES // 2, 1) * tables_ref[1:2, :]
-    keys = kv_ref[:, 0].reshape(-1, LANES)
-    values = kv_ref[:, 1].reshape(-1, LANES)
-    scores = lax.dot_general(
-        queries.astype(BF16), keys, (((1,), (1,)), ((), ())), preferred_element_type=F32
-    )
-    scores = jnp.where(bias_ref[...] < 0.0, MASK_FILL, scores)
-    terms = jnp.exp(scores - jnp.max(scores, axis=1, keepdims=True))
-    total = jnp.sum(terms, axis=1, keepdims=True)
-    context = jnp.dot(terms.astype(BF16), values, preferred_element_type=F32) / total
-    out_ref[...] = jnp.broadcast_to(context[None], (stores, heads, LANES)).reshape(-1, LANES).astype(BF16)
+    out_ref[...] = jnp.broadcast_to(queries[None], (sources, heads, LANES)).reshape(-1, LANES).astype(BF16)
+
+
+def in_parts(values, count):
+    parts = []
+    for _ in range(count):
+        part = values.astype(BF16).astype(F32)
+        parts.append(part)
+        values = values - part
+    return parts
+
+
+def block_kernel(layer_no, wanted_ref, queries_ref, pool_hbm, out_ref, blocks, sem):
+    copy = pltpu.make_async_copy(pool_hbm.at[layer_no, :, 0], blocks, sem)
+    copy.start()
+    requests = wanted_ref.shape[0]
+    heads = queries_ref.shape[0] // requests
+    queries = queries_ref[...].astype(F32)
+    copy.wait()
+    scores = jnp.concatenate(
+        [
+            lax.dot_general(
+                queries[r * heads : (r + 1) * heads].astype(BF16),
+                blocks[wanted_ref[r], 0],
+                (((1,), (1,)), ((), ())),
+                preferred_element_type=F32,
+            )
+            for r in range(requests)
+        ],
+        axis=0,
+    )
+    block_max = jnp.max(scores, axis=1, keepdims=True)
+    terms = jnp.exp(scores - block_max)
+    block_sum = jnp.sum(terms, axis=1, keepdims=True)
+    acc = jnp.concatenate(
+        [
+            jnp.dot(
+                terms[r * heads : (r + 1) * heads].astype(BF16),
+                blocks[wanted_ref[r], 1],
+                preferred_element_type=F32,
+            )
+            for r in range(requests)
+        ],
+        axis=0,
+    )
+    lane = lax.broadcasted_iota(jnp.int32, scores.shape, 1)
+    stats = jnp.zeros(scores.shape, F32)
+    for place, part in enumerate(in_parts(block_max, 3) + in_parts(block_sum, 2)):
+        stats = jnp.where(lane == place, part, stats)
+    both = jnp.concatenate(
+        [acc.reshape(requests, heads, LANES), stats.reshape(requests, heads, LANES)], axis=1
+    )
+    out_ref[...] = both.reshape(-1, LANES).astype(BF16)
+
+
+def combine_kernel(layer_no, pool_dev, homes_ref, chosen_ref, count_ref, received_ref, out_ref, used):
+    sources = homes_ref.shape[1]
+    heads = out_ref.shape[0] // sources
+    for s in range(sources):
+        used[s] = 0
+    for k in range(chosen_ref.shape[3]):
+        store = lax.div(homes_ref[0, chosen_ref[layer_no, 0, 0, k]], pool_dev)
+        used[store] = jnp.where(k < count_ref[layer_no, 0, 0], 1, used[store])
+    both = received_ref[...].astype(F32).reshape(sources, 2 * heads, LANES)
+    stats = both[:, heads:, :]
+    block_max = stats[:, :, 0:1] + stats[:, :, 1:2] + stats[:, :, 2:3]
+    block_sum = stats[:, :, 3:4] + stats[:, :, 4:5]
+    masked = [jnp.where(used[s] > 0, block_max[s], MASK_FILL) for s in range(sources)]
+    top = functools.reduce(jnp.maximum, masked)
+    numerator = jnp.zeros((heads, LANES), F32)
+    denominator = jnp.zeros((heads, 1), F32)
+    for s in range(sources):
+        rescale = jnp.exp(masked[s] - top)
+        numerator += rescale * both[s, :heads, :]
+        denominator += rescale * block_sum[s]
+    context = numerator / denominator
+    out_ref[...] = jnp.broadcast_to(context[None], (sources, heads, LANES)).reshape(-1, LANES).astype(BF16)
 
 
 def rows_of(packed, requests, blocks):
@@ -161,7 +247,7 @@
     total = x_ref[...].astype(F32) + ((own[...] + part_a[...]) + (part_b[...] + part_c[...]))
     out_ref[...] = total.astype(BF16)
     current = out_ref[...].astype(F32)
-    scaled = (current * gain_ref[pl.ds(layer_no, 1), :].astype(F32)).astype(BF16)
+    scaled = (current * gain_ref[layer_no : layer_no + 1, :].astype(F32)).astype(BF16)
     store_squares(packed, current, stride, blocks)
     store_zeros(packed, requests, stride, range(blocks + 2, half))
     store_zeros(packed, requests, stride, range(half + blocks, stride))
@@ -182,17 +268,6 @@
     gate = totals[:half] * inv
     act = gate / (1.0 + jnp.exp(-gate)) * (totals[half:] * inv)
     out_ref[...] = jnp.broadcast_to(act[None], (sources, half, LANES)).reshape(-1, LANES).astype(BF16)
-
-
-def serve_kernel(layer_no, wanted_ref, pool_ref, out_ref, sem):
-    requests = out_ref.shape[0]
-
-    def start(r, carry):
-        pltpu.make_async_copy(pool_ref.at[layer_no, wanted_ref[r], 0], out_ref.at[r], sem).start()
-        return carry
-
-    lax.fori_loop(0, requests, start, 0)
-    pltpu.make_async_copy(pool_ref.at[layer_no, :, 0], out_ref, sem).wait()
 
 
 def exchange(array, n_req):
@@ -225,7 +300,6 @@
 ):
     n_req = lax.axis_size("req")
     requests, width = hidden.shape
-    most_sel = chosen.shape[3]
     pool_dev = kv_pool.shape[1]
     block_tokens, head_size = kv_pool.shape[4:]
     heads = q_weight.shape[2] // head_size
@@ -237,64 +311,60 @@
     tables = rotary_tables(position, head_size)
     dma = pltpu.SemaphoreType.DMA
 
-    store_ids = jnp.arange(n_req)
-    homes = block_home[0]
-    at_store = homes[None, :] // pool_dev == store_ids[:, None]
-    slots = jnp.sum(jnp.where(at_store, homes[None, :] % pool_dev, 0), axis=1)
-    wanted = exchange(slots.astype(jnp.int32).reshape(n_req, 1), n_req).reshape(n_req)
-    fetched, biases = [], []
-    for layer_no in range(LAYERS):
-        served = call(
-            functools.partial(serve_kernel, layer_no),
-            jax.ShapeDtypeStruct((n_req, 2, block_tokens, head_size), BF16),
-            [SMEM, ANY],
-            [dma],
-            out_specs=ANY,
-        )(wanted, kv_pool)
-        fetched.append(exchange(served, n_req))
-        stores = jnp.sum(
-            jnp.where(chosen[layer_no, 0, 0][:, None] == store_ids[None, :], homes[None, :] // pool_dev, 0),
-            axis=1,
-        )
-        used = jnp.arange(most_sel) < chosen_count[layer_no, 0, 0]
-        valid = jnp.any((stores[None, :] == store_ids[:, None]) & used[None, :], axis=1)
-        bias = jnp.where(valid, 0.0, -1.0).astype(F32)
-        biases.append(jnp.broadcast_to(bias[:, None], (n_req, block_tokens)).reshape(1, -1))
-
     current = hidden
     parts = None
+    wanted = None
     for layer_no in range(LAYERS):
         payload_shape = jax.ShapeDtypeStruct((requests * q_rows, LANES), BF16)
-        scratch = [
-            pltpu.VMEM(q_weight.shape[1:], BF16),
-            pltpu.VMEM((requests * q_rows, LANES), F32),
-            dma,
-        ]
+        packed = pltpu.VMEM((requests * q_rows, LANES), F32)
+        weight = pltpu.VMEM(q_weight.shape[1:], BF16)
         if parts is None:
             payload = call(
-                functools.partial(first_query_kernel, layer_no),
+                functools.partial(first_query_kernel, pool_dev),
                 payload_shape,
-                [VMEM, VMEM, ANY],
-                scratch,
-            )(current, attn_gain, q_weight)
+                [HBM] * 4,
+                [
+                    pltpu.VMEM(hidden.shape, BF16),
+                    pltpu.VMEM(attn_gain.shape, BF16),
+                    weight,
+                    pltpu.VMEM(block_home.shape, jnp.int32),
+                    packed,
+                    dma((4,)),
+                ],
+            )(current, attn_gain, q_weight, block_home)
         else:
             current, payload = call(
                 functools.partial(query_kernel, layer_no),
                 [jax.ShapeDtypeStruct(current.shape, BF16), payload_shape],
-                [VMEM] * 6 + [ANY],
-                scratch,
+                [VMEM] * 6 + [HBM],
+                [weight, packed, dma],
             )(current, *parts, attn_gain, q_weight)
         received = exchange(payload, n_req)
+        if wanted is None:
+            wanted = received.reshape(n_req, q_rows, LANES)[:, heads + 2, 0].astype(jnp.int32)
+        rotated = call(
+            functools.partial(rotate_kernel, n_req),
+            jax.ShapeDtypeStruct((n_req * heads, LANES), BF16),
+            [VMEM] * 2,
+        )(received, tables)
+        queries = exchange(rotated, n_req)
+        stats = call(
+            functools.partial(block_kernel, layer_no),
+            jax.ShapeDtypeStruct((requests * 2 * heads, LANES), BF16),
+            [SMEM, VMEM, HBM],
+            [pltpu.VMEM((pool_dev, 2, block_tokens, head_size), BF16), dma],
+        )(wanted, queries, kv_pool)
         context = call(
-            attention_kernel,
+            functools.partial(combine_kernel, layer_no, pool_dev),
             jax.ShapeDtypeStruct((n_req * heads, LANES), BF16),
-            [VMEM] * 4,
-        )(received, tables, biases[layer_no], fetched[layer_no])
+            [SMEM] * 3 + [VMEM],
+            [pltpu.SMEM((n_req,), jnp.int32)],
+        )(block_home, chosen, chosen_count, exchange(stats, n_req))
         contexts = exchange(context, n_req)
         own = call(
             functools.partial(project_kernel, layer_no, requests),
             jax.ShapeDtypeStruct((requests, width), F32),
-            [VMEM, ANY],
+            [VMEM, HBM],
             [pltpu.VMEM(o_weight.shape[1:], BF16), pltpu.VMEM(contexts.shape, F32), dma],
         )(contexts, o_weight)
         attended, payload = call(
@@ -303,7 +373,7 @@
                 jax.ShapeDtypeStruct(current.shape, BF16),
                 jax.ShapeDtypeStruct((requests * 2 * f_rows, LANES), BF16),
             ],
-            [VMEM] * 6 + [ANY] * 2,
+            [VMEM] * 6 + [HBM] * 2,
             [
                 pltpu.VMEM(gate_weight.shape[1:], BF16),
                 pltpu.VMEM(up_weight.shape[1:], BF16),
@@ -321,7 +391,7 @@
         own = call(
             functools.partial(project_kernel, layer_no, requests),
             jax.ShapeDtypeStruct((requests, width), F32),
-            [VMEM, ANY],
+            [VMEM, HBM],
             [pltpu.VMEM(down_weight.shape[1:], BF16), pltpu.VMEM(acts.shape, F32), dma],
         )(acts, down_weight)
         current, parts = attended, [own] + tp_parts(own)

time: 229 us -> 209 us (0.913)
  blocking collectives: 64.1 us -> 126 us
  waiting for transfers between devices: 78.9 us -> 29.7 us
  starting transfers between devices: 47.8 us -> 28.2 us
  local copies, waits for them, and re-layouts: 19.9 us -> 10.4 us
  other arithmetic: 3.67 us -> 1.28 us
    all_to_all x5 -> x10, blocking collectives: 64.1 us -> 126 us  [exchange(): lax.all_to_all(blocks, 'req', split_axis=0, concat_axis=0, tiled=True)]
    all_to_all x6 -> x2, waiting for transfers between devices: 65 us -> 14.5 us  [exchange(): lax.all_to_all(blocks, 'req', split_axis=0, concat_axis=0, tiled=True)]
    all_to_all x6 -> x2, starting transfers between devices: 27.7 us -> 7.69 us  [exchange(): lax.all_to_all(blocks, 'req', split_axis=0, concat_axis=0, tiled=True)]
    unnamed x40 -> x43, local copies, waits for them, and re-layouts: 18.4 us -> 10.4 us
    pallas_call x5 -> x7, Pallas kernels: 6.31 us -> 6.89 us  [the longest x2 3.91 us: shards(): call(functools.partial(block_kernel, layer_no), jax.ShapeDtypeStruct((req...]
  transfers between devices with their start and end apart: 18 -> 14, of which waited for: 15 -> 8; matrix products, arithmetic and copies ran while one was open for 1% -> 0% of each run, Pallas kernels for 3% -> 0%
where the time goes in v3:
time: 209 us
  blocking collectives  126 us (60%)
  waiting for transfers between devices  29.7 us (14%)
  starting transfers between devices  28.2 us (13%)
  Pallas kernels  12.6 us (6%)
  local copies, waits for them, and re-layouts  10.4 us (5%)
    all_to_all x10, blocking collectives, exchange(): lax.all_to_all(blocks, 'req', split_axis=0, concat_axis=0, tiled=True)  126 us
    ppermute x12, starting transfers between devices, tp_parts(): lax.ppermute(partial_sum, 'tp', [(i, (i + shift) % n_tp) for i in range(n...  20.5 us
    ppermute x12, waiting for transfers between devices, tp_parts(): lax.ppermute(partial_sum, 'tp', [(i, (i + shift) % n_tp) for i in range(n...  15.2 us
    all_to_all x2, waiting for transfers between devices, exchange(): lax.all_to_all(blocks, 'req', split_axis=0, concat_axis=0, tiled=True)  14.5 us
    unnamed x43, local copies, waits for them, and re-layouts  10.4 us
    all_to_all x2, starting transfers between devices, exchange(): lax.all_to_all(blocks, 'req', split_axis=0, concat_axis=0, tiled=True)  7.69 us
  transfers between devices with their start and end apart: 14, of which 8 were waited for; matrix products, arithmetic and copies ran while one was open for 0% of the time, Pallas kernels for 0%

profile of v3, /device:TPU:0, one launch (start us, length us, event | category | flops | bytes accessed | tf_op | source)
XLA Modules:
  0.0 208.5 jit_solution(17814007396554194030)
XLA Ops:
  3.7 15.0 %all_to_all.60 = bf16[32,16,128]{2,1,0:T(8,128)(2,1)S(1)} all-to-all(bf16[32,16,128]{2,1,0:T(8,128)(2,1)S(1)} %bitcast.32), channel_id=1, replica_groups=mesh['req'=32,'tp'=4] {'req'}, dimensions={0} | all-to-all | bytes 262144 | tf_op jit(solution)/shard_map/all_to_all | solution.py:276
  20.2 3.8 %all-to-all-start.1 = ((bf16[32,8,128]{2,1,0:T(8,128)(2,1)}), bf16[32,8,128]{2,1,0:T(8,128)(2,1)S(1)}, u32[]{:S(2)}, u32[]{:S(2)}) async-start(bf16[32,8,128]{2,1,0:T(8,128)(2,1)} %bitcast.2), calls=%async_computation.1 | async-start | bytes 131072 | tf_op jit(solution)/shard_map/all_to_all | solution.py:276
  24.7 6.8 %all-to-all-done.1 = bf16[32,8,128]{2,1,0:T(8,128)(2,1)S(1)} async-done(((bf16[32,8,128]{2,1,0:T(8,128)(2,1)}), bf16[32,8,128]{2,1,0:T(8,128)(2,1)S(1)}, u32[]{:S(2)}, u32[]{:S(2)}) %all-to-all-start.1) | async-done | bytes 65568 | tf_op jit(solution)/shard_map/all_to_all | solution.py:276
  31.5 2.2 %copy-done = bf16[2,32,1,2,128,128]{5,4,3,2,1,0:T(8,128)(2,1)S(1)} copy-done((bf16[2,32,1,2,128,128]{5,4,3,2,1,0:T(8,128)(2,1)S(1)}, bf16[2,32,1,2,128,128]{5,4,3,2,1,0:T(8,128)(2,1)}, u32[]{:S(2)}) %copy-start) | copy-done | bytes 4194328
  33.7 2.3 %shard_map.129 = bf16[512,128]{1,0:T(8,128)(2,1)} custom-call(s32[32]{0:T(128)S(1)} %fusion.wanted_ref, bf16[256,128]{1,0:T(8,128)(2,1)S(1)} %bitcast.38, bf16[2,32,1,2,128,128]{5,4,3,2,1,0:T(8,128)(2,1)S(1)} %copy-done), custom_call_target="tpu_custom_call" | custom-call | tf_op jit(solution)/shard_map/pallas_call | solution.py:351
  36.0 3.9 %all-to-all-start.2 = ((bf16[32,16,128]{2,1,0:T(8,128)(2,1)}), bf16[32,16,128]{2,1,0:T(8,128)(2,1)S(1)}, u32[]{:S(2)}, u32[]{:S(2)}) async-start(bf16[32,16,128]{2,1,0:T(8,128)(2,1)} %bitcast.4), calls=%async_computation.2 | async-start | bytes 262144 | tf_op jit(solution)/shard_map/all_to_all | solution.py:276
  39.9 7.7 %all-to-all-done.2 = bf16[32,16,128]{2,1,0:T(8,128)(2,1)S(1)} async-done(((bf16[32,16,128]{2,1,0:T(8,128)(2,1)}), bf16[32,16,128]{2,1,0:T(8,128)(2,1)S(1)}, u32[]{:S(2)}, u32[]{:S(2)}) %all-to-all-start.2) | async-done | bytes 131104 | tf_op jit(solution)/shard_map/all_to_all | solution.py:276
  48.5 11.0 %all_to_all.61 = bf16[32,8,128]{2,1,0:T(8,128)(2,1)S(1)} all-to-all(bf16[32,8,128]{2,1,0:T(8,128)(2,1)S(1)} %bitcast.42), channel_id=1, replica_groups=mesh['req'=32,'tp'=4] {'req'}, dimensions={0} | all-to-all | bytes 131072 | tf_op jit(solution)/shard_map/all_to_all | solution.py:276
  59.7 4.1 %collective-permute-start.2 = (f32[32,256]{1,0:T(8,128)S(1)}, f32[32,256]{1,0:T(8,128)S(1)}, u32[]{:S(2)}, u32[]{:S(2)}) collective-permute-start(f32[32,256]{1,0:T(8,128)S(1)} %shard_map.131.own), channel_id=1, source_target_pairs={{0,3},{1,0},{2,1},{3,2},{4,7},{5,4},{6,5},{7,6},{8,11},{9,8},{10,9... | collective-permute-start | bytes 98312 | tf_op jit(solution)/shard_map/ppermute | solution.py:282
  65.7 3.6 %collective-permute-done.1.part_b = f32[32,256]{1,0:T(8,128)S(1)} collective-permute-done((f32[32,256]{1,0:T(8,128)S(1)}, f32[32,256]{1,0:T(8,128)S(1)}, u32[]{:S(2)}, u32[]{:S(2)}) %collective-permute-start.1) | collective-permute-done | bytes 32800 | tf_op jit(solution)/shard_map/ppermute | solution.py:282
  74.9 15.3 %all_to_all.62 = bf16[32,64,128]{2,1,0:T(8,128)(2,1)S(1)} all-to-all(bf16[32,64,128]{2,1,0:T(8,128)(2,1)S(1)} %bitcast.34), channel_id=1, replica_groups=mesh['req'=32,'tp'=4] {'req'}, dimensions={0} | all-to-all | bytes 1048576 | tf_op jit(solution)/shard_map/all_to_all | solution.py:276
  90.3 12.6 %all_to_all.63 = bf16[32,32,128]{2,1,0:T(8,128)(2,1)S(1)} all-to-all(bf16[32,32,128]{2,1,0:T(8,128)(2,1)S(1)} %bitcast.26), channel_id=1, replica_groups=mesh['req'=32,'tp'=4] {'req'}, dimensions={0} | all-to-all | bytes 524288 | tf_op jit(solution)/shard_map/all_to_all | solution.py:276
  103.8 3.2 %collective-permute-start.5 = (f32[32,256]{1,0:T(8,128)S(1)}, f32[32,256]{1,0:T(8,128)S(1)}, u32[]{:S(2)}, u32[]{:S(2)}) collective-permute-start(f32[32,256]{1,0:T(8,128)S(1)} %shard_map.134.own), channel_id=1, source_target_pairs={{0,3},{1,0},{2,1},{3,2},{4,7},{5,4},{6,5},{7,6},{8,11},{9,8},{10,9... | collective-permute-start | bytes 98312 | tf_op jit(solution)/shard_map/ppermute | solution.py:282
  108.7 3.9 %collective-permute-done.4.part_b = f32[32,256]{1,0:T(8,128)S(1)} collective-permute-done((f32[32,256]{1,0:T(8,128)S(1)}, f32[32,256]{1,0:T(8,128)S(1)}, u32[]{:S(2)}, u32[]{:S(2)}) %collective-permute-start.4) | collective-permute-done | bytes 32800 | tf_op jit(solution)/shard_map/ppermute | solution.py:282
  112.9 11.6 %all_to_all.64 = bf16[32,16,128]{2,1,0:T(8,128)(2,1)S(1)} all-to-all(bf16[32,16,128]{2,1,0:T(8,128)(2,1)S(1)} %bitcast.45), channel_id=1, replica_groups=mesh['req'=32,'tp'=4] {'req'}, dimensions={0} | all-to-all | bytes 262144 | tf_op jit(solution)/shard_map/all_to_all | solution.py:276
  124.6 10.9 %all_to_all.65 = bf16[32,8,128]{2,1,0:T(8,128)(2,1)S(1)} all-to-all(bf16[32,8,128]{2,1,0:T(8,128)(2,1)S(1)} %bitcast.40), channel_id=1, replica_groups=mesh['req'=32,'tp'=4] {'req'}, dimensions={0} | all-to-all | bytes 131072 | tf_op jit(solution)/shard_map/all_to_all | solution.py:276
  137.2 11.2 %all_to_all.66 = bf16[32,16,128]{2,1,0:T(8,128)(2,1)S(1)} all-to-all(bf16[32,16,128]{2,1,0:T(8,128)(2,1)S(1)} %bitcast.31), channel_id=1, replica_groups=mesh['req'=32,'tp'=4] {'req'}, dimensions={0} | all-to-all | bytes 262144 | tf_op jit(solution)/shard_map/all_to_all | solution.py:276
  149.2 11.0 %all_to_all.67 = bf16[32,8,128]{2,1,0:T(8,128)(2,1)S(1)} all-to-all(bf16[32,8,128]{2,1,0:T(8,128)(2,1)S(1)} %bitcast.41), channel_id=1, replica_groups=mesh['req'=32,'tp'=4] {'req'}, dimensions={0} | all-to-all | bytes 131072 | tf_op jit(solution)/shard_map/all_to_all | solution.py:276
  160.5 3.2 %collective-permute-start.8 = (f32[32,256]{1,0:T(8,128)S(1)}, f32[32,256]{1,0:T(8,128)S(1)}, u32[]{:S(2)}, u32[]{:S(2)}) collective-permute-start(f32[32,256]{1,0:T(8,128)S(1)} %shard_map.139.own), channel_id=1, source_target_pairs={{0,3},{1,0},{2,1},{3,2},{4,7},{5,4},{6,5},{7,6},{8,11},{9,8},{10,9... | collective-permute-start | bytes 98312 | tf_op jit(solution)/shard_map/ppermute | solution.py:282
  165.4 3.7 %collective-permute-done.7.part_b = f32[32,256]{1,0:T(8,128)S(1)} collective-permute-done((f32[32,256]{1,0:T(8,128)S(1)}, f32[32,256]{1,0:T(8,128)S(1)}, u32[]{:S(2)}, u32[]{:S(2)}) %collective-permute-start.7) | collective-permute-done | bytes 32800 | tf_op jit(solution)/shard_map/ppermute | solution.py:282
  170.7 15.1 %all_to_all.68 = bf16[32,64,128]{2,1,0:T(8,128)(2,1)S(1)} all-to-all(bf16[32,64,128]{2,1,0:T(8,128)(2,1)S(1)} %bitcast.33), channel_id=1, replica_groups=mesh['req'=32,'tp'=4] {'req'}, dimensions={0} | all-to-all | bytes 1048576 | tf_op jit(solution)/shard_map/all_to_all | solution.py:276
  185.9 12.4 %all_to_all.69 = bf16[32,32,128]{2,1,0:T(8,128)(2,1)S(1)} all-to-all(bf16[32,32,128]{2,1,0:T(8,128)(2,1)S(1)} %bitcast.27), channel_id=1, replica_groups=mesh['req'=32,'tp'=4] {'req'}, dimensions={0} | all-to-all | bytes 524288 | tf_op jit(solution)/shard_map/all_to_all | solution.py:276
  199.2 3.2 %collective-permute-start.11 = (f32[32,256]{1,0:T(8,128)S(1)}, f32[32,256]{1,0:T(8,128)S(1)}, u32[]{:S(2)}, u32[]{:S(2)}) collective-permute-start(f32[32,256]{1,0:T(8,128)S(1)} %shard_map.142), channel_id=1, source_target_pairs={{0,3},{1,0},{2,1},{3,2},{4,7},{5,4},{6,5},{7,6},{8,11},{9,8},{10,9... | collective-permute-start | bytes 98312 | tf_op jit(solution)/shard_map/ppermute | solution.py:282
  204.0 3.9 %collective-permute-done.10 = f32[32,256]{1,0:T(8,128)S(1)} collective-permute-done((f32[32,256]{1,0:T(8,128)S(1)}, f32[32,256]{1,0:T(8,128)S(1)}, u32[]{:S(2)}, u32[]{:S(2)}) %collective-permute-start.10) | collective-permute-done | bytes 32800 | tf_op jit(solution)/shard_map/ppermute | solution.py:282
  (75 shorter events, 26.6 us)
Async XLA Ops:
  3.3 44.3 %copy-start.13 = (s32[1,32]{1,0:T(1,128)S(1)}, s32[1,32]{1,0:T(1,128)}, u32[]{:S(2)}) copy-start(s32[1,32]{1,0:T(1,128)} %homes_ref.3) | copy-start | bytes 388
  3.3 44.3 %copy-start.14 = (s32[2,1,1,24]{3,2,1,0:T(1,128)S(1)}, s32[2,1,1,24]{3,2,1,0:T(1,128)}, u32[]{:S(2)}) copy-start(s32[2,1,1,24]{3,2,1,0:T(1,128)} %chosen_ref.3) | copy-start | bytes 580
  3.3 56.2 %copy-start.9 = (bf16[2,1024,256]{2,1,0:T(8,128)(2,1)S(1)}, bf16[2,1024,256]{2,1,0:T(8,128)(2,1)}, u32[]{:S(2)}) copy-start(bf16[2,1024,256]{2,1,0:T(8,128)(2,1)} %weight_ref.6) | copy-start | bytes 3145732
  3.7 65.6 %copy-start.11 = (bf16[32,256]{1,0:T(8,128)(2,1)S(1)}, bf16[32,256]{1,0:T(8,128)(2,1)}, u32[]{:S(2)}) copy-start(bf16[32,256]{1,0:T(8,128)(2,1)} %x_ref.1) | copy-start | bytes 49156
  3.7 65.6 %copy-start.19 = (bf16[2,256]{1,0:T(2,128)(2,1)S(1)}, bf16[2,256]{1,0:T(2,128)(2,1)}, u32[]{:S(2)}) copy-start(bf16[2,256]{1,0:T(2,128)(2,1)} %gain_ref.5) | copy-start | bytes 3076
  20.2 11.3 %all-to-all-start.1 = ((bf16[32,8,128]{2,1,0:T(8,128)(2,1)}), bf16[32,8,128]{2,1,0:T(8,128)(2,1)S(1)}, u32[]{:S(2)}, u32[]{:S(2)}) async-start(bf16[32,8,128]{2,1,0:T(8,128)(2,1)} %bitcast.2), calls=%async_computation.1 | async-start | bytes 131072 | tf_op jit(solution)/shard_map/all_to_all | solution.py:276
  36.0 11.7 %all-to-all-start.2 = ((bf16[32,16,128]{2,1,0:T(8,128)(2,1)}), bf16[32,16,128]{2,1,0:T(8,128)(2,1)S(1)}, u32[]{:S(2)}, u32[]{:S(2)}) async-start(bf16[32,16,128]{2,1,0:T(8,128)(2,1)} %bitcast.4), calls=%async_computation.2 | async-start | bytes 262144 | tf_op jit(solution)/shard_map/all_to_all | solution.py:276
  59.7 6.0 %collective-permute-start.2 = (f32[32,256]{1,0:T(8,128)S(1)}, f32[32,256]{1,0:T(8,128)S(1)}, u32[]{:S(2)}, u32[]{:S(2)}) collective-permute-start(f32[32,256]{1,0:T(8,128)S(1)} %shard_map.131.own), channel_id=1, source_target_pairs={{0,3},{1,0},{2,1},{3,2},{4,7},{5,4},{6,5},{7,6},{8,11},{9,8},{10,9... | collective-permute-start | bytes 98312 | tf_op jit(solution)/shard_map/ppermute | solution.py:282
  63.8 5.5 %collective-permute-start.1 = (f32[32,256]{1,0:T(8,128)S(1)}, f32[32,256]{1,0:T(8,128)S(1)}, u32[]{:S(2)}, u32[]{:S(2)}) collective-permute-start(f32[32,256]{1,0:T(8,128)S(1)} %shard_map.131.own), channel_id=1, source_target_pairs={{0,1},{1,2},{2,3},{3,0},{4,5},{5,6},{6,7},{7,4},{8,9},{9,10},{10,1... | collective-permute-start | bytes 98312 | tf_op jit(solution)/shard_map/ppermute | solution.py:282
  63.8 5.5 %collective-permute-start = (f32[32,256]{1,0:T(8,128)S(1)}, f32[32,256]{1,0:T(8,128)S(1)}, u32[]{:S(2)}, u32[]{:S(2)}) collective-permute-start(f32[32,256]{1,0:T(8,128)S(1)} %shard_map.131.own), channel_id=1, source_target_pairs={{0,2},{1,3},{2,0},{3,1},{4,6},{5,7},{6,4},{7,5},{8,10},{9,11},{10,... | collective-permute-start | bytes 98312 | tf_op jit(solution)/shard_map/ppermute | solution.py:282
  74.9 37.6 %copy-start.8 = (bf16[2,256,1024]{2,1,0:T(8,128)(2,1)S(1)}, bf16[2,256,1024]{2,1,0:T(8,128)(2,1)}, u32[]{:S(2)}) copy-start(bf16[2,256,1024]{2,1,0:T(8,128)(2,1)} %weight_hbm.3) | copy-start | bytes 3145732
  74.9 49.5 %copy-start.16 = (f32[2,128]{1,0:T(2,128)S(1)}, f32[2,128]{1,0:T(2,128)}, u32[]{:S(2)}) copy-start(f32[2,128]{1,0:T(2,128)} %constant.2.clone.tables_ref) | copy-start | bytes 3076
  90.2 45.3 %copy-start.1 = (bf16[2,32,1,2,128,128]{5,4,3,2,1,0:T(8,128)(2,1)S(1)}, bf16[2,32,1,2,128,128]{5,4,3,2,1,0:T(8,128)(2,1)}, u32[]{:S(2)}) copy-start(bf16[2,32,1,2,128,128]{5,4,3,2,1,0:T(8,128)(2,1)} %pool_hbm.3) | copy-start | bytes 12582916
  103.8 4.8 %collective-permute-start.5 = (f32[32,256]{1,0:T(8,128)S(1)}, f32[32,256]{1,0:T(8,128)S(1)}, u32[]{:S(2)}, u32[]{:S(2)}) collective-permute-start(f32[32,256]{1,0:T(8,128)S(1)} %shard_map.134.own), channel_id=1, source_target_pairs={{0,3},{1,0},{2,1},{3,2},{4,7},{5,4},{6,5},{7,6},{8,11},{9,8},{10,9... | collective-permute-start | bytes 98312 | tf_op jit(solution)/shard_map/ppermute | solution.py:282
  107.1 5.5 %collective-permute-start.4 = (f32[32,256]{1,0:T(8,128)S(1)}, f32[32,256]{1,0:T(8,128)S(1)}, u32[]{:S(2)}, u32[]{:S(2)}) collective-permute-start(f32[32,256]{1,0:T(8,128)S(1)} %shard_map.134.own), channel_id=1, source_target_pairs={{0,1},{1,2},{2,3},{3,0},{4,5},{5,6},{6,7},{7,4},{8,9},{9,10},{10,1... | collective-permute-start | bytes 98312 | tf_op jit(solution)/shard_map/ppermute | solution.py:282
  107.1 5.5 %collective-permute-start.3 = (f32[32,256]{1,0:T(8,128)S(1)}, f32[32,256]{1,0:T(8,128)S(1)}, u32[]{:S(2)}, u32[]{:S(2)}) collective-permute-start(f32[32,256]{1,0:T(8,128)S(1)} %shard_map.134.own), channel_id=1, source_target_pairs={{0,2},{1,3},{2,0},{3,1},{4,6},{5,7},{6,4},{7,5},{8,10},{9,11},{10,... | collective-permute-start | bytes 98312 | tf_op jit(solution)/shard_map/ppermute | solution.py:282
  112.5 56.6 %copy-start.3 = (bf16[2,256,3584]{2,1,0:T(8,128)(2,1)S(1)}, bf16[2,256,3584]{2,1,0:T(8,128)(2,1)}, u32[]{:S(2)}) copy-start(bf16[2,256,3584]{2,1,0:T(8,128)(2,1)} %gate_ref.3) | copy-start | bytes 11010052
  112.6 56.6 %copy-start.5 = (bf16[2,256,3584]{2,1,0:T(8,128)(2,1)S(1)}, bf16[2,256,3584]{2,1,0:T(8,128)(2,1)}, u32[]{:S(2)}) copy-start(bf16[2,256,3584]{2,1,0:T(8,128)(2,1)} %up_ref.3) | copy-start | bytes 11010052
  160.5 5.0 %collective-permute-start.8 = (f32[32,256]{1,0:T(8,128)S(1)}, f32[32,256]{1,0:T(8,128)S(1)}, u32[]{:S(2)}, u32[]{:S(2)}) collective-permute-start(f32[32,256]{1,0:T(8,128)S(1)} %shard_map.139.own), channel_id=1, source_target_pairs={{0,3},{1,0},{2,1},{3,2},{4,7},{5,4},{6,5},{7,6},{8,11},{9,8},{10,9... | collective-permute-start | bytes 98312 | tf_op jit(solution)/shard_map/ppermute | solution.py:282
  163.7 5.5 %collective-permute-start.7 = (f32[32,256]{1,0:T(8,128)S(1)}, f32[32,256]{1,0:T(8,128)S(1)}, u32[]{:S(2)}, u32[]{:S(2)}) collective-permute-start(f32[32,256]{1,0:T(8,128)S(1)} %shard_map.139.own), channel_id=1, source_target_pairs={{0,1},{1,2},{2,3},{3,0},{4,5},{5,6},{6,7},{7,4},{8,9},{9,10},{10,1... | collective-permute-start | bytes 98312 | tf_op jit(solution)/shard_map/ppermute | solution.py:282
  163.7 5.5 %collective-permute-start.6 = (f32[32,256]{1,0:T(8,128)S(1)}, f32[32,256]{1,0:T(8,128)S(1)}, u32[]{:S(2)}, u32[]{:S(2)}) collective-permute-start(f32[32,256]{1,0:T(8,128)S(1)} %shard_map.139.own), channel_id=1, source_target_pairs={{0,2},{1,3},{2,0},{3,1},{4,6},{5,7},{6,4},{7,5},{8,10},{9,11},{10,... | collective-permute-start | bytes 98312 | tf_op jit(solution)/shard_map/ppermute | solution.py:282
  199.2 4.8 %collective-permute-start.11 = (f32[32,256]{1,0:T(8,128)S(1)}, f32[32,256]{1,0:T(8,128)S(1)}, u32[]{:S(2)}, u32[]{:S(2)}) collective-permute-start(f32[32,256]{1,0:T(8,128)S(1)} %shard_map.142), channel_id=1, source_target_pairs={{0,3},{1,0},{2,1},{3,2},{4,7},{5,4},{6,5},{7,6},{8,11},{9,8},{10,9... | collective-permute-start | bytes 98312 | tf_op jit(solution)/shard_map/ppermute | solution.py:282
  202.4 5.5 %collective-permute-start.10 = (f32[32,256]{1,0:T(8,128)S(1)}, f32[32,256]{1,0:T(8,128)S(1)}, u32[]{:S(2)}, u32[]{:S(2)}) collective-permute-start(f32[32,256]{1,0:T(8,128)S(1)} %shard_map.142), channel_id=1, source_target_pairs={{0,1},{1,2},{2,3},{3,0},{4,5},{5,6},{6,7},{7,4},{8,9},{9,10},{10,1... | collective-permute-start | bytes 98312 | tf_op jit(solution)/shard_map/ppermute | solution.py:282
  202.4 5.5 %collective-permute-start.9 = (f32[32,256]{1,0:T(8,128)S(1)}, f32[32,256]{1,0:T(8,128)S(1)}, u32[]{:S(2)}, u32[]{:S(2)}) collective-permute-start(f32[32,256]{1,0:T(8,128)S(1)} %shard_map.142), channel_id=1, source_target_pairs={{0,2},{1,3},{2,0},{3,1},{4,6},{5,7},{6,4},{7,5},{8,10},{9,11},{10,... | collective-permute-start | bytes 98312 | tf_op jit(solution)/shard_map/ppermute | solution.py:282
  (11 other events, 113.9 us)

commit v4 on v3

v4 whole, which is shorter than its diff:
```python
import functools
import math

import jax
import jax.numpy as jnp
import numpy as np
from jax import lax
from jax.experimental import pallas as pl
from jax.experimental.pallas import tpu as pltpu
from jax.sharding import PartitionSpec as P

D = 8192
LAYERS = 2
LANES = 128

MASK_FILL = -1e30
EPSILON = 1e-05

VMEM = pl.BlockSpec(memory_space=pltpu.VMEM)
SMEM = pl.BlockSpec(memory_space=pltpu.SMEM)
HBM = pl.BlockSpec(memory_space=pltpu.HBM)
F32 = jnp.float32
BF16 = jnp.bfloat16


def rotary_tables(position, head_size):
    freq_idx = np.arange(head_size // 2)
    angles = position * np.exp(freq_idx * (-2.0 * math.log(500000.0) / head_size))
    cosine, sine_part = np.cos(angles), np.sin(angles)
    scale = head_size**-0.5
    tables = np.stack([np.concatenate([cosine, cosine]), np.concatenate([-sine_part, sine_part])])
    return jnp.asarray(tables * scale, F32)


def call(kernel, out_shape, in_specs, scratch=(), limit=16, out_specs=None, flops=0, nbytes=0):
    return pl.pallas_call(
        kernel,
        out_shape=out_shape,
        in_specs=in_specs,
        out_specs=out_specs if out_specs is not None else jax.tree.map(lambda _: VMEM, out_shape),
        scratch_shapes=list(scratch),
        compiler_params=pltpu.CompilerParams(vmem_limit_bytes=limit * 1024 * 1024),
        cost_estimate=pl.CostEstimate(flops=flops, bytes_accessed=nbytes, transcendentals=0),
    )


def halves(values):
    middle = values.shape[0] // 2
    first = lax.rem(lax.axis_index("req"), 2) == 0
    keep = jnp.where(first, values[:middle], values[middle:])
    send = jnp.where(first, values[middle:], values[:middle])
    return keep, send


def joined(own, other):
    first = lax.rem(lax.axis_index("req"), 2) == 0
    return jnp.concatenate([jnp.where(first, own, other), jnp.where(first, other, own)], axis=0)


def squares_in_lanes(current):
    squares = jnp.sum(current * current, axis=1, keepdims=True)
    high = squares.astype(BF16).astype(F32)
    lane = lax.broadcasted_iota(jnp.int32, (current.shape[0], LANES), 1)
    return jnp.where(lane == 0, high, jnp.where(lane == 1, squares - high, 0.0))


def store_blocks(packed, product, stride, row):
    requests, width = product.shape
    for k in range(width // LANES):
        packed[pl.ds(row + k, requests, stride=stride), :] = product[:, k * LANES : (k + 1) * LANES]


def spread(packed, values, stride):
    for k in range(stride):
        packed[pl.ds(k, values.shape[0], stride=stride), :] = values
    return packed[...]


def rows_of(packed, requests, blocks):
    stride = packed.shape[0] // requests
    return jnp.concatenate(
        [packed[pl.ds(k, requests, stride=stride), :].astype(BF16) for k in range(blocks)], axis=1
    )


def repeat_into(out_ref, values):
    rows = values.shape[0]
    for i in range(out_ref.shape[0] // rows):
        out_ref[i * rows : (i + 1) * rows, :] = values


def queries_of(current, gain, weight, packed, keep_ref, send_ref, table=None):
    requests = current.shape[0]
    heads = weight.shape[1] // LANES
    scaled = (current * gain).astype(BF16)
    product = jnp.dot(scaled, weight[...], preferred_element_type=F32)
    store_blocks(packed, product, heads, 0)
    extra = squares_in_lanes(current)
    if table is not None:
        extra = extra + table
    rows = packed.shape[0] // 2
    keep, send = halves(packed[...])
    keep_ref[:rows, :] = keep
    send_ref[:rows, :] = send.astype(BF16)
    keep, send = halves(extra)
    keep_ref[rows:, :] = keep
    send_ref[rows:, :] = send.astype(BF16)


def slot_table(homes, chosen, counts, pool_dev, requests):
    n_blocks = homes.shape[1]
    shape = (n_blocks, n_blocks)
    row = lax.broadcasted_iota(jnp.int32, shape, 0)
    col = lax.broadcasted_iota(jnp.int32, shape, 1)
    places = jnp.broadcast_to(homes, shape)
    here = lax.div(places, pool_dev) == row

    def across(column):
        return jnp.sum(jnp.where(row == col, column, 0.0), axis=0, keepdims=True)

    slots = jnp.sum(jnp.where(here, lax.rem(places, pool_dev), 0).astype(F32), axis=1, keepdims=True)
    found = [jnp.zeros((1, n_blocks), F32), across(slots)]
    for layer_no in range(LAYERS):
        listed = chosen[layer_no]
        entry = lax.broadcasted_iota(jnp.int32, (n_blocks, listed.shape[1]), 1)
        block = lax.broadcasted_iota(jnp.int32, (n_blocks, listed.shape[1]), 0)
        hit = (listed == block) & (entry < counts[layer_no])
        taken = across(jnp.max(jnp.where(hit, 1.0, 0.0), axis=1, keepdims=True))
        found.append(across(jnp.max(jnp.where(here, taken, 0.0), axis=1, keepdims=True)))
    line = jnp.concatenate(found, axis=1)
    mine = lax.broadcasted_iota(jnp.int32, (requests, LANES), 0) == lax.axis_index("req")
    return jnp.where(mine, line, 0.0)


def first_query_kernel(
    pool_dev,
    x_hbm,
    gain_hbm,
    weight_hbm,
    homes_hbm,
    chosen_hbm,
    count_hbm,
    keep_ref,
    send_ref,
    x,
    gain,
    weight,
    homes,
    chosen,
    counts,
    packed,
    sems,
):
    copies = [
        pltpu.make_async_copy(source, target, sems.at[i])
        for i, (source, target) in enumerate(
            [
                (homes_hbm, homes),
                (chosen_hbm, chosen),
                (count_hbm, counts),
                (x_hbm, x),
                (gain_hbm, gain),
                (weight_hbm.at[0], weight),
            ]
        )
    ]
    for copy in copies:
        copy.start()
    for copy in copies[:3]:
        copy.wait()
    lists = [chosen[i : i + 1, :] for i in range(LAYERS)]
    limits = [counts[i : i + 1, :] for i in range(LAYERS)]
    table = slot_table(homes[...], lists, limits, pool_dev, x.shape[0])
    for copy in copies[3:]:
        copy.wait()
    queries_of(x[...].astype(F32), gain[0:1, :].astype(F32), weight, packed, keep_ref, send_ref, table)


def query_kernel(
    layer_no, x_ref, own, part_a, part_b, part_c, gain_ref, weight_hbm, out_ref, keep_ref, send_ref, weight, packed, sem
):
    copy = pltpu.make_async_copy(weight_hbm.at[layer_no], weight, sem)
    copy.start()
    total = x_ref[...].astype(F32) + ((own[...] + part_a[...]) + (part_b[...] + part_c[...]))
    out_ref[...] = total.astype(BF16)
    current = out_ref[...].astype(F32)
    copy.wait()
    gain = gain_ref[layer_no : layer_no + 1, :].astype(F32)
    queries_of(current, gain, weight, packed, keep_ref, send_ref)


def pair_sum_kernel(keep_ref, received_ref, out_ref):
    repeat_into(out_ref, (keep_ref[...] + received_ref[...].astype(F32)).astype(BF16))


def rotate_kernel(heads, received_ref, tables_ref, out_ref, factors):
    rows = factors.shape[0]
    sources = received_ref.shape[0] // (rows + rows // heads)
    totals = jnp.sum(received_ref[...].astype(F32).reshape(sources, -1, LANES), axis=0)
    extra = totals[rows:]
    inv = lax.rsqrt((extra[:, 0:1] + extra[:, 1:2]) / D + EPSILON)
    queries = totals[:rows] * spread(factors, jnp.broadcast_to(inv, extra.shape), heads)
    queries = queries * tables_ref[0:1, :] + pltpu.roll(queries, LANES // 2, 1) * tables_ref[1:2, :]
    out_ref[:rows, :] = queries.astype(BF16)
    if out_ref.shape[0] > rows:
        out_ref[rows:, :] = extra.astype(BF16)


def in_parts(values, count):
    parts = []
    for _ in range(count):
        part = values.astype(BF16).astype(F32)
        parts.append(part)
        values = values - part
    return parts


def stats_in_lanes(block_max, block_sum):
    shape = (block_max.shape[0], LANES)
    lane = lax.broadcasted_iota(jnp.int32, shape, 1)
    stats = jnp.zeros(shape, F32)
    for place, part in enumerate(in_parts(block_max, 3) + in_parts(block_sum, 2)):
        stats = jnp.where(lane == place, part, stats)
    return stats


def block_kernel(
    layer_no, own_ref, other_ref, own_table, other_table, pool_hbm, keep_ref, send_ref, blocks, packed, sem
):
    copy = pltpu.make_async_copy(pool_hbm.at[layer_no, :, 0], blocks, sem)
    copy.start()
    rows = packed.shape[0]
    n_slots = blocks.shape[0]
    requests = 2 * (own_table.shape[0] - rows // 2)
    heads = rows // requests
    me = lax.axis_index("req")
    queries = joined(own_ref[: rows // 2].astype(F32), other_ref[: rows // 2].astype(F32))
    table = joined(own_table[rows // 2 :].astype(F32), other_table[rows // 2 :].astype(F32))
    lane = lax.broadcasted_iota(jnp.int32, table.shape, 1)
    slots = jnp.sum(jnp.where(lane == n_slots + me, table, 0.0), axis=1, keepdims=True)
    used = jnp.sum(jnp.where(lane == (2 + layer_no) * n_slots + me, table, 0.0), axis=1, keepdims=True)
    used = spread(packed, jnp.broadcast_to(used, table.shape), heads)
    request = lax.broadcasted_iota(jnp.int32, (requests, rows), 0)
    column = lax.broadcasted_iota(jnp.int32, (requests, rows), 1)
    target = jnp.where(
        lax.div(column, heads) == request, slots * heads + lax.rem(column, heads).astype(F32), 0.0
    )
    target = jnp.sum(target, axis=0, keepdims=True).astype(jnp.int32)
    place = lax.broadcasted_iota(jnp.int32, (rows, rows), 0) == target
    by_slot = jnp.where(place, 1.0, 0.0)
    queries = jnp.dot(by_slot.astype(BF16), queries.astype(BF16), preferred_element_type=F32)
    copy.wait()
    scores = jnp.concatenate(
        [
            lax.dot_general(
                queries[p * heads : (p + 1) * heads].astype(BF16),
                blocks[p, 0],
                (((1,), (1,)), ((), ())),
                preferred_element_type=F32,
            )
            for p in range(n_slots)
        ],
        axis=0,
    )
    block_max = jnp.max(scores, axis=1, keepdims=True)
    terms = jnp.exp(scores - block_max)
    block_sum = jnp.sum(terms, axis=1, keepdims=True)
    acc = jnp.concatenate(
        [
            jnp.dot(
                terms[p * heads : (p + 1) * heads].astype(BF16), blocks[p, 1], preferred_element_type=F32
            )
            for p in range(n_slots)
        ],
        axis=0,
    )
    both = jnp.concatenate([acc, stats_in_lanes(block_max, block_sum)], axis=1).astype(BF16)
    both = jnp.dot(by_slot.T.astype(BF16), both, preferred_element_type=F32)
    lane = lax.broadcasted_iota(jnp.int32, (rows, LANES), 1)
    unused = jnp.where(lane == 0, MASK_FILL, 0.0)
    stats = jnp.where((used > 0.0) | (lane > 2), both[:, LANES:], unused)
    for at, values in ((0, both[:, :LANES]), (rows // 2, stats)):
        keep, send = halves(values)
        keep_ref[at : at + rows // 2, :] = keep
        send_ref[at : at + rows // 2, :] = send.astype(BF16)


def merge_kernel(keep_ref, received_ref, out_ref):
    rows = keep_ref.shape[0] // 2
    sides = []
    for both in (keep_ref[...], received_ref[...].astype(F32)):
        stats = both[rows:]
        block_max = stats[:, 0:1] + stats[:, 1:2] + stats[:, 2:3]
        sides.append((block_max, stats[:, 3:4] + stats[:, 4:5], both[:rows]))
    top = jnp.maximum(sides[0][0], sides[1][0])
    rescale = [jnp.exp(side[0] - top) for side in sides]
    total = rescale[0] * sides[0][1] + rescale[1] * sides[1][1]
    acc = rescale[0] * sides[0][2] + rescale[1] * sides[1][2]
    stats = stats_in_lanes(top, total).T
    extra = out_ref.shape[0] // 16 - rows
    repeat_into(out_ref, jnp.concatenate([acc, stats[:extra]], axis=0).astype(BF16))


def combine_kernel(sources, received_ref, out_ref):
    rows = out_ref.shape[0]
    both = received_ref[...].astype(F32).reshape(sources, -1, LANES)
    stats = [both[s, rows : rows + 8, :] for s in range(sources)]
    block_max = jnp.concatenate([x[0:1] + x[1:2] + x[2:3] for x in stats], axis=0)
    block_sum = jnp.concatenate([x[3:4] + x[4:5] for x in stats], axis=0)
    rescale = jnp.exp(block_max - jnp.max(block_max, axis=0, keepdims=True))
    factors = rescale / jnp.sum(rescale * block_sum, axis=0, keepdims=True)
    factors = jnp.concatenate([factors, jnp.zeros((LANES - sources, LANES), F32)], axis=0).T
    context = jnp.zeros((rows, LANES), F32)
    for s in range(sources):
        context += both[s, :rows, :] * factors[:, s : s + 1]
    out_ref[...] = context.astype(BF16)


def project_kernel(layer_no, requests, own_ref, other_ref, weight_hbm, out_ref, weight, packed, sem):
    copy = pltpu.make_async_copy(weight_hbm.at[layer_no], weight, sem)
    copy.start()
    packed[...] = joined(own_ref[...].astype(F32), other_ref[...].astype(F32))
    rows = rows_of(packed, requests, weight.shape[0] // LANES)
    copy.wait()
    out_ref[...] = jnp.dot(rows, weight[...], preferred_element_type=F32)


def gate_up_kernel(
    layer_no,
    x_ref,
    own,
    part_a,
    part_b,
    part_c,
    gain_ref,
    gate_hbm,
    up_hbm,
    out_ref,
    keep_ref,
    send_ref,
    gate,
    up,
    packed,
    sems,
):
    gate_copy = pltpu.make_async_copy(gate_hbm.at[layer_no], gate, sems.at[0])
    up_copy = pltpu.make_async_copy(up_hbm.at[layer_no], up, sems.at[1])
    gate_copy.start()
    up_copy.start()
    requests = x_ref.shape[0]
    stride = packed.shape[0] // requests
    half = stride // 2
    blocks = gate.shape[1] // LANES
    total = x_ref[...].astype(F32) + ((own[...] + part_a[...]) + (part_b[...] + part_c[...]))
    out_ref[...] = total.astype(BF16)
    current = out_ref[...].astype(F32)
    scaled = (current * gain_ref[layer_no : layer_no + 1, :].astype(F32)).astype(BF16)
    zeros = jnp.zeros((requests, LANES), F32)
    packed[pl.ds(blocks, requests, stride=stride), :] = squares_in_lanes(current)
    for row in [*range(blocks + 1, half), *range(half + blocks, stride)]:
        packed[pl.ds(row, requests, stride=stride), :] = zeros
    gate_copy.wait()
    store_blocks(packed, jnp.dot(scaled, gate[...], preferred_element_type=F32), stride, 0)
    up_copy.wait()
    store_blocks(packed, jnp.dot(scaled, up[...], preferred_element_type=F32), stride, half)
    keep, send = halves(packed[...])
    keep_ref[...] = keep
    send_ref[...] = send.astype(BF16)


def activation_kernel(blocks, sources, received_ref, out_ref):
    half = out_ref.shape[0] // sources
    totals = jnp.sum(received_ref[...].astype(F32).reshape(sources, 2 * half, LANES), axis=0)
    squares = totals[blocks : blocks + 1, 0:1] + totals[blocks : blocks + 1, 1:2]
    inv = lax.rsqrt(squares / D + EPSILON)
    gate = totals[:half] * inv
    act = gate / (1.0 + jnp.exp(-gate)) * (totals[half:] * inv)
    repeat_into(out_ref, act.astype(BF16))


def exchange(array, n_req):
    shape = array.shape
    sides = [list(range(core, n_req, 2)) for core in range(2)]
    count = n_req // 2
    blocks = array.reshape((count, shape[0] // count) + shape[1:])
    return lax.all_to_all(
        blocks, "req", split_axis=0, concat_axis=0, tiled=True, axis_index_groups=sides
    ).reshape(shape)


def from_pair(array, n_req):
    return lax.ppermute(array, "req", [(i, i ^ 1) for i in range(n_req)])


def tp_parts(partial_sum):
    n_tp = lax.axis_size("tp")
    return [
        lax.ppermute(partial_sum, "tp", [(i, (i + shift) % n_tp) for i in range(n_tp)])
        for shift in (2, 1, 3)
    ]


def shards(
    hidden,
    attn_gain,
    q_weight,
    o_weight,
    ffn_gain,
    gate_weight,
    up_weight,
    down_weight,
    kv_pool,
    block_home,
    chosen,
    chosen_count,
):
    n_req = lax.axis_size("req")
    requests, width = hidden.shape
    pool_dev = kv_pool.shape[1]
    block_tokens, head_size = kv_pool.shape[4:]
    heads = q_weight.shape[2] // head_size
    hidden_units = gate_weight.shape[2]
    side = n_req // 2
    q_rows = requests * heads // 2
    sent_rows = q_rows + requests // 2
    f_rows = 32
    blocks = hidden_units // LANES
    position = float(block_home.shape[1] * block_tokens - 1)
    tables = rotary_tables(position, head_size)
    dma = pltpu.SemaphoreType.DMA

    def rows_type(rows, kind=BF16):
        return jax.ShapeDtypeStruct((rows, LANES), kind)

    def rows_scratch(rows):
        return pltpu.VMEM((rows, LANES), F32)

    current = hidden
    parts = None
    slots = None
    for layer_no in range(LAYERS):
        halves_type = [rows_type(sent_rows, F32), rows_type(sent_rows)]
        packed = rows_scratch(2 * q_rows)
        weight = pltpu.VMEM(q_weight.shape[1:], BF16)
        if parts is None:
            keep, send = call(
                functools.partial(first_query_kernel, pool_dev),
                halves_type,
                [HBM] * 6,
                [
                    pltpu.VMEM(hidden.shape, BF16),
                    pltpu.VMEM(attn_gain.shape, BF16),
                    weight,
                    pltpu.VMEM(block_home.shape, jnp.int32),
                    pltpu.VMEM((LAYERS, chosen.shape[3]), jnp.int32),
                    pltpu.VMEM((LAYERS, 1), jnp.int32),
                    packed,
                    dma((6,)),
                ],
                limit=62,
            )(
                current,
                attn_gain,
                q_weight,
                block_home,
                chosen.reshape(LAYERS, -1),
                chosen_count.reshape(LAYERS, 1),
            )
        else:
            current, keep, send = call(
                functools.partial(query_kernel, layer_no),
                [jax.ShapeDtypeStruct(current.shape, BF16)] + halves_type,
                [VMEM] * 6 + [HBM],
                [weight, packed, dma],
            )(current, *parts, attn_gain, q_weight)
        payload = call(pair_sum_kernel, rows_type(side * sent_rows), [VMEM] * 2)(
            keep, from_pair(send, n_req)
        )
        own = call(
            functools.partial(rotate_kernel, heads),
            rows_type(sent_rows if slots is None else q_rows),
            [VMEM] * 2,
            [rows_scratch(q_rows)],
        )(exchange(payload, n_req), tables)
        other = from_pair(own, n_req)
        if slots is None:
            slots = (own, other)
        keep, send = call(
            functools.partial(block_kernel, layer_no),
            [rows_type(2 * q_rows, F32), rows_type(2 * q_rows)],
            [VMEM] * 4 + [HBM],
            [
                pltpu.VMEM((pool_dev, 2, block_tokens, head_size), BF16),
                rows_scratch(2 * q_rows),
                dma,
            ],
        )(own, other, *slots, kv_pool)
        payload = call(merge_kernel, rows_type(side * sent_rows), [VMEM] * 2)(
            keep, from_pair(send, n_req)
        )
        context = call(functools.partial(combine_kernel, side), rows_type(q_rows), [VMEM])(
            exchange(payload, n_req)
        )
        own = call(
            functools.partial(project_kernel, layer_no, requests),
            jax.ShapeDtypeStruct((requests, width), F32),
            [VMEM, VMEM, HBM],
            [pltpu.VMEM(o_weight.shape[1:], BF16), rows_scratch(2 * q_rows), dma],
        )(context, from_pair(context, n_req), o_weight)
        attended, keep, send = call(
            functools.partial(gate_up_kernel, layer_no),
            [
                jax.ShapeDtypeStruct(current.shape, BF16),
                rows_type(requests * f_rows, F32),
                rows_type(requests * f_rows),
            ],
            [VMEM] * 6 + [HBM] * 2,
            [
                pltpu.VMEM(gate_weight.shape[1:], BF16),
                pltpu.VMEM(up_weight.shape[1:], BF16),
                rows_scratch(requests * 2 * f_rows),
                dma((2,)),
            ],
        )(current, own, *tp_parts(own), ffn_gain, gate_weight, up_weight)
        payload = call(pair_sum_kernel, rows_type(requests * f_rows), [VMEM] * 2)(
            keep, from_pair(send, n_req)
        )
        act = call(
            functools.partial(activation_kernel, blocks, side), rows_type(side * f_rows), [VMEM]
        )(exchange(payload, n_req))
        acts = exchange(act, n_req)
        own = call(
            functools.partial(project_kernel, layer_no, requests),
            jax.ShapeDtypeStruct((requests, width), F32),
            [VMEM, VMEM, HBM],
            [pltpu.VMEM(down_weight.shape[1:], BF16), rows_scratch(requests * f_rows), dma],
        )(acts, from_pair(acts, n_req), down_weight)
        current, parts = attended, [own] + tp_parts(own)
    total = (parts[0] + parts[1]) + (parts[2] + parts[3])
    return (current.astype(F32) + total).astype(BF16)


def solution(mesh):
    return jax.shard_map(
        shards,
        mesh=mesh,
        in_specs=(
            P(None, "req"),
            P(None, "req"),
            P(None, "req", "tp"),
            P(None, "tp", "req"),
            P(None, "req"),
            P(None, "req", "tp"),
            P(None, "req", "tp"),
            P(None, "tp", "req"),
            P(None, "req", "tp", None, None, None),
            P("req", None),
            P(None, "req", "tp", None),
            P(None, "req", "tp"),
        ),
        out_specs=P(None, "req"),
        check_vma=False,
    )
```

time: 209 us -> 185 us (0.89)
  blocking collectives: 126 us -> 113 us
  starting transfers between devices: 28.2 us -> 21.7 us
  local copies, waits for them, and re-layouts: 10.4 us -> 5.1 us
    ppermute x0 -> x12, waiting for transfers between devices: none -> 15.3 us  [from_pair(): return lax.ppermute(array, 'req', [(i, i ^ 1) for i in range(n_req)])]
    all_to_all x2 -> x0, waiting for transfers between devices: 14.5 us -> none  [exchange(): lax.all_to_all(blocks, 'req', split_axis=0, concat_axis=0, tiled=True)]
    all_to_all x10 -> x8, blocking collectives: 126 us -> 113 us  [exchange(): lax.all_to_all(blocks, 'req', split_axis=0, concat_axis=0, tiled=True, ax...]
    all_to_all x2 -> x0, starting transfers between devices: 7.69 us -> none  [exchange(): lax.all_to_all(blocks, 'req', split_axis=0, concat_axis=0, tiled=True)]
    unnamed x43 -> x26, local copies, waits for them, and re-layouts: 10.4 us -> 3.8 us
    pallas_call x9 -> x15, Pallas kernels: 7.09 us -> 7.89 us  [the longest x2 3.15 us: shards(): call(functools.partial(block_kernel, layer_no), [rows_type(2 * q_rows, F3...]
  transfers between devices with their start and end apart: 14 -> 24, of which waited for: 8 -> 19; matrix products, arithmetic and copies ran while one was open for 0% -> 0% of each run, Pallas kernels for 0% -> 0%
where the time goes in v4:
time: 185 us
  blocking collectives  113 us (61%)
  waiting for transfers between devices  30.7 us (17%)
  starting transfers between devices  21.7 us (12%)
  Pallas kernels  13.6 us (7%)
  local copies, waits for them, and re-layouts  5.1 us (3%)
    all_to_all x8, blocking collectives, exchange(): lax.all_to_all(blocks, 'req', split_axis=0, concat_axis=0, tiled=True, ax...  113 us
    ppermute x12, starting transfers between devices, tp_parts(): lax.ppermute(partial_sum, 'tp', [(i, (i + shift) % n_tp) for i in range(n...  20.3 us
    ppermute x12, waiting for transfers between devices, tp_parts(): lax.ppermute(partial_sum, 'tp', [(i, (i + shift) % n_tp) for i in range(n...  15.4 us
    ppermute x12, waiting for transfers between devices, from_pair(): return lax.ppermute(array, 'req', [(i, i ^ 1) for i in range(n_req)])  15.3 us
    unnamed x26, local copies, waits for them, and re-layouts  3.8 us
  transfers between devices with their start and end apart: 24, of which 19 were waited for; matrix products, arithmetic and copies ran while one was open for 0% of the time, Pallas kernels for 0%

profile of v4, /device:TPU:0, one launch (start us, length us, event | category | flops | bytes accessed | tf_op | source)
XLA Modules:
  0.0 184.8 jit_solution(11161722351111395816)
XLA Ops:
  1.3 2.0 %shard_map.127 = (f32[144,128]{1,0:T(8,128)}, bf16[144,128]{1,0:T(8,128)(2,1)}) custom-call(bf16[32,256]{1,0:T(8,128)(2,1)} %x_ref.1, bf16[2,256]{1,0:T(2,128)(2,1)} %gain_ref.4, bf16[2,256,1024]{2,1,0:T(8,128)(2,1)} %weight_hbm.9, s32[1,32]{1,0:T(1,128)} %homes_hbm.1, s32[2,24]{1,0:T(2,128)} %bitcast.36, s32[2,1]{1,0:T(2,128)} %copy.14.count_hbm), custom_call_target="tpu_custom_call" | custom-call | tf_op jit(solution)/shard_map/pallas_call | solution.py:446
  5.8 19.6 %all_to_all.40 = bf16[16,144,128]{2,1,0:T(8,128)(2,1)S(1)} all-to-all(bf16[16,144,128]{2,1,0:T(8,128)(2,1)S(1)} %bitcast.18), channel_id=1, replica_groups={{0,8,16,24,32,40,48,56,64,72,80,88,96,104,112,120},{4,12,20,28,36,44,52..., dimensions={0} | all-to-all | bytes 1179648 | tf_op jit(solution)/shard_map/all_to_all | solution.py:386
  27.7 2.2 %copy-done = bf16[2,32,1,2,128,128]{5,4,3,2,1,0:T(8,128)(2,1)S(1)} copy-done((bf16[2,32,1,2,128,128]{5,4,3,2,1,0:T(8,128)(2,1)S(1)}, bf16[2,32,1,2,128,128]{5,4,3,2,1,0:T(8,128)(2,1)}, u32[]{:S(2)}) %copy-start) | copy-done | bytes 4194328
  29.9 1.6 shard_map.130
  33.1 15.7 %all_to_all.41 = bf16[16,144,128]{2,1,0:T(8,128)(2,1)S(1)} all-to-all(bf16[16,144,128]{2,1,0:T(8,128)(2,1)S(1)} %bitcast.19), channel_id=1, replica_groups={{0,8,16,24,32,40,48,56,64,72,80,88,96,104,112,120},{4,12,20,28,36,44,52..., dimensions={0} | all-to-all | bytes 1179648 | tf_op jit(solution)/shard_map/all_to_all | solution.py:386
  51.0 4.1 %collective-permute-start.6 = (f32[32,256]{1,0:T(8,128)S(1)}, f32[32,256]{1,0:T(8,128)S(1)}, u32[]{:S(2)}, u32[]{:S(2)}) collective-permute-start(f32[32,256]{1,0:T(8,128)S(1)} %shard_map.133.own), channel_id=1, source_target_pairs={{0,3},{1,0},{2,1},{3,2},{4,7},{5,4},{6,5},{7,6},{8,11},{9,8},{10,9... | collective-permute-start | bytes 98312 | tf_op jit(solution)/shard_map/ppermute | solution.py:398
  55.1 1.9 %collective-permute-start.4 = (f32[32,256]{1,0:T(8,128)S(1)}, f32[32,256]{1,0:T(8,128)S(1)}, u32[]{:S(2)}, u32[]{:S(2)}) collective-permute-start(f32[32,256]{1,0:T(8,128)S(1)} %shard_map.133.own), channel_id=1, source_target_pairs={{0,2},{1,3},{2,0},{3,1},{4,6},{5,7},{6,4},{7,5},{8,10},{9,11},{10,... | collective-permute-start | bytes 98312 | tf_op jit(solution)/shard_map/ppermute | solution.py:398
  56.9 3.6 %collective-permute-done.5.part_b = f32[32,256]{1,0:T(8,128)S(1)} collective-permute-done((f32[32,256]{1,0:T(8,128)S(1)}, f32[32,256]{1,0:T(8,128)S(1)}, u32[]{:S(2)}, u32[]{:S(2)}) %collective-permute-start.5) | collective-permute-done | bytes 32800 | tf_op jit(solution)/shard_map/ppermute | solution.py:398
  60.6 1.6 shard_map.134
  63.9 12.1 %all_to_all.42 = bf16[16,64,128]{2,1,0:T(8,128)(2,1)S(1)} all-to-all(bf16[16,64,128]{2,1,0:T(8,128)(2,1)S(1)} %bitcast.28), channel_id=1, replica_groups={{0,8,16,24,32,40,48,56,64,72,80,88,96,104,112,120},{4,12,20,28,36,44,52..., dimensions={0} | all-to-all | bytes 524288 | tf_op jit(solution)/shard_map/all_to_all | solution.py:386
  76.1 10.9 %all_to_all.43 = bf16[16,32,128]{2,1,0:T(8,128)(2,1)S(1)} all-to-all(bf16[16,32,128]{2,1,0:T(8,128)(2,1)S(1)} %bitcast.34), channel_id=1, replica_groups={{0,8,16,24,32,40,48,56,64,72,80,88,96,104,112,120},{4,12,20,28,36,44,52..., dimensions={0} | all-to-all | bytes 262144 | tf_op jit(solution)/shard_map/all_to_all | solution.py:386
  89.3 3.2 %collective-permute-start.11 = (f32[32,256]{1,0:T(8,128)S(1)}, f32[32,256]{1,0:T(8,128)S(1)}, u32[]{:S(2)}, u32[]{:S(2)}) collective-permute-start(f32[32,256]{1,0:T(8,128)S(1)} %shard_map.137.own), channel_id=1, source_target_pairs={{0,3},{1,0},{2,1},{3,2},{4,7},{5,4},{6,5},{7,6},{8,11},{9,8},{10,9... | collective-permute-start | bytes 98312 | tf_op jit(solution)/shard_map/ppermute | solution.py:398
  92.5 1.5 collective-permute-start.9
  94.1 3.9 %collective-permute-done.10.part_b = f32[32,256]{1,0:T(8,128)S(1)} collective-permute-done((f32[32,256]{1,0:T(8,128)S(1)}, f32[32,256]{1,0:T(8,128)S(1)}, u32[]{:S(2)}, u32[]{:S(2)}) %collective-permute-start.10) | collective-permute-done | bytes 32800 | tf_op jit(solution)/shard_map/ppermute | solution.py:398
  99.6 15.7 %all_to_all.44 = bf16[16,144,128]{2,1,0:T(8,128)(2,1)S(1)} all-to-all(bf16[16,144,128]{2,1,0:T(8,128)(2,1)S(1)} %bitcast.20), channel_id=1, replica_groups={{0,8,16,24,32,40,48,56,64,72,80,88,96,104,112,120},{4,12,20,28,36,44,52..., dimensions={0} | all-to-all | bytes 1179648 | tf_op jit(solution)/shard_map/all_to_all | solution.py:386
  116.8 1.6 shard_map.141
  120.1 15.7 %all_to_all.45 = bf16[16,144,128]{2,1,0:T(8,128)(2,1)S(1)} all-to-all(bf16[16,144,128]{2,1,0:T(8,128)(2,1)S(1)} %bitcast.22), channel_id=1, replica_groups={{0,8,16,24,32,40,48,56,64,72,80,88,96,104,112,120},{4,12,20,28,36,44,52..., dimensions={0} | all-to-all | bytes 1179648 | tf_op jit(solution)/shard_map/all_to_all | solution.py:386
  138.1 3.2 %collective-permute-start.18 = (f32[32,256]{1,0:T(8,128)S(1)}, f32[32,256]{1,0:T(8,128)S(1)}, u32[]{:S(2)}, u32[]{:S(2)}) collective-permute-start(f32[32,256]{1,0:T(8,128)S(1)} %shard_map.144.own), channel_id=1, source_target_pairs={{0,3},{1,0},{2,1},{3,2},{4,7},{5,4},{6,5},{7,6},{8,11},{9,8},{10,9... | collective-permute-start | bytes 98312 | tf_op jit(solution)/shard_map/ppermute | solution.py:398
  142.9 3.9 %collective-permute-done.17.part_b = f32[32,256]{1,0:T(8,128)S(1)} collective-permute-done((f32[32,256]{1,0:T(8,128)S(1)}, f32[32,256]{1,0:T(8,128)S(1)}, u32[]{:S(2)}, u32[]{:S(2)}) %collective-permute-start.17) | collective-permute-done | bytes 32800 | tf_op jit(solution)/shard_map/ppermute | solution.py:398
  146.8 1.6 shard_map.145
  150.1 12.1 %all_to_all.46 = bf16[16,64,128]{2,1,0:T(8,128)(2,1)S(1)} all-to-all(bf16[16,64,128]{2,1,0:T(8,128)(2,1)S(1)} %bitcast.29), channel_id=1, replica_groups={{0,8,16,24,32,40,48,56,64,72,80,88,96,104,112,120},{4,12,20,28,36,44,52..., dimensions={0} | all-to-all | bytes 524288 | tf_op jit(solution)/shard_map/all_to_all | solution.py:386
  162.4 10.9 %all_to_all.47 = bf16[16,32,128]{2,1,0:T(8,128)(2,1)S(1)} all-to-all(bf16[16,32,128]{2,1,0:T(8,128)(2,1)S(1)} %bitcast.35), channel_id=1, replica_groups={{0,8,16,24,32,40,48,56,64,72,80,88,96,104,112,120},{4,12,20,28,36,44,52..., dimensions={0} | all-to-all | bytes 262144 | tf_op jit(solution)/shard_map/all_to_all | solution.py:386
  175.5 3.2 %collective-permute-start.23 = (f32[32,256]{1,0:T(8,128)S(1)}, f32[32,256]{1,0:T(8,128)S(1)}, u32[]{:S(2)}, u32[]{:S(2)}) collective-permute-start(f32[32,256]{1,0:T(8,128)S(1)} %shard_map.148), channel_id=1, source_target_pairs={{0,3},{1,0},{2,1},{3,2},{4,7},{5,4},{6,5},{7,6},{8,11},{9,8},{10,9... | collective-permute-start | bytes 98312 | tf_op jit(solution)/shard_map/ppermute | solution.py:398
  180.3 3.9 %collective-permute-done.22 = f32[32,256]{1,0:T(8,128)S(1)} collective-permute-done((f32[32,256]{1,0:T(8,128)S(1)}, f32[32,256]{1,0:T(8,128)S(1)}, u32[]{:S(2)}, u32[]{:S(2)}) %collective-permute-start.22) | collective-permute-done | bytes 32800 | tf_op jit(solution)/shard_map/ppermute | solution.py:398
  (82 shorter events, 28.8 us)
Async XLA Ops:
  3.3 1.5 collective-permute-start
  26.4 1.3 collective-permute-start.1
  31.4 1.3 collective-permute-start.2
  49.4 1.3 collective-permute-start.3
  51.0 6.0 %collective-permute-start.6 = (f32[32,256]{1,0:T(8,128)S(1)}, f32[32,256]{1,0:T(8,128)S(1)}, u32[]{:S(2)}, u32[]{:S(2)}) collective-permute-start(f32[32,256]{1,0:T(8,128)S(1)} %shard_map.133.own), channel_id=1, source_target_pairs={{0,3},{1,0},{2,1},{3,2},{4,7},{5,4},{6,5},{7,6},{8,11},{9,8},{10,9... | collective-permute-start | bytes 98312 | tf_op jit(solution)/shard_map/ppermute | solution.py:398
  55.1 5.5 %collective-permute-start.5 = (f32[32,256]{1,0:T(8,128)S(1)}, f32[32,256]{1,0:T(8,128)S(1)}, u32[]{:S(2)}, u32[]{:S(2)}) collective-permute-start(f32[32,256]{1,0:T(8,128)S(1)} %shard_map.133.own), channel_id=1, source_target_pairs={{0,1},{1,2},{2,3},{3,0},{4,5},{5,6},{6,7},{7,4},{8,9},{9,10},{10,1... | collective-permute-start | bytes 98312 | tf_op jit(solution)/shard_map/ppermute | solution.py:398
  55.1 5.5 %collective-permute-start.4 = (f32[32,256]{1,0:T(8,128)S(1)}, f32[32,256]{1,0:T(8,128)S(1)}, u32[]{:S(2)}, u32[]{:S(2)}) collective-permute-start(f32[32,256]{1,0:T(8,128)S(1)} %shard_map.133.own), channel_id=1, source_target_pairs={{0,2},{1,3},{2,0},{3,1},{4,6},{5,7},{6,4},{7,5},{8,10},{9,11},{10,... | collective-permute-start | bytes 98312 | tf_op jit(solution)/shard_map/ppermute | solution.py:398
  62.2 1.6 collective-permute-start.7
  87.0 1.3 collective-permute-start.8
  89.3 4.8 %collective-permute-start.11 = (f32[32,256]{1,0:T(8,128)S(1)}, f32[32,256]{1,0:T(8,128)S(1)}, u32[]{:S(2)}, u32[]{:S(2)}) collective-permute-start(f32[32,256]{1,0:T(8,128)S(1)} %shard_map.137.own), channel_id=1, source_target_pairs={{0,3},{1,0},{2,1},{3,2},{4,7},{5,4},{6,5},{7,6},{8,11},{9,8},{10,9... | collective-permute-start | bytes 98312 | tf_op jit(solution)/shard_map/ppermute | solution.py:398
  92.5 5.5 %collective-permute-start.10 = (f32[32,256]{1,0:T(8,128)S(1)}, f32[32,256]{1,0:T(8,128)S(1)}, u32[]{:S(2)}, u32[]{:S(2)}) collective-permute-start(f32[32,256]{1,0:T(8,128)S(1)} %shard_map.137.own), channel_id=1, source_target_pairs={{0,1},{1,2},{2,3},{3,0},{4,5},{5,6},{6,7},{7,4},{8,9},{9,10},{10,1... | collective-permute-start | bytes 98312 | tf_op jit(solution)/shard_map/ppermute | solution.py:398
  92.5 5.5 %collective-permute-start.9 = (f32[32,256]{1,0:T(8,128)S(1)}, f32[32,256]{1,0:T(8,128)S(1)}, u32[]{:S(2)}, u32[]{:S(2)}) collective-permute-start(f32[32,256]{1,0:T(8,128)S(1)} %shard_map.137.own), channel_id=1, source_target_pairs={{0,2},{1,3},{2,0},{3,1},{4,6},{5,7},{6,4},{7,5},{8,10},{9,11},{10,... | collective-permute-start | bytes 98312 | tf_op jit(solution)/shard_map/ppermute | solution.py:398
  98.3 1.3 collective-permute-start.12
  115.5 1.3 collective-permute-start.13
  118.4 1.3 collective-permute-start.14
  136.3 1.5 collective-permute-start.15
  138.1 4.8 %collective-permute-start.18 = (f32[32,256]{1,0:T(8,128)S(1)}, f32[32,256]{1,0:T(8,128)S(1)}, u32[]{:S(2)}, u32[]{:S(2)}) collective-permute-start(f32[32,256]{1,0:T(8,128)S(1)} %shard_map.144.own), channel_id=1, source_target_pairs={{0,3},{1,0},{2,1},{3,2},{4,7},{5,4},{6,5},{7,6},{8,11},{9,8},{10,9... | collective-permute-start | bytes 98312 | tf_op jit(solution)/shard_map/ppermute | solution.py:398
  141.3 5.5 %collective-permute-start.17 = (f32[32,256]{1,0:T(8,128)S(1)}, f32[32,256]{1,0:T(8,128)S(1)}, u32[]{:S(2)}, u32[]{:S(2)}) collective-permute-start(f32[32,256]{1,0:T(8,128)S(1)} %shard_map.144.own), channel_id=1, source_target_pairs={{0,1},{1,2},{2,3},{3,0},{4,5},{5,6},{6,7},{7,4},{8,9},{9,10},{10,1... | collective-permute-start | bytes 98312 | tf_op jit(solution)/shard_map/ppermute | solution.py:398
  141.3 5.5 %collective-permute-start.16 = (f32[32,256]{1,0:T(8,128)S(1)}, f32[32,256]{1,0:T(8,128)S(1)}, u32[]{:S(2)}, u32[]{:S(2)}) collective-permute-start(f32[32,256]{1,0:T(8,128)S(1)} %shard_map.144.own), channel_id=1, source_target_pairs={{0,2},{1,3},{2,0},{3,1},{4,6},{5,7},{6,4},{7,5},{8,10},{9,11},{10,... | collective-permute-start | bytes 98312 | tf_op jit(solution)/shard_map/ppermute | solution.py:398
  148.4 1.6 collective-permute-start.19
  173.2 1.3 collective-permute-start.20
  175.5 4.8 %collective-permute-start.23 = (f32[32,256]{1,0:T(8,128)S(1)}, f32[32,256]{1,0:T(8,128)S(1)}, u32[]{:S(2)}, u32[]{:S(2)}) collective-permute-start(f32[32,256]{1,0:T(8,128)S(1)} %shard_map.148), channel_id=1, source_target_pairs={{0,3},{1,0},{2,1},{3,2},{4,7},{5,4},{6,5},{7,6},{8,11},{9,8},{10,9... | collective-permute-start | bytes 98312 | tf_op jit(solution)/shard_map/ppermute | solution.py:398
  178.7 5.5 %collective-permute-start.22 = (f32[32,256]{1,0:T(8,128)S(1)}, f32[32,256]{1,0:T(8,128)S(1)}, u32[]{:S(2)}, u32[]{:S(2)}) collective-permute-start(f32[32,256]{1,0:T(8,128)S(1)} %shard_map.148), channel_id=1, source_target_pairs={{0,1},{1,2},{2,3},{3,0},{4,5},{5,6},{6,7},{7,4},{8,9},{9,10},{10,1... | collective-permute-start | bytes 98312 | tf_op jit(solution)/shard_map/ppermute | solution.py:398
  178.7 5.5 %collective-permute-start.21 = (f32[32,256]{1,0:T(8,128)S(1)}, f32[32,256]{1,0:T(8,128)S(1)}, u32[]{:S(2)}, u32[]{:S(2)}) collective-permute-start(f32[32,256]{1,0:T(8,128)S(1)} %shard_map.148), channel_id=1, source_target_pairs={{0,2},{1,3},{2,0},{3,1},{4,6},{5,7},{6,4},{7,5},{8,10},{9,11},{10,... | collective-permute-start | bytes 98312 | tf_op jit(solution)/shard_map/ppermute | solution.py:398
  (13 other events, 357.0 us)

commit v5 on v4

v5 whole, which is shorter than its diff:
```python
import functools
import math

import jax
import jax.numpy as jnp
import numpy as np
from jax import lax
from jax.experimental import pallas as pl
from jax.experimental.pallas import tpu as pltpu
from jax.sharding import PartitionSpec as P

D = 8192
LAYERS = 2
LANES = 128

MASK_FILL = -1e30
EPSILON = 1e-05

VMEM = pl.BlockSpec(memory_space=pltpu.VMEM)
SMEM = pl.BlockSpec(memory_space=pltpu.SMEM)
HBM = pl.BlockSpec(memory_space=pltpu.HBM)
F32 = jnp.float32
BF16 = jnp.bfloat16


def rotary_tables(position, head_size):
    freq_idx = np.arange(head_size // 2)
    angles = position * np.exp(freq_idx * (-2.0 * math.log(500000.0) / head_size))
    cosine, sine_part = np.cos(angles), np.sin(angles)
    scale = head_size**-0.5
    tables = np.stack([np.concatenate([cosine, cosine]), np.concatenate([-sine_part, sine_part])])
    return jnp.asarray(tables * scale, F32)


def call(kernel, out_shape, in_specs, scratch=(), limit=16, out_specs=None, flops=0, nbytes=0):
    return pl.pallas_call(
        kernel,
        out_shape=out_shape,
        in_specs=in_specs,
        out_specs=out_specs if out_specs is not None else jax.tree.map(lambda _: VMEM, out_shape),
        scratch_shapes=list(scratch),
        compiler_params=pltpu.CompilerParams(vmem_limit_bytes=limit * 1024 * 1024),
        cost_estimate=pl.CostEstimate(flops=flops, bytes_accessed=nbytes, transcendentals=0),
    )


def core_side():
    return lax.rem(lax.axis_index("req"), 2)


def joined(own, other, axis):
    first = core_side() == 0
    return jnp.concatenate([jnp.where(first, own, other), jnp.where(first, other, own)], axis=axis)


def pair_copies(own_hbm, other_hbm, own_target, other_target, sems):
    return [
        pltpu.make_async_copy(own_hbm, own_target, sems.at[0]),
        pltpu.make_async_copy(other_hbm, other_target, sems.at[1]),
    ]


def side_slices(size):
    side = core_side()
    return (
        pl.ds(pl.multiple_of(side * size, LANES), size),
        pl.ds(pl.multiple_of((1 - side) * size, LANES), size),
    )


def column_copies(layer_no, own_hbm, other_hbm, weight, sems):
    own, other = side_slices(own_hbm.shape[2])
    return pair_copies(
        own_hbm.at[layer_no], other_hbm.at[layer_no], weight.at[:, own], weight.at[:, other], sems
    )


def row_copies(layer_no, own_hbm, other_hbm, weight, sems):
    half, _ = side_slices(weight.shape[1])
    own, other = side_slices(own_hbm.shape[1])
    return pair_copies(
        own_hbm.at[layer_no, :, half],
        other_hbm.at[layer_no, :, half],
        weight.at[own],
        weight.at[other],
        sems,
    )


def start_all(copies):
    for copy in copies:
        copy.start()


def wait_all(copies):
    for copy in copies:
        copy.wait()


def squares_in_lanes(current):
    squares = jnp.sum(current * current, axis=1, keepdims=True)
    high = squares.astype(BF16).astype(F32)
    lane = lax.broadcasted_iota(jnp.int32, (current.shape[0], LANES), 1)
    return jnp.where(lane == 0, high, jnp.where(lane == 1, squares - high, 0.0))


def store_blocks(packed, product):
    requests, width = product.shape
    blocks = width // LANES
    for k in range(blocks):
        packed[pl.ds(k, requests, stride=blocks), :] = product[:, k * LANES : (k + 1) * LANES]
    return packed[...]


def spread(packed, values, stride):
    for k in range(stride):
        packed[pl.ds(k, values.shape[0], stride=stride), :] = values
    return packed[...]


def rows_of(packed, requests, blocks):
    return jnp.concatenate(
        [packed[pl.ds(k, requests, stride=blocks), :] for k in range(blocks)], axis=1
    )


def repeat_into(out_ref, values):
    rows = values.shape[0]
    for i in range(out_ref.shape[0] // rows):
        out_ref[i * rows : (i + 1) * rows, :] = values


def pair_sum(current, parts):
    a, b, c, d = [part[...].astype(F32) for part in parts]
    return (current[...].astype(F32) + ((a + b) + (c + d))).astype(BF16)


def slot_table(homes, chosen, counts, pool_dev, requests):
    n_blocks = homes.shape[1]
    shape = (n_blocks, n_blocks)
    row = lax.broadcasted_iota(jnp.int32, shape, 0)
    col = lax.broadcasted_iota(jnp.int32, shape, 1)
    places = jnp.broadcast_to(homes, shape)
    here = lax.div(places, pool_dev) == row

    def across(column):
        return jnp.sum(jnp.where(row == col, column, 0.0), axis=0, keepdims=True)

    slots = jnp.sum(jnp.where(here, lax.rem(places, pool_dev), 0).astype(F32), axis=1, keepdims=True)
    found = [jnp.zeros((1, n_blocks), F32), across(slots)]
    for layer_no in range(LAYERS):
        listed = chosen[layer_no]
        entry = lax.broadcasted_iota(jnp.int32, (n_blocks, listed.shape[1]), 1)
        block = lax.broadcasted_iota(jnp.int32, (n_blocks, listed.shape[1]), 0)
        hit = (listed == block) & (entry < counts[layer_no])
        taken = across(jnp.max(jnp.where(hit, 1.0, 0.0), axis=1, keepdims=True))
        found.append(across(jnp.max(jnp.where(here, taken, 0.0), axis=1, keepdims=True)))
    line = jnp.concatenate(found, axis=1)
    mine = lax.broadcasted_iota(jnp.int32, (requests, LANES), 0) == lax.axis_index("req")
    return jnp.where(mine, line, 0.0)


def first_query_kernel(
    pool_dev,
    x_hbm,
    gain_hbm,
    weight_hbm,
    homes_hbm,
    chosen_hbm,
    count_hbm,
    keep_ref,
    send_ref,
    x,
    gain,
    weight,
    homes,
    chosen,
    counts,
    packed,
    sems,
):
    copies = [
        pltpu.make_async_copy(source, target, sems.at[i])
        for i, (source, target) in enumerate(
            [
                (homes_hbm, homes),
                (chosen_hbm, chosen),
                (count_hbm, counts),
                (x_hbm, x),
                (gain_hbm, gain),
                (weight_hbm.at[0], weight),
            ]
        )
    ]
    start_all(copies)
    wait_all(copies[:3])
    lists = [chosen[i : i + 1, :] for i in range(LAYERS)]
    limits = [counts[i : i + 1, :] for i in range(LAYERS)]
    table = slot_table(homes[...], lists, limits, pool_dev, x.shape[0])
    wait_all(copies[3:])
    current = x[...].astype(F32)
    scaled = (current * gain[0:1, :].astype(F32)).astype(BF16)
    product = jnp.dot(scaled, weight[...], preferred_element_type=F32)
    middle = product.shape[1] // 2
    first = core_side() == 0
    rows = packed.shape[0]
    keep_ref[:rows, :] = store_blocks(packed, jnp.where(first, product[:, :middle], product[:, middle:]))
    send = store_blocks(packed, jnp.where(first, product[:, middle:], product[:, :middle]))
    send_ref[:rows, :] = send.astype(BF16)
    extra = squares_in_lanes(current) + table
    keep_ref[rows:, :] = extra
    send_ref[rows:, :] = extra.astype(BF16)


def pair_total_kernel(keep_ref, received_ref, out_ref):
    repeat_into(out_ref, (keep_ref[...] + received_ref[...].astype(F32)).astype(BF16))


def pair_state_kernel(x, x_other, gain, gain_other, ffn, ffn_other, x_out, gain_out, ffn_out):
    for own, other, out in ((x, x_other, x_out), (gain, gain_other, gain_out), (ffn, ffn_other, ffn_out)):
        out[...] = joined(own[...].astype(F32), other[...].astype(F32), 1).astype(BF16)


def query_kernel(
    layer_no, x_ref, a, b, c, d, gain_ref, own_hbm, other_hbm, out_ref, payload_ref, weight, packed, sems
):
    copies = row_copies(layer_no, own_hbm, other_hbm, weight, sems)
    start_all(copies)
    out_ref[...] = pair_sum(x_ref, (a, b, c, d))
    current = out_ref[...].astype(F32)
    scaled = (current * gain_ref[layer_no : layer_no + 1, :].astype(F32)).astype(BF16)
    extra = squares_in_lanes(current)
    wait_all(copies)
    product = jnp.dot(scaled, weight[...], preferred_element_type=F32)
    rows = jnp.concatenate([store_blocks(packed, product), extra], axis=0)
    repeat_into(payload_ref, rows.astype(BF16))


def in_parts(values, count):
    parts = []
    for _ in range(count):
        part = values.astype(BF16).astype(F32)
        parts.append(part)
        values = values - part
    return parts


def stats_in_lanes(block_max, block_sum):
    shape = (block_max.shape[0], LANES)
    lane = lax.broadcasted_iota(jnp.int32, shape, 1)
    stats = jnp.zeros(shape, F32)
    for place, part in enumerate(in_parts(block_max, 3) + in_parts(block_sum, 2)):
        stats = jnp.where(lane == place, part, stats)
    return stats


def block_kernel(
    layer_no, sources, received_ref, table_ref, tables_ref, own_hbm, other_hbm, out_ref, table_out, blocks, packed, sems
):
    copies = pair_copies(
        own_hbm.at[layer_no, :, 0], other_hbm.at[layer_no, :, 0], blocks.at[0], blocks.at[1], sems
    )
    start_all(copies)
    rows = packed.shape[0]
    n_slots = blocks.shape[1]
    totals = jnp.sum(received_ref[...].astype(F32).reshape(sources, -1, LANES), axis=0)
    extra = totals[rows:]
    requests = extra.shape[0]
    heads = rows // requests
    inv = lax.rsqrt((extra[:, 0:1] + extra[:, 1:2]) / D + EPSILON)
    queries = totals[:rows] * spread(packed, jnp.broadcast_to(inv, extra.shape), heads)
    queries = queries * tables_ref[0:1, :] + pltpu.roll(queries, LANES // 2, 1) * tables_ref[1:2, :]
    queries = queries.astype(BF16)

    table = extra if table_ref is None else table_ref[...]
    if table_out is not None:
        table_out[...] = extra
    me = lax.axis_index("req")
    lane = lax.broadcasted_iota(jnp.int32, table.shape, 1)
    request = lax.broadcasted_iota(jnp.int32, (requests, rows), 0)
    column = lax.broadcasted_iota(jnp.int32, (requests, rows), 1)
    row = lax.broadcasted_iota(jnp.int32, (2 * n_slots * heads, rows), 0)
    head = lax.rem(column, heads).astype(F32)
    places, used = [], []
    for b in range(2):
        store = me if b == 0 else me + 1 - 2 * core_side()
        slots = jnp.sum(jnp.where(lane == n_slots + store, table, 0.0), axis=1, keepdims=True)
        taken = jnp.where(lane == (2 + layer_no) * n_slots + store, table, 0.0)
        taken = jnp.broadcast_to(jnp.sum(taken, axis=1, keepdims=True), table.shape)
        used.append(spread(packed, taken, heads))
        target = jnp.where(
            lax.div(column, heads) == request, slots * (2 * heads) + (head + b * heads), 0.0
        )
        target = jnp.sum(target, axis=0, keepdims=True).astype(jnp.int32)
        places.append(jnp.where(row == target, 1.0, 0.0))
    by_slot = jnp.concatenate(places, axis=1)
    queries = jnp.dot(
        by_slot.astype(BF16), jnp.concatenate([queries, queries], axis=0), preferred_element_type=F32
    )
    group = 2 * heads
    mine = lax.broadcasted_iota(jnp.int32, (group, LANES), 0) < heads
    wait_all(copies)

    def of_slot(left, p, part, contract):
        left = left[p * group : (p + 1) * group].astype(BF16)
        sides = [
            lax.dot_general(
                left, blocks[b, p, part], (((1,), (contract,)), ((), ())), preferred_element_type=F32
            )
            for b in range(2)
        ]
        return jnp.where(mine, sides[0], sides[1])

    scores = jnp.concatenate([of_slot(queries, p, 0, 1) for p in range(n_slots)], axis=0)
    block_max = jnp.max(scores, axis=1, keepdims=True)
    terms = jnp.exp(scores - block_max)
    block_sum = jnp.sum(terms, axis=1, keepdims=True)
    acc = jnp.concatenate([of_slot(terms, p, 1, 0) for p in range(n_slots)], axis=0)
    both = jnp.concatenate([acc, stats_in_lanes(block_max, block_sum)], axis=1).astype(BF16)
    both = jnp.dot(by_slot.T.astype(BF16), both, preferred_element_type=F32)
    sides = []
    for b in range(2):
        side = both[b * rows : (b + 1) * rows]
        stats = side[:, LANES:]
        block_max = stats[:, 0:1] + stats[:, 1:2] + stats[:, 2:3]
        block_max = jnp.where(used[b][:, 0:1] > 0.0, block_max, MASK_FILL)
        sides.append((block_max, stats[:, 3:4] + stats[:, 4:5], side[:, :LANES]))
    top = jnp.maximum(sides[0][0], sides[1][0])
    rescale = [jnp.exp(side[0] - top) for side in sides]
    total = rescale[0] * sides[0][1] + rescale[1] * sides[1][1]
    acc = rescale[0] * sides[0][2] + rescale[1] * sides[1][2]
    stats = stats_in_lanes(top, total).T
    extra = out_ref.shape[0] // sources - rows
    repeat_into(out_ref, jnp.concatenate([acc, stats[:extra]], axis=0).astype(BF16))


def first_block_kernel(sources, received_ref, tables_ref, own_hbm, other_hbm, out_ref, table_out, *scratch):
    block_kernel(
        0, sources, received_ref, None, tables_ref, own_hbm, other_hbm, out_ref, table_out, *scratch
    )


def later_block_kernel(
    layer_no, sources, received_ref, table_ref, tables_ref, own_hbm, other_hbm, out_ref, *scratch
):
    block_kernel(
        layer_no, sources, received_ref, table_ref, tables_ref, own_hbm, other_hbm, out_ref, None, *scratch
    )


def combine_kernel(sources, received_ref, out_ref):
    rows = out_ref.shape[0]
    both = received_ref[...].astype(F32).reshape(sources, -1, LANES)
    stats = [both[s, rows : rows + 8, :] for s in range(sources)]
    block_max = jnp.concatenate([x[0:1] + x[1:2] + x[2:3] for x in stats], axis=0)
    block_sum = jnp.concatenate([x[3:4] + x[4:5] for x in stats], axis=0)
    rescale = jnp.exp(block_max - jnp.max(block_max, axis=0, keepdims=True))
    factors = rescale / jnp.sum(rescale * block_sum, axis=0, keepdims=True)
    factors = jnp.concatenate([factors, jnp.zeros((LANES - sources, LANES), F32)], axis=0).T
    context = jnp.zeros((rows, LANES), F32)
    for s in range(sources):
        context += both[s, :rows, :] * factors[:, s : s + 1]
    out_ref[...] = context.astype(BF16)


def context_kernel(
    layer_no, requests, own_ref, other_ref, own_hbm, other_hbm, out_ref, weight, packed, sems
):
    copies = column_copies(layer_no, own_hbm, other_hbm, weight, sems)
    start_all(copies)
    sides = []
    for ref in (own_ref, other_ref):
        packed[...] = ref[...].astype(F32)
        sides.append(rows_of(packed, requests, packed.shape[0] // requests))
    rows = joined(sides[0], sides[1], 1).astype(BF16)
    wait_all(copies)
    out_ref[...] = jnp.dot(rows, weight[...], preferred_element_type=F32).astype(BF16)


def gate_up_kernel(
    layer_no,
    chunk,
    x_ref,
    a,
    b,
    c,
    d,
    gain_ref,
    gate_hbm,
    gate_other,
    up_hbm,
    up_other,
    out_ref,
    payload_ref,
    gate,
    up,
    packed,
    sems,
):
    gate_copies = row_copies(layer_no, gate_hbm, gate_other, gate, sems.at[0])
    up_copies = row_copies(layer_no, up_hbm, up_other, up, sems.at[1])
    start_all(gate_copies)
    start_all(up_copies)
    requests = x_ref.shape[0]
    per_chunk = chunk // (packed.shape[0] // requests)
    stride = packed.shape[0] // requests
    count = requests // per_chunk
    blocks = gate.shape[1] // LANES
    half = stride // 2

    def store(row, values):
        for q in range(per_chunk):
            packed[pl.ds(q * stride + row, count, stride=chunk), :] = values[q * count : (q + 1) * count]

    out_ref[...] = pair_sum(x_ref, (a, b, c, d))
    current = out_ref[...].astype(F32)
    scaled = (current * gain_ref[layer_no : layer_no + 1, :].astype(F32)).astype(BF16)
    zeros = jnp.zeros((requests, LANES), F32)
    store(blocks, squares_in_lanes(current))
    for row in [*range(blocks + 1, half), *range(half + blocks, stride)]:
        store(row, zeros)
    for first, copies, weight in ((0, gate_copies, gate), (half, up_copies, up)):
        wait_all(copies)
        product = jnp.dot(scaled, weight[...], preferred_element_type=F32)
        for k in range(blocks):
            store(first + k, product[:, k * LANES : (k + 1) * LANES])
    payload_ref[...] = packed[...].astype(BF16)


def activation_kernel(blocks, sources, half, received_ref, out_ref):
    totals = jnp.sum(received_ref[...].astype(F32).reshape(sources, -1, LANES), axis=0)
    acts = []
    for at in range(0, totals.shape[0], 2 * half):
        squares = totals[at + blocks : at + blocks + 1, 0:1] + totals[at + blocks : at + blocks + 1, 1:2]
        inv = lax.rsqrt(squares / D + EPSILON)
        gate = totals[at : at + half] * inv
        acts.append(gate / (1.0 + jnp.exp(-gate)) * (totals[at + half : at + 2 * half] * inv))
    repeat_into(out_ref, jnp.concatenate(acts, axis=0).astype(BF16))


def down_kernel(
    layer_no, half, chunk, received_ref, own_hbm, other_hbm, out_ref, weight, packed, sems
):
    copies = column_copies(layer_no, own_hbm, other_hbm, weight, sems)
    start_all(copies)
    packed[...] = received_ref[...].astype(F32)
    blocks = weight.shape[0] // LANES // 2
    per_chunk = chunk // half
    count = out_ref.shape[0] // per_chunk
    columns = []
    for side in range(2):
        for k in range(blocks):
            columns.append(
                jnp.concatenate(
                    [
                        packed[pl.ds(side * chunk + q * half + k, count, stride=2 * chunk), :]
                        for q in range(per_chunk)
                    ],
                    axis=0,
                ).astype(BF16)
            )
    rows = jnp.concatenate(columns, axis=1)
    wait_all(copies)
    out_ref[...] = jnp.dot(rows, weight[...], preferred_element_type=F32).astype(BF16)


def last_kernel(x_ref, a, b, c, d, out_ref):
    total = pair_sum(x_ref, (a, b, c, d)).astype(F32)
    width = out_ref.shape[1]
    out_ref[...] = jnp.where(core_side() == 0, total[:, :width], total[:, width:]).astype(BF16)


def exchange(array, n_req):
    shape = array.shape
    sides = [list(range(core, n_req, 2)) for core in range(2)]
    count = n_req // 2
    blocks = array.reshape((count, shape[0] // count) + shape[1:])
    return lax.all_to_all(
        blocks, "req", split_axis=0, concat_axis=0, tiled=True, axis_index_groups=sides
    ).reshape(shape)


def exchange_all(array, n_req):
    shape = array.shape
    blocks = array.reshape((n_req, shape[0] // n_req) + shape[1:])
    return lax.all_to_all(blocks, "req", split_axis=0, concat_axis=0, tiled=True).reshape(shape)


def from_pair(array, n_req):
    return lax.ppermute(array, "req", [(i, i ^ 1) for i in range(n_req)])


def tp_parts(partial_sum):
    n_tp = lax.axis_size("tp")
    one, three, two = [
        lax.ppermute(partial_sum, "tp", [(i, (i + shift) % n_tp) for i in range(n_tp)])
        for shift in (1, 3, 2)
    ]
    return [partial_sum, two, one, three]


def shards(
    hidden,
    attn_gain,
    q_weight,
    o_weight,
    ffn_gain,
    gate_weight,
    up_weight,
    down_weight,
    kv_pool,
    block_home,
    chosen,
    chosen_count,
):
    n_req = lax.axis_size("req")
    requests, width = hidden.shape
    pool_dev = kv_pool.shape[1]
    block_tokens, head_size = kv_pool.shape[4:]
    heads = q_weight.shape[2] // head_size // 2
    side = n_req // 2
    q_rows = requests * heads
    sent_rows = q_rows + requests
    stat_rows = q_rows + 16
    f_rows = 16
    hidden_half = gate_weight.shape[2] // 2
    blocks = hidden_half // LANES
    tables = rotary_tables(float(block_home.shape[1] * block_tokens - 1), head_size)
    dma = pltpu.SemaphoreType.DMA

    def rows_type(rows, kind=BF16):
        return jax.ShapeDtypeStruct((rows, LANES), kind)

    def rows_scratch(rows):
        return pltpu.VMEM((rows, LANES), F32)

    def pair_type(rows):
        return jax.ShapeDtypeStruct((rows, 2 * width), BF16)

    keep, send = call(
        functools.partial(first_query_kernel, pool_dev),
        [rows_type(sent_rows, F32), rows_type(sent_rows)],
        [HBM] * 6,
        [
            pltpu.VMEM(hidden.shape, BF16),
            pltpu.VMEM(attn_gain.shape, BF16),
            pltpu.VMEM(q_weight.shape[1:], BF16),
            pltpu.VMEM(block_home.shape, jnp.int32),
            pltpu.VMEM((LAYERS, chosen.shape[3]), jnp.int32),
            pltpu.VMEM((LAYERS, 1), jnp.int32),
            rows_scratch(q_rows),
            dma((6,)),
        ],
        limit=62,
    )(
        hidden,
        attn_gain,
        q_weight,
        block_home,
        chosen.reshape(LAYERS, -1),
        chosen_count.reshape(LAYERS, 1),
    )
    payload = call(pair_total_kernel, rows_type(side * sent_rows), [VMEM] * 2)(
        keep, from_pair(send, n_req)
    )
    pool_other = from_pair(kv_pool, n_req)
    o_other = from_pair(o_weight, n_req)
    gate_other = from_pair(gate_weight, n_req)
    up_other = from_pair(up_weight, n_req)
    down_other = from_pair(down_weight, n_req)
    q_other = from_pair(q_weight, n_req)
    current, attn_gain, ffn_gain = call(
        pair_state_kernel,
        [pair_type(requests), pair_type(LAYERS), pair_type(LAYERS)],
        [VMEM] * 6,
    )(
        hidden,
        from_pair(hidden, n_req),
        attn_gain,
        from_pair(attn_gain, n_req),
        ffn_gain,
        from_pair(ffn_gain, n_req),
    )

    parts = None
    table = None
    for layer_no in range(LAYERS):
        if parts is not None:
            current, payload = call(
                functools.partial(query_kernel, layer_no),
                [pair_type(requests), rows_type(side * sent_rows)],
                [VMEM] * 6 + [HBM] * 2,
                [
                    pltpu.VMEM((2 * width, heads * head_size), BF16),
                    rows_scratch(q_rows),
                    dma((2,)),
                ],
            )(current, *parts, attn_gain, q_weight, q_other)
        received = exchange(payload, n_req)
        scratch = [
            pltpu.VMEM((2, pool_dev, 2, block_tokens, head_size), BF16),
            rows_scratch(q_rows),
            dma((2,)),
        ]
        if table is None:
            payload, table = call(
                functools.partial(first_block_kernel, side),
                [rows_type(side * stat_rows), rows_type(requests, F32)],
                [VMEM] * 2 + [HBM] * 2,
                scratch,
            )(received, tables, kv_pool, pool_other)
        else:
            payload = call(
                functools.partial(later_block_kernel, layer_no, side),
                rows_type(side * stat_rows),
                [VMEM] * 3 + [HBM] * 2,
                scratch,
            )(received, table, tables, kv_pool, pool_other)
        context = call(functools.partial(combine_kernel, side), rows_type(q_rows), [VMEM])(
            exchange(payload, n_req)
        )
        own = call(
            functools.partial(context_kernel, layer_no, requests),
            pair_type(requests),
            [VMEM] * 2 + [HBM] * 2,
            [pltpu.VMEM((o_weight.shape[1], 2 * width), BF16), rows_scratch(q_rows), dma((2,))],
        )(context, from_pair(context, n_req), o_weight, o_other)
        chunk = requests // side * 2 * f_rows
        current, payload = call(
            functools.partial(gate_up_kernel, layer_no, chunk),
            [pair_type(requests), rows_type(requests * 2 * f_rows)],
            [VMEM] * 6 + [HBM] * 4,
            [
                pltpu.VMEM((2 * width, hidden_half), BF16),
                pltpu.VMEM((2 * width, hidden_half), BF16),
                rows_scratch(requests * 2 * f_rows),
                dma((2, 2)),
            ],
        )(current, *tp_parts(own), ffn_gain, gate_weight, gate_other, up_weight, up_other)
        chunk = requests // side * f_rows
        act = call(
            functools.partial(activation_kernel, blocks, side, f_rows),
            rows_type(n_req * chunk),
            [VMEM],
        )(exchange(payload, n_req))
        own = call(
            functools.partial(down_kernel, layer_no, f_rows, chunk),
            pair_type(requests),
            [VMEM] + [HBM] * 2,
            [
                pltpu.VMEM((down_weight.shape[1], 2 * width), BF16),
                rows_scratch(n_req * chunk),
                dma((2,)),
            ],
        )(exchange_all(act, n_req), down_weight, down_other)
        parts = tp_parts(own)
    return call(last_kernel, jax.ShapeDtypeStruct(hidden.shape, BF16), [VMEM] * 5)(current, *parts)


def solution(mesh):
    return jax.shard_map(
        shards,
        mesh=mesh,
        in_specs=(
            P(None, "req"),
            P(None, "req"),
            P(None, "req", "tp"),
            P(None, "tp", "req"),
            P(None, "req"),
            P(None, "req", "tp"),
            P(None, "req", "tp"),
            P(None, "tp", "req"),
            P(None, "req", "tp", None, None, None),
            P("req", None),
            P(None, "req", "tp", None),
            P(None, "req", "tp"),
        ),
        out_specs=P(None, "req"),
        check_vma=False,
    )
```

time: 185 us -> 194 us (1.049)
  blocking collectives: 113 us -> 64.3 us
  waiting for transfers between devices: 30.7 us -> 49.3 us
  starting transfers between devices: 21.7 us -> 38.5 us
  Pallas kernels: 13.6 us -> 27.1 us
  local copies, waits for them, and re-layouts: 5.1 us -> 14 us
    all_to_all x8 -> x4, blocking collectives: 113 us -> 52.3 us  [exchange(): lax.all_to_all(blocks, 'req', split_axis=0, concat_axis=0, tiled=True, ax...]
    all_to_all x0 -> x3, waiting for transfers between devices: none -> 30.9 us  [the longest x2 22 us: exchange(): lax.all_to_all(blocks, 'req', split_axis=0, concat_axis=0, tiled=True, ax...]
    all_to_all x0 -> x3, starting transfers between devices: none -> 15.2 us  [the longest x2 11.4 us: exchange(): lax.all_to_all(blocks, 'req', split_axis=0, concat_axis=0, tiled=True, ax...]
    pallas_call x20 -> x15, Pallas kernels: 12.6 us -> 25 us  [the longest x2 4.95 us: shards(): call(functools.partial(down_kernel, layer_no, f_rows, chunk), pair_type(r...]
    all_to_all x0 -> x1, blocking collectives: none -> 12.1 us  [exchange_all(): lax.all_to_all(blocks, 'req', split_axis=0, concat_axis=0, tiled=True)]
    unnamed x26 -> x38, local copies, waits for them, and re-layouts: 3.8 us -> 12.7 us
    ppermute x12, waiting for transfers between devices: 15.3 us -> 8.1 us  [from_pair(): return lax.ppermute(array, 'req', [(i, i ^ 1) for i in range(n_req)])]
    ppermute x12, waiting for transfers between devices: 15.4 us -> 10.3 us  [tp_parts(): lax.ppermute(partial_sum, 'tp', [(i, (i + shift) % n_tp) for i in range(n...]
  transfers between devices with their start and end apart: 24 -> 27, of which waited for: 19 -> 19; matrix products, arithmetic and copies ran while one was open for 0% -> 1% of each run, Pallas kernels for 0% -> 8%
where the time goes in v5:
time: 194 us; the launch traced here: 193 us
  blocking collectives  64.3 us (33%)
  waiting for transfers between devices  49.3 us (25%)
  starting transfers between devices  38.5 us (20%)
  Pallas kernels  27.1 us (14%)
  local copies, waits for them, and re-layouts  14 us (7%)
    all_to_all x4, blocking collectives, exchange(): lax.all_to_all(blocks, 'req', split_axis=0, concat_axis=0, tiled=True, ax...  52.3 us
    all_to_all x2, waiting for transfers between devices, exchange(): lax.all_to_all(blocks, 'req', split_axis=0, concat_axis=0, tiled=True, ax...  22 us
    ppermute x12, starting transfers between devices, tp_parts(): lax.ppermute(partial_sum, 'tp', [(i, (i + shift) % n_tp) for i in range(n...  21.2 us
    unnamed x38, local copies, waits for them, and re-layouts  12.7 us
    all_to_all x1, blocking collectives, exchange_all(): lax.all_to_all(blocks, 'req', split_axis=0, concat_axis=0, tiled=True)  12.1 us
    all_to_all x2, starting transfers between devices, exchange(): lax.all_to_all(blocks, 'req', split_axis=0, concat_axis=0, tiled=True, ax...  11.4 us
    ppermute x12, waiting for transfers between devices, tp_parts(): lax.ppermute(partial_sum, 'tp', [(i, (i + shift) % n_tp) for i in range(n...  10.3 us
    all_to_all x1, waiting for transfers between devices, exchange_all(): lax.all_to_all(blocks, 'req', split_axis=0, concat_axis=0, tiled=True)  8.89 us
  transfers between devices with their start and end apart: 27, of which 19 were waited for; matrix products, arithmetic and copies ran while one was open for 1% of the time, Pallas kernels for 8%

profile of v5, /device:TPU:0, one launch (start us, length us, event | category | flops | bytes accessed | tf_op | source)
XLA Modules:
  0.0 193.5 jit_solution(3399670619901283708)
XLA Ops:
  4.5 3.0 %collective-permute-done.3.received_ref = bf16[160,128]{1,0:T(8,128)(2,1)S(1)} collective-permute-done((bf16[160,128]{1,0:T(8,128)(2,1)}, bf16[160,128]{1,0:T(8,128)(2,1)S(1)}, u32[]{:S(2)}, u32[]{:S(2)}) %collective-permute-start.3) | collective-permute-done | bytes 40992 | tf_op jit(solution)/shard_map/ppermute | solution.py:490
  9.3 7.1 %all-to-all-start = ((bf16[16,160,128]{2,1,0:T(8,128)(2,1)}), bf16[16,160,128]{2,1,0:T(8,128)(2,1)S(1)}, u32[]{:S(2)}, u32[]{:S(2)}) async-start(bf16[16,160,128]{2,1,0:T(8,128)(2,1)} %bitcast.2), calls=%async_computation | async-start | bytes 1310720 | tf_op jit(solution)/shard_map/all_to_all | solution.py:478
  16.5 13.1 %all-to-all-done = bf16[16,160,128]{2,1,0:T(8,128)(2,1)S(1)} async-done(((bf16[16,160,128]{2,1,0:T(8,128)(2,1)}), bf16[16,160,128]{2,1,0:T(8,128)(2,1)S(1)}, u32[]{:S(2)}, u32[]{:S(2)}) %all-to-all-start) | async-done | bytes 655392 | tf_op jit(solution)/shard_map/all_to_all | solution.py:478
  30.5 2.2 %copy-done = bf16[2,32,1,2,128,128]{5,4,3,2,1,0:T(8,128)(2,1)S(1)} copy-done((bf16[2,32,1,2,128,128]{5,4,3,2,1,0:T(8,128)(2,1)S(1)}, bf16[2,32,1,2,128,128]{5,4,3,2,1,0:T(8,128)(2,1)}, u32[]{:S(2)}) %copy-start) | copy-done | bytes 4194328
  34.5 4.5 %shard_map.130 = (bf16[2304,128]{1,0:T(8,128)(2,1)S(1)}, f32[32,128]{1,0:T(8,128)S(1)}) custom-call(bf16[2560,128]{1,0:T(8,128)(2,1)S(1)} %bitcast.18, f32[2,128]{1,0:T(2,128)S(1)} %copy-done.15, bf16[2,32,1,2,128,128]{5,4,3,2,1,0:T(8,128)(2,1)S(1)} %copy-done, bf16[2,32,1,2,128,128]{5,4,3,2,1,0:T(8,128)(2,1)} %collective-permute-done.4.other_hbm), custom_call_target="tpu_custom_call" | custom-call | tf_op jit(solution)/shard_map/pallas_call | solution.py:606
  39.8 4.2 %all-to-all-start.1 = ((bf16[16,144,128]{2,1,0:T(8,128)(2,1)}), bf16[16,144,128]{2,1,0:T(8,128)(2,1)}, u32[]{:S(2)}, u32[]{:S(2)}) async-start(bf16[16,144,128]{2,1,0:T(8,128)(2,1)} %bitcast.28), calls=%async_computation.1 | async-start | bytes 1179648 | tf_op jit(solution)/shard_map/all_to_all | solution.py:478
  46.7 8.9 %all-to-all-done.1 = bf16[16,144,128]{2,1,0:T(8,128)(2,1)} async-done(((bf16[16,144,128]{2,1,0:T(8,128)(2,1)}), bf16[16,144,128]{2,1,0:T(8,128)(2,1)}, u32[]{:S(2)}, u32[]{:S(2)}) %all-to-all-start.1) | async-done | bytes 589856 | tf_op jit(solution)/shard_map/all_to_all | solution.py:478
  59.6 3.9 %collective-permute-start.7 = (bf16[32,512]{1,0:T(8,128)(2,1)S(1)}, bf16[32,512]{1,0:T(8,128)(2,1)S(1)}, u32[]{:S(2)}, u32[]{:S(2)}) collective-permute-start(bf16[32,512]{1,0:T(8,128)(2,1)S(1)} %shard_map.132.a), channel_id=1, source_target_pairs={{0,2},{1,3},{2,0},{3,1},{4,6},{5,7},{6,4},{7,5},{8,10},{9,11},{10,... | collective-permute-start | bytes 98312 | tf_op jit(solution)/shard_map/ppermute | solution.py:496
  64.5 2.2 %collective-permute-start.9 = (bf16[32,512]{1,0:T(8,128)(2,1)S(1)}, bf16[32,512]{1,0:T(8,128)(2,1)S(1)}, u32[]{:S(2)}, u32[]{:S(2)}) collective-permute-start(bf16[32,512]{1,0:T(8,128)(2,1)S(1)} %shard_map.132.a), channel_id=1, source_target_pairs={{0,3},{1,0},{2,1},{3,2},{4,7},{5,4},{6,5},{7,6},{8,11},{9,8},{10,9... | collective-permute-start | bytes 98312 | tf_op jit(solution)/shard_map/ppermute | solution.py:496
  68.6 2.0 %copy-done.4 = bf16[2,256,3584]{2,1,0:T(8,128)(2,1)S(1)} copy-done((bf16[2,256,3584]{2,1,0:T(8,128)(2,1)S(1)}, bf16[2,256,3584]{2,1,0:T(8,128)(2,1)}, u32[]{:S(2)}) %copy-start.4) | copy-done | bytes 3670040
  72.7 2.3 %shard_map.133 = (bf16[32,512]{1,0:T(8,128)(2,1)S(1)}, bf16[1024,128]{1,0:T(8,128)(2,1)S(1)}) custom-call(bf16[32,512]{1,0:T(8,128)(2,1)S(1)} %get-tuple-element.18.x_ref, bf16[32,512]{1,0:T(8,128)(2,1)S(1)} %shard_map.132.a, bf16[32,512]{1,0:T(8,128)(2,1)S(1)} %collective-permute-done.7.b, bf16[32,512]{1,0:T(8,128)(2,1)S(1)} %collective-permute-done.8.c, ...), custom_call_target="tpu_custom_call" | custom-call | tf_op jit(solution)/shard_map/pallas_call | solution.py:629
  75.0 11.7 %all_to_all.40 = bf16[16,64,128]{2,1,0:T(8,128)(2,1)S(1)} all-to-all(bf16[16,64,128]{2,1,0:T(8,128)(2,1)S(1)} %bitcast.30), channel_id=1, replica_groups={{0,8,16,24,32,40,48,56,64,72,80,88,96,104,112,120},{4,12,20,28,36,44,52..., dimensions={0} | all-to-all | bytes 524288 | tf_op jit(solution)/shard_map/all_to_all | solution.py:478
  87.5 3.9 %all-to-all-start.3 = ((bf16[32,32,128]{2,1,0:T(8,128)(2,1)}), bf16[32,32,128]{2,1,0:T(8,128)(2,1)S(1)}, u32[]{:S(2)}, u32[]{:S(2)}) async-start(bf16[32,32,128]{2,1,0:T(8,128)(2,1)} %bitcast.8), calls=%async_computation.3 | async-start | bytes 524288 | tf_op jit(solution)/shard_map/all_to_all | solution.py:486
  91.4 8.9 %all-to-all-done.3 = bf16[32,32,128]{2,1,0:T(8,128)(2,1)S(1)} async-done(((bf16[32,32,128]{2,1,0:T(8,128)(2,1)}), bf16[32,32,128]{2,1,0:T(8,128)(2,1)S(1)}, u32[]{:S(2)}, u32[]{:S(2)}) %all-to-all-start.3) | async-done | bytes 262176 | tf_op jit(solution)/shard_map/all_to_all | solution.py:486
  102.3 2.5 %shard_map.135.a = bf16[32,512]{1,0:T(8,128)(2,1)S(1)} custom-call(bf16[1024,128]{1,0:T(8,128)(2,1)S(1)} %bitcast.25, bf16[2,3584,256]{2,1,0:T(8,128)(2,1)S(1)} %copy-done.2, bf16[2,3584,256]{2,1,0:T(8,128)(2,1)} %collective-permute-done.12.other_hbm), custom_call_target="tpu_custom_call" | custom-call | tf_op jit(solution)/shard_map/pallas_call | solution.py:646
  106.4 2.6 %collective-permute-start.14 = (bf16[32,512]{1,0:T(8,128)(2,1)S(1)}, bf16[32,512]{1,0:T(8,128)(2,1)S(1)}, u32[]{:S(2)}, u32[]{:S(2)}) collective-permute-start(bf16[32,512]{1,0:T(8,128)(2,1)S(1)} %shard_map.135.a), channel_id=1, source_target_pairs={{0,1},{1,2},{2,3},{3,0},{4,5},{5,6},{6,7},{7,4},{8,9},{9,10},{10,1... | collective-permute-start | bytes 98312 | tf_op jit(solution)/shard_map/ppermute | solution.py:496
  114.2 14.9 %all_to_all.41 = bf16[16,160,128]{2,1,0:T(8,128)(2,1)S(1)} all-to-all(bf16[16,160,128]{2,1,0:T(8,128)(2,1)S(1)} %bitcast.27), channel_id=1, replica_groups={{0,8,16,24,32,40,48,56,64,72,80,88,96,104,112,120},{4,12,20,28,36,44,52..., dimensions={0} | all-to-all | bytes 1310720 | tf_op jit(solution)/shard_map/all_to_all | solution.py:478
  129.2 4.2 %shard_map.137 = bf16[2304,128]{1,0:T(8,128)(2,1)S(1)} custom-call(bf16[2560,128]{1,0:T(8,128)(2,1)S(1)} %bitcast.19, f32[32,128]{1,0:T(8,128)S(1)} %get-tuple-element.28.table_ref, f32[2,128]{1,0:T(2,128)S(1)} %copy-done.16, bf16[2,32,1,2,128,128]{5,4,3,2,1,0:T(8,128)(2,1)S(1)} %copy-done.1, bf16[2,32,1,2,128,128]{5,4,3,2,1,0:T(8,128)(2,1)} %collective-permute-done.4.other_hbm), custom_call_target="tpu_custom_call" | custom-call | tf_op jit(solution)/shard_map/pallas_call | solution.py:613
  133.3 13.9 %all_to_all.42 = bf16[16,144,128]{2,1,0:T(8,128)(2,1)S(1)} all-to-all(bf16[16,144,128]{2,1,0:T(8,128)(2,1)S(1)} %bitcast.20), channel_id=1, replica_groups={{0,8,16,24,32,40,48,56,64,72,80,88,96,104,112,120},{4,12,20,28,36,44,52..., dimensions={0} | all-to-all | bytes 1179648 | tf_op jit(solution)/shard_map/all_to_all | solution.py:478
  156.2 2.4 %shard_map.140 = (bf16[32,512]{1,0:T(8,128)(2,1)S(1)}, bf16[1024,128]{1,0:T(8,128)(2,1)S(1)}) custom-call(bf16[32,512]{1,0:T(8,128)(2,1)S(1)} %get-tuple-element.26.x_ref, bf16[32,512]{1,0:T(8,128)(2,1)S(1)} %shard_map.139.a, bf16[32,512]{1,0:T(8,128)(2,1)S(1)} %collective-permute-done.18.b, bf16[32,512]{1,0:T(8,128)(2,1)S(1)} %collective-permute-done.19.c, ...), custom_call_target="tpu_custom_call" | custom-call | tf_op jit(solution)/shard_map/pallas_call | solution.py:629
  158.7 11.8 %all_to_all.43 = bf16[16,64,128]{2,1,0:T(8,128)(2,1)S(1)} all-to-all(bf16[16,64,128]{2,1,0:T(8,128)(2,1)S(1)} %bitcast.29), channel_id=1, replica_groups={{0,8,16,24,32,40,48,56,64,72,80,88,96,104,112,120},{4,12,20,28,36,44,52..., dimensions={0} | all-to-all | bytes 524288 | tf_op jit(solution)/shard_map/all_to_all | solution.py:478
  170.7 12.1 %all_to_all.44 = bf16[32,32,128]{2,1,0:T(8,128)(2,1)S(1)} all-to-all(bf16[32,32,128]{2,1,0:T(8,128)(2,1)S(1)} %bitcast.24), channel_id=1, replica_groups=mesh['req'=32,'tp'=4] {'req'}, dimensions={0} | all-to-all | bytes 524288 | tf_op jit(solution)/shard_map/all_to_all | solution.py:486
  182.8 2.4 %shard_map.142.a = bf16[32,512]{1,0:T(8,128)(2,1)S(1)} custom-call(bf16[1024,128]{1,0:T(8,128)(2,1)S(1)} %bitcast.26, bf16[2,3584,256]{2,1,0:T(8,128)(2,1)S(1)} %copy-done.3, bf16[2,3584,256]{2,1,0:T(8,128)(2,1)} %collective-permute-done.12.other_hbm), custom_call_target="tpu_custom_call" | custom-call | tf_op jit(solution)/shard_map/pallas_call | solution.py:646
  186.8 2.1 %collective-permute-start.22 = (bf16[32,512]{1,0:T(8,128)(2,1)S(1)}, bf16[32,512]{1,0:T(8,128)(2,1)S(1)}, u32[]{:S(2)}, u32[]{:S(2)}) collective-permute-start(bf16[32,512]{1,0:T(8,128)(2,1)S(1)} %shard_map.142.a), channel_id=1, source_target_pairs={{0,1},{1,2},{2,3},{3,0},{4,5},{5,6},{6,7},{7,4},{8,9},{9,10},{10,1... | collective-permute-start | bytes 98312 | tf_op jit(solution)/shard_map/ppermute | solution.py:496
  (91 shorter events, 46.3 us)
Async XLA Ops:
  0.0 30.5 %collective-permute-start.4 = (bf16[2,32,1,2,128,128]{5,4,3,2,1,0:T(8,128)(2,1)}, bf16[2,32,1,2,128,128]{5,4,3,2,1,0:T(8,128)(2,1)}, u32[]{:S(2)}, u32[]{:S(2)}) collective-permute-start(bf16[2,32,1,2,128,128]{5,4,3,2,1,0:T(8,128)(2,1)} %own_hbm.11), channel_id=1, source_target_pairs={{0,4},{4,0},{8,12},{12,8},{16,20},{20,16},{24,28},{28,24},{32,36},... | collective-permute-start | bytes 12582920 | tf_op jit(solution)/shard_map/ppermute | solution.py:490
  0.0 63.5 %collective-permute-start.10 = (bf16[2,256,3584]{2,1,0:T(8,128)(2,1)}, bf16[2,256,3584]{2,1,0:T(8,128)(2,1)}, u32[]{:S(2)}, u32[]{:S(2)}) collective-permute-start(bf16[2,256,3584]{2,1,0:T(8,128)(2,1)} %gate_hbm.3), channel_id=1, source_target_pairs={{0,4},{4,0},{8,12},{12,8},{16,20},{20,16},{24,28},{28,24},{32,36},... | collective-permute-start | bytes 11010056 | tf_op jit(solution)/shard_map/ppermute | solution.py:490
  0.5 64.0 %collective-permute-start.11 = (bf16[2,256,3584]{2,1,0:T(8,128)(2,1)}, bf16[2,256,3584]{2,1,0:T(8,128)(2,1)}, u32[]{:S(2)}, u32[]{:S(2)}) collective-permute-start(bf16[2,256,3584]{2,1,0:T(8,128)(2,1)} %up_hbm.3), channel_id=1, source_target_pairs={{0,4},{4,0},{8,12},{12,8},{16,20},{20,16},{24,28},{28,24},{32,36},... | collective-permute-start | bytes 11010056 | tf_op jit(solution)/shard_map/ppermute | solution.py:490
  0.5 90.9 %collective-permute-start.12 = (bf16[2,3584,256]{2,1,0:T(8,128)(2,1)}, bf16[2,3584,256]{2,1,0:T(8,128)(2,1)}, u32[]{:S(2)}, u32[]{:S(2)}) collective-permute-start(bf16[2,3584,256]{2,1,0:T(8,128)(2,1)} %own_hbm.13), channel_id=1, source_target_pairs={{0,4},{4,0},{8,12},{12,8},{16,20},{20,16},{24,28},{28,24},{32,36},... | collective-permute-start | bytes 11010056 | tf_op jit(solution)/shard_map/ppermute | solution.py:490
  4.4 3.1 %collective-permute-start.3 = (bf16[160,128]{1,0:T(8,128)(2,1)}, bf16[160,128]{1,0:T(8,128)(2,1)S(1)}, u32[]{:S(2)}, u32[]{:S(2)}) collective-permute-start(bf16[160,128]{1,0:T(8,128)(2,1)} %get-tuple-element.20), channel_id=1, source_target_pairs={{0,4},{4,0},{8,12},{12,8},{16,20},{20,16},{24,28},{28,24},{32,36},... | collective-permute-start | bytes 122888 | tf_op jit(solution)/shard_map/ppermute | solution.py:490
  9.3 20.4 %all-to-all-start = ((bf16[16,160,128]{2,1,0:T(8,128)(2,1)}), bf16[16,160,128]{2,1,0:T(8,128)(2,1)S(1)}, u32[]{:S(2)}, u32[]{:S(2)}) async-start(bf16[16,160,128]{2,1,0:T(8,128)(2,1)} %bitcast.2), calls=%async_computation | async-start | bytes 1310720 | tf_op jit(solution)/shard_map/all_to_all | solution.py:478
  16.4 40.7 %collective-permute-start.6 = (bf16[2,1024,256]{2,1,0:T(8,128)(2,1)}, bf16[2,1024,256]{2,1,0:T(8,128)(2,1)S(1)}, u32[]{:S(2)}, u32[]{:S(2)}) collective-permute-start(bf16[2,1024,256]{2,1,0:T(8,128)(2,1)} %own_hbm.12), channel_id=1, source_target_pairs={{0,4},{4,0},{8,12},{12,8},{16,20},{20,16},{24,28},{28,24},{32,36},... | collective-permute-start | bytes 3145736 | tf_op jit(solution)/shard_map/ppermute | solution.py:490
  39.8 15.7 %all-to-all-start.1 = ((bf16[16,144,128]{2,1,0:T(8,128)(2,1)}), bf16[16,144,128]{2,1,0:T(8,128)(2,1)}, u32[]{:S(2)}, u32[]{:S(2)}) async-start(bf16[16,144,128]{2,1,0:T(8,128)(2,1)} %bitcast.28), calls=%async_computation.1 | async-start | bytes 1179648 | tf_op jit(solution)/shard_map/all_to_all | solution.py:478
  46.5 63.2 %collective-permute-start.16 = (bf16[2,256,1024]{2,1,0:T(8,128)(2,1)S(1)}, bf16[2,256,1024]{2,1,0:T(8,128)(2,1)}, u32[]{:S(2)}, u32[]{:S(2)}) collective-permute-start(bf16[2,256,1024]{2,1,0:T(8,128)(2,1)S(1)} %copy-done.8), channel_id=1, source_target_pairs={{0,4},{4,0},{8,12},{12,8},{16,20},{20,16},{24,28},{28,24},{32,36},... | collective-permute-start | bytes 3145736 | tf_op jit(solution)/shard_map/ppermute | solution.py:490
  57.1 1.3 collective-permute-start.5
  59.6 7.1 %collective-permute-start.7 = (bf16[32,512]{1,0:T(8,128)(2,1)S(1)}, bf16[32,512]{1,0:T(8,128)(2,1)S(1)}, u32[]{:S(2)}, u32[]{:S(2)}) collective-permute-start(bf16[32,512]{1,0:T(8,128)(2,1)S(1)} %shard_map.132.a), channel_id=1, source_target_pairs={{0,2},{1,3},{2,0},{3,1},{4,6},{5,7},{6,4},{7,5},{8,10},{9,11},{10,... | collective-permute-start | bytes 98312 | tf_op jit(solution)/shard_map/ppermute | solution.py:496
  63.5 5.1 %collective-permute-start.8 = (bf16[32,512]{1,0:T(8,128)(2,1)S(1)}, bf16[32,512]{1,0:T(8,128)(2,1)S(1)}, u32[]{:S(2)}, u32[]{:S(2)}) collective-permute-start(bf16[32,512]{1,0:T(8,128)(2,1)S(1)} %shard_map.132.a), channel_id=1, source_target_pairs={{0,1},{1,2},{2,3},{3,0},{4,5},{5,6},{6,7},{7,4},{8,9},{9,10},{10,1... | collective-permute-start | bytes 98312 | tf_op jit(solution)/shard_map/ppermute | solution.py:496
  64.5 4.1 %collective-permute-start.9 = (bf16[32,512]{1,0:T(8,128)(2,1)S(1)}, bf16[32,512]{1,0:T(8,128)(2,1)S(1)}, u32[]{:S(2)}, u32[]{:S(2)}) collective-permute-start(bf16[32,512]{1,0:T(8,128)(2,1)S(1)} %shard_map.132.a), channel_id=1, source_target_pairs={{0,3},{1,0},{2,1},{3,2},{4,7},{5,4},{6,5},{7,6},{8,11},{9,8},{10,9... | collective-permute-start | bytes 98312 | tf_op jit(solution)/shard_map/ppermute | solution.py:496
  87.5 12.8 %all-to-all-start.3 = ((bf16[32,32,128]{2,1,0:T(8,128)(2,1)}), bf16[32,32,128]{2,1,0:T(8,128)(2,1)S(1)}, u32[]{:S(2)}, u32[]{:S(2)}) async-start(bf16[32,32,128]{2,1,0:T(8,128)(2,1)} %bitcast.8), calls=%async_computation.3 | async-start | bytes 524288 | tf_op jit(solution)/shard_map/all_to_all | solution.py:486
  104.9 5.5 %collective-permute-start.13 = (bf16[32,512]{1,0:T(8,128)(2,1)S(1)}, bf16[32,512]{1,0:T(8,128)(2,1)S(1)}, u32[]{:S(2)}, u32[]{:S(2)}) collective-permute-start(bf16[32,512]{1,0:T(8,128)(2,1)S(1)} %shard_map.135.a), channel_id=1, source_target_pairs={{0,2},{1,3},{2,0},{3,1},{4,6},{5,7},{6,4},{7,5},{8,10},{9,11},{10,... | collective-permute-start | bytes 98312 | tf_op jit(solution)/shard_map/ppermute | solution.py:496
  106.4 5.1 %collective-permute-start.14 = (bf16[32,512]{1,0:T(8,128)(2,1)S(1)}, bf16[32,512]{1,0:T(8,128)(2,1)S(1)}, u32[]{:S(2)}, u32[]{:S(2)}) collective-permute-start(bf16[32,512]{1,0:T(8,128)(2,1)S(1)} %shard_map.135.a), channel_id=1, source_target_pairs={{0,1},{1,2},{2,3},{3,0},{4,5},{5,6},{6,7},{7,4},{8,9},{9,10},{10,1... | collective-permute-start | bytes 98312 | tf_op jit(solution)/shard_map/ppermute | solution.py:496
  109.1 3.9 %collective-permute-start.15 = (bf16[32,512]{1,0:T(8,128)(2,1)S(1)}, bf16[32,512]{1,0:T(8,128)(2,1)S(1)}, u32[]{:S(2)}, u32[]{:S(2)}) collective-permute-start(bf16[32,512]{1,0:T(8,128)(2,1)S(1)} %shard_map.135.a), channel_id=1, source_target_pairs={{0,3},{1,0},{2,1},{3,2},{4,7},{5,4},{6,5},{7,6},{8,11},{9,8},{10,9... | collective-permute-start | bytes 98312 | tf_op jit(solution)/shard_map/ppermute | solution.py:496
  147.7 1.3 collective-permute-start.17
  149.4 5.6 %collective-permute-start.18 = (bf16[32,512]{1,0:T(8,128)(2,1)S(1)}, bf16[32,512]{1,0:T(8,128)(2,1)S(1)}, u32[]{:S(2)}, u32[]{:S(2)}) collective-permute-start(bf16[32,512]{1,0:T(8,128)(2,1)S(1)} %shard_map.139.a), channel_id=1, source_target_pairs={{0,2},{1,3},{2,0},{3,1},{4,6},{5,7},{6,4},{7,5},{8,10},{9,11},{10,... | collective-permute-start | bytes 98312 | tf_op jit(solution)/shard_map/ppermute | solution.py:496
  150.7 5.1 %collective-permute-start.19 = (bf16[32,512]{1,0:T(8,128)(2,1)S(1)}, bf16[32,512]{1,0:T(8,128)(2,1)S(1)}, u32[]{:S(2)}, u32[]{:S(2)}) collective-permute-start(bf16[32,512]{1,0:T(8,128)(2,1)S(1)} %shard_map.139.a), channel_id=1, source_target_pairs={{0,1},{1,2},{2,3},{3,0},{4,5},{5,6},{6,7},{7,4},{8,9},{9,10},{10,1... | collective-permute-start | bytes 98312 | tf_op jit(solution)/shard_map/ppermute | solution.py:496
  152.3 3.9 %collective-permute-start.20 = (bf16[32,512]{1,0:T(8,128)(2,1)S(1)}, bf16[32,512]{1,0:T(8,128)(2,1)S(1)}, u32[]{:S(2)}, u32[]{:S(2)}) collective-permute-start(bf16[32,512]{1,0:T(8,128)(2,1)S(1)} %shard_map.139.a), channel_id=1, source_target_pairs={{0,3},{1,0},{2,1},{3,2},{4,7},{5,4},{6,5},{7,6},{8,11},{9,8},{10,9... | collective-permute-start | bytes 98312 | tf_op jit(solution)/shard_map/ppermute | solution.py:496
  185.2 5.5 %collective-permute-start.21 = (bf16[32,512]{1,0:T(8,128)(2,1)S(1)}, bf16[32,512]{1,0:T(8,128)(2,1)S(1)}, u32[]{:S(2)}, u32[]{:S(2)}) collective-permute-start(bf16[32,512]{1,0:T(8,128)(2,1)S(1)} %shard_map.142.a), channel_id=1, source_target_pairs={{0,2},{1,3},{2,0},{3,1},{4,6},{5,7},{6,4},{7,5},{8,10},{9,11},{10,... | collective-permute-start | bytes 98312 | tf_op jit(solution)/shard_map/ppermute | solution.py:496
  186.8 5.1 %collective-permute-start.22 = (bf16[32,512]{1,0:T(8,128)(2,1)S(1)}, bf16[32,512]{1,0:T(8,128)(2,1)S(1)}, u32[]{:S(2)}, u32[]{:S(2)}) collective-permute-start(bf16[32,512]{1,0:T(8,128)(2,1)S(1)} %shard_map.142.a), channel_id=1, source_target_pairs={{0,1},{1,2},{2,3},{3,0},{4,5},{5,6},{6,7},{7,4},{8,9},{9,10},{10,1... | collective-permute-start | bytes 98312 | tf_op jit(solution)/shard_map/ppermute | solution.py:496
  188.9 3.9 %collective-permute-start.23 = (bf16[32,512]{1,0:T(8,128)(2,1)S(1)}, bf16[32,512]{1,0:T(8,128)(2,1)S(1)}, u32[]{:S(2)}, u32[]{:S(2)}) collective-permute-start(bf16[32,512]{1,0:T(8,128)(2,1)S(1)} %shard_map.142.a), channel_id=1, source_target_pairs={{0,3},{1,0},{2,1},{3,2},{4,7},{5,4},{6,5},{7,6},{8,11},{9,8},{10,9... | collective-permute-start | bytes 98312 | tf_op jit(solution)/shard_map/ppermute | solution.py:496
  (22 other events, 227.0 us)

commit v6 on v5

--- a/solution.py
+++ b/solution.py
@@ -32,7 +32,7 @@
     return jnp.asarray(tables * scale, F32)
 
 
-def call(kernel, out_shape, in_specs, scratch=(), limit=16, out_specs=None, flops=0, nbytes=0):
+def call(kernel, out_shape, in_specs, scratch=(), limit=16, out_specs=None, flops=10000000000, nbytes=0):
     return pl.pallas_call(
         kernel,
         out_shape=out_shape,
@@ -194,8 +194,8 @@
     ]
     start_all(copies)
     wait_all(copies[:3])
-    lists = [chosen[i : i + 1, :] for i in range(LAYERS)]
-    limits = [counts[i : i + 1, :] for i in range(LAYERS)]
+    lists = [chosen[i, 0] for i in range(LAYERS)]
+    limits = [counts[:, i : i + 1] for i in range(LAYERS)]
     table = slot_table(homes[...], lists, limits, pool_dev, x.shape[0])
     wait_all(copies[3:])
     current = x[...].astype(F32)
@@ -257,12 +257,23 @@
 def block_kernel(
     layer_no, sources, received_ref, table_ref, tables_ref, own_hbm, other_hbm, out_ref, table_out, blocks, packed, sems
 ):
-    copies = pair_copies(
-        own_hbm.at[layer_no, :, 0], other_hbm.at[layer_no, :, 0], blocks.at[0], blocks.at[1], sems
-    )
-    start_all(copies)
+    n_slots = blocks.shape[1]
+    piece = n_slots // 2
+    copies = [
+        [
+            pltpu.make_async_copy(
+                pool.at[layer_no, pl.ds(at, piece), 0, part],
+                blocks.at[b, pl.ds(at, piece), part],
+                sems.at[part * 2 + at // piece, b],
+            )
+            for b, pool in enumerate((own_hbm, other_hbm))
+        ]
+        for part in range(2)
+        for at in (0, piece)
+    ]
+    for pair in copies:
+        start_all(pair)
     rows = packed.shape[0]
-    n_slots = blocks.shape[1]
     totals = jnp.sum(received_ref[...].astype(F32).reshape(sources, -1, LANES), axis=0)
     extra = totals[rows:]
     requests = extra.shape[0]
@@ -299,17 +310,16 @@
     )
     group = 2 * heads
     mine = lax.broadcasted_iota(jnp.int32, (group, LANES), 0) < heads
-    wait_all(copies)
 
     def of_slot(left, p, part, contract):
-        left = left[p * group : (p + 1) * group].astype(BF16)
-        sides = [
-            lax.dot_general(
-                left, blocks[b, p, part], (((1,), (contract,)), ((), ())), preferred_element_type=F32
-            )
-            for b in range(2)
-        ]
-        return jnp.where(mine, sides[0], sides[1])
+        if p % piece == 0:
+            wait_all(copies[part * 2 + p // piece])
+        left = left[p * group : (p + 1) * group]
+        left = jnp.concatenate([jnp.where(mine, left, 0.0), jnp.where(mine, 0.0, left)], axis=1)
+        right = jnp.concatenate([blocks[0, p, part], blocks[1, p, part]], axis=contract)
+        return lax.dot_general(
+            left.astype(BF16), right, (((1,), (contract,)), ((), ())), preferred_element_type=F32
+        )
 
     scores = jnp.concatenate([of_slot(queries, p, 0, 1) for p in range(n_slots)], axis=0)
     block_max = jnp.max(scores, axis=1, keepdims=True)
@@ -397,10 +407,23 @@
     packed,
     sems,
 ):
-    gate_copies = row_copies(layer_no, gate_hbm, gate_other, gate, sems.at[0])
-    up_copies = row_copies(layer_no, up_hbm, up_other, up, sems.at[1])
-    start_all(gate_copies)
-    start_all(up_copies)
+    width = gate.shape[1]
+    piece = width // 2
+    own_rows, other_rows = side_slices(gate_hbm.shape[1])
+    steps = []
+    for i, (own, other, weight) in enumerate(((gate_hbm, gate_other, gate), (up_hbm, up_other, up))):
+        for j in range(2):
+            columns = pl.ds(pl.multiple_of(core_side() * width + j * piece, LANES), piece)
+            local = pl.ds(j * piece, piece)
+            copies = pair_copies(
+                own.at[layer_no, :, columns],
+                other.at[layer_no, :, columns],
+                weight.at[own_rows, local],
+                weight.at[other_rows, local],
+                sems.at[i * 2 + j],
+            )
+            start_all(copies)
+            steps.append((i, j, copies, weight))
     requests = x_ref.shape[0]
     per_chunk = chunk // (packed.shape[0] // requests)
     stride = packed.shape[0] // requests
@@ -419,11 +442,11 @@
     store(blocks, squares_in_lanes(current))
     for row in [*range(blocks + 1, half), *range(half + blocks, stride)]:
         store(row, zeros)
-    for first, copies, weight in ((0, gate_copies, gate), (half, up_copies, up)):
+    for i, j, copies, weight in steps:
         wait_all(copies)
-        product = jnp.dot(scaled, weight[...], preferred_element_type=F32)
-        for k in range(blocks):
-            store(first + k, product[:, k * LANES : (k + 1) * LANES])
+        product = jnp.dot(scaled, weight[:, j * piece : (j + 1) * piece], preferred_element_type=F32)
+        for k in range(piece // LANES):
+            store(i * half + j * (piece // LANES) + k, product[:, k * LANES : (k + 1) * LANES])
     payload_ref[...] = packed[...].astype(BF16)
 
 
@@ -441,14 +464,28 @@
 def down_kernel(
     layer_no, half, chunk, received_ref, own_hbm, other_hbm, out_ref, weight, packed, sems
 ):
-    copies = column_copies(layer_no, own_hbm, other_hbm, weight, sems)
-    start_all(copies)
+    depth = weight.shape[0] // 2
+    own_columns, other_columns = side_slices(own_hbm.shape[2])
+    steps = []
+    for side in range(2):
+        rows = pl.ds(side * depth, depth)
+        steps.append(
+            pair_copies(
+                own_hbm.at[layer_no, rows],
+                other_hbm.at[layer_no, rows],
+                weight.at[rows, own_columns],
+                weight.at[rows, other_columns],
+                sems.at[side],
+            )
+        )
+        start_all(steps[side])
     packed[...] = received_ref[...].astype(F32)
     blocks = weight.shape[0] // LANES // 2
     per_chunk = chunk // half
     count = out_ref.shape[0] // per_chunk
-    columns = []
+    total = 0.0
     for side in range(2):
+        columns = []
         for k in range(blocks):
             columns.append(
                 jnp.concatenate(
@@ -459,9 +496,12 @@
                     axis=0,
                 ).astype(BF16)
             )
-    rows = jnp.concatenate(columns, axis=1)
-    wait_all(copies)
-    out_ref[...] = jnp.dot(rows, weight[...], preferred_element_type=F32).astype(BF16)
+        rows = jnp.concatenate(columns, axis=1)
+        wait_all(steps[side])
+        total += jnp.dot(
+            rows, weight[side * depth : (side + 1) * depth], preferred_element_type=F32
+        )
+    out_ref[...] = total.astype(BF16)
 
 
 def last_kernel(x_ref, a, b, c, d, out_ref):
@@ -546,29 +586,32 @@
             pltpu.VMEM(attn_gain.shape, BF16),
             pltpu.VMEM(q_weight.shape[1:], BF16),
             pltpu.VMEM(block_home.shape, jnp.int32),
-            pltpu.VMEM((LAYERS, chosen.shape[3]), jnp.int32),
-            pltpu.VMEM((LAYERS, 1), jnp.int32),
+            pltpu.VMEM(chosen.shape, jnp.int32),
+            pltpu.VMEM((1, LAYERS), jnp.int32),
             rows_scratch(q_rows),
             dma((6,)),
         ],
-        limit=62,
+        limit=61,
     )(
         hidden,
         attn_gain,
         q_weight,
         block_home,
-        chosen.reshape(LAYERS, -1),
-        chosen_count.reshape(LAYERS, 1),
+        chosen,
+        chosen_count.reshape(1, LAYERS),
     )
     payload = call(pair_total_kernel, rows_type(side * sent_rows), [VMEM] * 2)(
         keep, from_pair(send, n_req)
     )
-    pool_other = from_pair(kv_pool, n_req)
-    o_other = from_pair(o_weight, n_req)
-    gate_other = from_pair(gate_weight, n_req)
-    up_other = from_pair(up_weight, n_req)
-    down_other = from_pair(down_weight, n_req)
-    q_other = from_pair(q_weight, n_req)
+    payload, kv_later, o_later, gate_later, up_later, down_later, q_later = lax.optimization_barrier(
+        (payload, kv_pool, o_weight, gate_weight, up_weight, down_weight, q_weight)
+    )
+    pool_other = from_pair(kv_later, n_req)
+    o_other = from_pair(o_later, n_req)
+    gate_other = from_pair(gate_later, n_req)
+    up_other = from_pair(up_later, n_req)
+    down_other = from_pair(down_later, n_req)
+    q_other = from_pair(q_later, n_req)
     current, attn_gain, ffn_gain = call(
         pair_state_kernel,
         [pair_type(requests), pair_type(LAYERS), pair_type(LAYERS)],
@@ -600,7 +643,7 @@
         scratch = [
             pltpu.VMEM((2, pool_dev, 2, block_tokens, head_size), BF16),
             rows_scratch(q_rows),
-            dma((2,)),
+            dma((4, 2)),
         ]
         if table is None:
             payload, table = call(
@@ -634,7 +677,7 @@
                 pltpu.VMEM((2 * width, hidden_half), BF16),
                 pltpu.VMEM((2 * width, hidden_half), BF16),
                 rows_scratch(requests * 2 * f_rows),
-                dma((2, 2)),
+                dma((4, 2)),
             ],
         )(current, *tp_parts(own), ffn_gain, gate_weight, gate_other, up_weight, up_other)
         chunk = requests // side * f_rows
@@ -650,7 +693,7 @@
             [
                 pltpu.VMEM((down_weight.shape[1], 2 * width), BF16),
                 rows_scratch(n_req * chunk),
-                dma((2,)),
+                dma((2, 2)),
             ],
         )(exchange_all(act, n_req), down_weight, down_other)
         parts = tp_parts(own)

time: 194 us -> 177 us (0.912)
  local copies, waits for them, and re-layouts: 14 us -> 0.97 us
  waiting for transfers between devices: 49.3 us -> 46.8 us
    unnamed x38 -> x22, local copies, waits for them, and re-layouts: 12.7 us -> 0.97 us
    ppermute x12, waiting for transfers between devices: 8.1 us -> 3.63 us  [from_pair(): return lax.ppermute(array, 'req', [(i, i ^ 1) for i in range(n_req)])]
    all_to_all x2, waiting for transfers between devices: 22 us -> 24.3 us  [exchange(): lax.all_to_all(blocks, 'req', split_axis=0, concat_axis=0, tiled=True, ax...]
  transfers between devices with their start and end apart: 27 -> 27, of which waited for: 19 -> 17; matrix products, arithmetic and copies ran while one was open for 1% -> 0% of each run, Pallas kernels for 8% -> 6%
where the time goes in v6:
time: 177 us; the launch traced here: 176 us
  blocking collectives  64.1 us (36%)
  waiting for transfers between devices  46.8 us (26%)
  starting transfers between devices  38.5 us (22%)
  Pallas kernels  25.7 us (15%)
    all_to_all x4, blocking collectives, exchange(): lax.all_to_all(blocks, 'req', split_axis=0, concat_axis=0, tiled=True, ax...  52 us
    all_to_all x2, waiting for transfers between devices, exchange(): lax.all_to_all(blocks, 'req', split_axis=0, concat_axis=0, tiled=True, ax...  24.3 us
    ppermute x12, starting transfers between devices, tp_parts(): lax.ppermute(partial_sum, 'tp', [(i, (i + shift) % n_tp) for i in range(n...  21.2 us
    all_to_all x1, blocking collectives, exchange_all(): lax.all_to_all(blocks, 'req', split_axis=0, concat_axis=0, tiled=True)  12.1 us
    all_to_all x2, starting transfers between devices, exchange(): lax.all_to_all(blocks, 'req', split_axis=0, concat_axis=0, tiled=True, ax...  10.7 us
    ppermute x12, waiting for transfers between devices, tp_parts(): lax.ppermute(partial_sum, 'tp', [(i, (i + shift) % n_tp) for i in range(n...  10.2 us
    all_to_all x1, waiting for transfers between devices, exchange_all(): lax.all_to_all(blocks, 'req', split_axis=0, concat_axis=0, tiled=True)  8.65 us
    pallas_call x2, Pallas kernels, shards(): call(functools.partial(down_kernel, layer_no, f_rows, chunk), pair_type(r...  5.59 us
  transfers between devices with their start and end apart: 27, of which 17 were waited for; matrix products, arithmetic and copies ran while one was open for 0% of the time, Pallas kernels for 6%

profile of v6, /device:TPU:0, one launch (start us, length us, event | category | flops | bytes accessed | tf_op | source)
XLA Modules:
  0.0 176.3 jit_solution(916149731384709656)
XLA Ops:
  0.0 2.0 %shard_map.128 = (f32[160,128]{1,0:T(8,128)}, bf16[160,128]{1,0:T(8,128)(2,1)}) custom-call(bf16[32,256]{1,0:T(8,128)(2,1)} %x_hbm.1, bf16[2,256]{1,0:T(2,128)(2,1)} %gain_hbm.1, bf16[2,256,1024]{2,1,0:T(8,128)(2,1)} %own_hbm.10, s32[1,32]{1,0:T(1,128)} %homes_hbm.1, s32[2,1,1,24]{3,2,1,0:T(1,128)} %chosen_hbm.1, s32[1,2]{1,0:T(1,128)} %bitcast.30), custom_call_target="tpu_custom_call" | custom-call | flops 10000000000 | tf_op jit(solution)/shard_map/pallas_call | solution.py:580
  5.5 7.1 %all-to-all-start = ((bf16[16,160,128]{2,1,0:T(8,128)(2,1)}), bf16[16,160,128]{2,1,0:T(8,128)(2,1)S(1)}, u32[]{:S(2)}, u32[]{:S(2)}) async-start(bf16[16,160,128]{2,1,0:T(8,128)(2,1)} %bitcast.1), calls=%async_computation | async-start | bytes 1310720 | tf_op jit(solution)/shard_map/all_to_all | solution.py:518
  13.2 12.9 %all-to-all-done = bf16[16,160,128]{2,1,0:T(8,128)(2,1)S(1)} async-done(((bf16[16,160,128]{2,1,0:T(8,128)(2,1)}), bf16[16,160,128]{2,1,0:T(8,128)(2,1)S(1)}, u32[]{:S(2)}, u32[]{:S(2)}) %all-to-all-start) | async-done | bytes 655392 | tf_op jit(solution)/shard_map/all_to_all | solution.py:518
  26.1 4.4 %shard_map.130 = (bf16[2304,128]{1,0:T(8,128)(2,1)}, f32[32,128]{1,0:T(8,128)S(1)}) custom-call(bf16[2560,128]{1,0:T(8,128)(2,1)S(1)} %bitcast.17, f32[2,128]{1,0:T(2,128)S(1)} %copy-done.9, bf16[2,32,1,2,128,128]{5,4,3,2,1,0:T(8,128)(2,1)} %own_hbm.11, bf16[2,32,1,2,128,128]{5,4,3,2,1,0:T(8,128)(2,1)} %collective-permute-done.4.other_hbm), custom_call_target="tpu_custom_call" | custom-call | flops 10000000000 | tf_op jit(solution)/shard_map/pallas_call | solution.py:649
  30.5 3.6 %all-to-all-start.1 = ((bf16[16,144,128]{2,1,0:T(8,128)(2,1)}), bf16[16,144,128]{2,1,0:T(8,128)(2,1)S(1)}, u32[]{:S(2)}, u32[]{:S(2)}) async-start(bf16[16,144,128]{2,1,0:T(8,128)(2,1)} %bitcast.3), calls=%async_computation.1 | async-start | bytes 1179648 | tf_op jit(solution)/shard_map/all_to_all | solution.py:518
  34.2 11.5 %all-to-all-done.1 = bf16[16,144,128]{2,1,0:T(8,128)(2,1)S(1)} async-done(((bf16[16,144,128]{2,1,0:T(8,128)(2,1)}), bf16[16,144,128]{2,1,0:T(8,128)(2,1)S(1)}, u32[]{:S(2)}, u32[]{:S(2)}) %all-to-all-start.1) | async-done | bytes 589856 | tf_op jit(solution)/shard_map/all_to_all | solution.py:518
  49.1 3.9 %collective-permute-start.7 = (bf16[32,512]{1,0:T(8,128)(2,1)S(1)}, bf16[32,512]{1,0:T(8,128)(2,1)S(1)}, u32[]{:S(2)}, u32[]{:S(2)}) collective-permute-start(bf16[32,512]{1,0:T(8,128)(2,1)S(1)} %shard_map.132.a), channel_id=1, source_target_pairs={{0,2},{1,3},{2,0},{3,1},{4,6},{5,7},{6,4},{7,5},{8,10},{9,11},{10,... | collective-permute-start | bytes 98312 | tf_op jit(solution)/shard_map/ppermute | solution.py:536
  54.0 2.2 %collective-permute-start.9 = (bf16[32,512]{1,0:T(8,128)(2,1)S(1)}, bf16[32,512]{1,0:T(8,128)(2,1)S(1)}, u32[]{:S(2)}, u32[]{:S(2)}) collective-permute-start(bf16[32,512]{1,0:T(8,128)(2,1)S(1)} %shard_map.132.a), channel_id=1, source_target_pairs={{0,3},{1,0},{2,1},{3,2},{4,7},{5,4},{6,5},{7,6},{8,11},{9,8},{10,9... | collective-permute-start | bytes 98312 | tf_op jit(solution)/shard_map/ppermute | solution.py:536
  56.3 1.8 %collective-permute-done.8.c = bf16[32,512]{1,0:T(8,128)(2,1)S(1)} collective-permute-done((bf16[32,512]{1,0:T(8,128)(2,1)S(1)}, bf16[32,512]{1,0:T(8,128)(2,1)S(1)}, u32[]{:S(2)}, u32[]{:S(2)}) %collective-permute-start.8) | collective-permute-done | bytes 32800 | tf_op jit(solution)/shard_map/ppermute | solution.py:536
  58.1 2.4 %shard_map.133 = (bf16[32,512]{1,0:T(8,128)(2,1)S(1)}, bf16[1024,128]{1,0:T(8,128)(2,1)S(1)}) custom-call(bf16[32,512]{1,0:T(8,128)(2,1)S(1)} %get-tuple-element.25.x_ref, bf16[32,512]{1,0:T(8,128)(2,1)S(1)} %shard_map.132.a, bf16[32,512]{1,0:T(8,128)(2,1)S(1)} %collective-permute-done.7.b, bf16[32,512]{1,0:T(8,128)(2,1)S(1)} %collective-permute-done.8.c, ...), custom_call_target="tpu_custom_call" | custom-call | flops 10000000000 | tf_op jit(solution)/shard_map/pallas_call | solution.py:672
  60.5 11.7 %all_to_all.40 = bf16[16,64,128]{2,1,0:T(8,128)(2,1)S(1)} all-to-all(bf16[16,64,128]{2,1,0:T(8,128)(2,1)S(1)} %bitcast.25), channel_id=1, replica_groups={{0,8,16,24,32,40,48,56,64,72,80,88,96,104,112,120},{4,12,20,28,36,44,52..., dimensions={0} | all-to-all | bytes 524288 | tf_op jit(solution)/shard_map/all_to_all | solution.py:518
  73.0 3.9 %all-to-all-start.3 = ((bf16[32,32,128]{2,1,0:T(8,128)(2,1)}), bf16[32,32,128]{2,1,0:T(8,128)(2,1)S(1)}, u32[]{:S(2)}, u32[]{:S(2)}) async-start(bf16[32,32,128]{2,1,0:T(8,128)(2,1)} %bitcast.7), calls=%async_computation.3 | async-start | bytes 524288 | tf_op jit(solution)/shard_map/all_to_all | solution.py:526
  77.2 8.6 %all-to-all-done.3 = bf16[32,32,128]{2,1,0:T(8,128)(2,1)S(1)} async-done(((bf16[32,32,128]{2,1,0:T(8,128)(2,1)}), bf16[32,32,128]{2,1,0:T(8,128)(2,1)S(1)}, u32[]{:S(2)}, u32[]{:S(2)}) %all-to-all-start.3) | async-done | bytes 262176 | tf_op jit(solution)/shard_map/all_to_all | solution.py:526
  85.8 2.8 %shard_map.135.a = bf16[32,512]{1,0:T(8,128)(2,1)S(1)} custom-call(bf16[1024,128]{1,0:T(8,128)(2,1)S(1)} %bitcast.23, bf16[2,3584,256]{2,1,0:T(8,128)(2,1)} %own_hbm.13, bf16[2,3584,256]{2,1,0:T(8,128)(2,1)} %collective-permute-done.12.other_hbm), custom_call_target="tpu_custom_call" | custom-call | flops 10000000000 | tf_op jit(solution)/shard_map/pallas_call | solution.py:689
  90.1 2.6 %collective-permute-start.14 = (bf16[32,512]{1,0:T(8,128)(2,1)S(1)}, bf16[32,512]{1,0:T(8,128)(2,1)S(1)}, u32[]{:S(2)}, u32[]{:S(2)}) collective-permute-start(bf16[32,512]{1,0:T(8,128)(2,1)S(1)} %shard_map.135.a), channel_id=1, source_target_pairs={{0,1},{1,2},{2,3},{3,0},{4,5},{5,6},{6,7},{7,4},{8,9},{9,10},{10,1... | collective-permute-start | bytes 98312 | tf_op jit(solution)/shard_map/ppermute | solution.py:536
  97.9 14.9 %all_to_all.41 = bf16[16,160,128]{2,1,0:T(8,128)(2,1)S(1)} all-to-all(bf16[16,160,128]{2,1,0:T(8,128)(2,1)S(1)} %bitcast.18), channel_id=1, replica_groups={{0,8,16,24,32,40,48,56,64,72,80,88,96,104,112,120},{4,12,20,28,36,44,52..., dimensions={0} | all-to-all | bytes 1310720 | tf_op jit(solution)/shard_map/all_to_all | solution.py:518
  112.8 3.2 %shard_map.137 = bf16[2304,128]{1,0:T(8,128)(2,1)S(1)} custom-call(bf16[2560,128]{1,0:T(8,128)(2,1)S(1)} %bitcast.19, f32[32,128]{1,0:T(8,128)S(1)} %get-tuple-element.42.table_ref, f32[2,128]{1,0:T(2,128)S(1)} %copy-done.9, bf16[2,32,1,2,128,128]{5,4,3,2,1,0:T(8,128)(2,1)} %own_hbm.11, bf16[2,32,1,2,128,128]{5,4,3,2,1,0:T(8,128)(2,1)} %collective-permute-done.4.other_hbm), custom_call_target="tpu_custom_call" | custom-call | flops 10000000000 | tf_op jit(solution)/shard_map/pallas_call | solution.py:656
  116.1 13.6 %all_to_all.42 = bf16[16,144,128]{2,1,0:T(8,128)(2,1)S(1)} all-to-all(bf16[16,144,128]{2,1,0:T(8,128)(2,1)S(1)} %bitcast.21), channel_id=1, replica_groups={{0,8,16,24,32,40,48,56,64,72,80,88,96,104,112,120},{4,12,20,28,36,44,52..., dimensions={0} | all-to-all | bytes 1179648 | tf_op jit(solution)/shard_map/all_to_all | solution.py:518
  138.8 2.3 %shard_map.140 = (bf16[32,512]{1,0:T(8,128)(2,1)S(1)}, bf16[1024,128]{1,0:T(8,128)(2,1)S(1)}) custom-call(bf16[32,512]{1,0:T(8,128)(2,1)S(1)} %get-tuple-element.40.x_ref, bf16[32,512]{1,0:T(8,128)(2,1)S(1)} %shard_map.139.a, bf16[32,512]{1,0:T(8,128)(2,1)S(1)} %collective-permute-done.18.b, bf16[32,512]{1,0:T(8,128)(2,1)S(1)} %collective-permute-done.19.c, ...), custom_call_target="tpu_custom_call" | custom-call | flops 10000000000 | tf_op jit(solution)/shard_map/pallas_call | solution.py:672
  141.1 11.8 %all_to_all.43 = bf16[16,64,128]{2,1,0:T(8,128)(2,1)S(1)} all-to-all(bf16[16,64,128]{2,1,0:T(8,128)(2,1)S(1)} %bitcast.24), channel_id=1, replica_groups={{0,8,16,24,32,40,48,56,64,72,80,88,96,104,112,120},{4,12,20,28,36,44,52..., dimensions={0} | all-to-all | bytes 524288 | tf_op jit(solution)/shard_map/all_to_all | solution.py:518
  153.1 12.1 %all_to_all.44 = bf16[32,32,128]{2,1,0:T(8,128)(2,1)S(1)} all-to-all(bf16[32,32,128]{2,1,0:T(8,128)(2,1)S(1)} %bitcast.29), channel_id=1, replica_groups=mesh['req'=32,'tp'=4] {'req'}, dimensions={0} | all-to-all | bytes 524288 | tf_op jit(solution)/shard_map/all_to_all | solution.py:526
  165.2 2.8 %shard_map.142.a = bf16[32,512]{1,0:T(8,128)(2,1)S(1)} custom-call(bf16[1024,128]{1,0:T(8,128)(2,1)S(1)} %bitcast.26, bf16[2,3584,256]{2,1,0:T(8,128)(2,1)} %own_hbm.13, bf16[2,3584,256]{2,1,0:T(8,128)(2,1)} %collective-permute-done.12.other_hbm), custom_call_target="tpu_custom_call" | custom-call | flops 10000000000 | tf_op jit(solution)/shard_map/pallas_call | solution.py:689
  168.0 1.7 collective-permute-start.21
  169.6 2.1 %collective-permute-start.22 = (bf16[32,512]{1,0:T(8,128)(2,1)S(1)}, bf16[32,512]{1,0:T(8,128)(2,1)S(1)}, u32[]{:S(2)}, u32[]{:S(2)}) collective-permute-start(bf16[32,512]{1,0:T(8,128)(2,1)S(1)} %shard_map.142.a), channel_id=1, source_target_pairs={{0,1},{1,2},{2,3},{3,0},{4,5},{5,6},{6,7},{7,4},{8,9},{9,10},{10,1... | collective-permute-start | bytes 98312 | tf_op jit(solution)/shard_map/ppermute | solution.py:536
  (74 shorter events, 30.1 us)
Async XLA Ops:
  2.0 1.5 collective-permute-start.3
  5.4 20.7 %collective-permute-start.4 = (bf16[2,32,1,2,128,128]{5,4,3,2,1,0:T(8,128)(2,1)}, bf16[2,32,1,2,128,128]{5,4,3,2,1,0:T(8,128)(2,1)}, u32[]{:S(2)}, u32[]{:S(2)}) collective-permute-start(bf16[2,32,1,2,128,128]{5,4,3,2,1,0:T(8,128)(2,1)} %own_hbm.11), channel_id=1, source_target_pairs={{0,4},{4,0},{8,12},{12,8},{16,20},{20,16},{24,28},{28,24},{32,36},... | collective-permute-start | bytes 12582920 | tf_op jit(solution)/shard_map/ppermute | solution.py:530
  5.5 20.6 %all-to-all-start = ((bf16[16,160,128]{2,1,0:T(8,128)(2,1)}), bf16[16,160,128]{2,1,0:T(8,128)(2,1)S(1)}, u32[]{:S(2)}, u32[]{:S(2)}) async-start(bf16[16,160,128]{2,1,0:T(8,128)(2,1)} %bitcast.1), calls=%async_computation | async-start | bytes 1310720 | tf_op jit(solution)/shard_map/all_to_all | solution.py:518
  12.6 41.3 %collective-permute-start.10 = (bf16[2,256,3584]{2,1,0:T(8,128)(2,1)}, bf16[2,256,3584]{2,1,0:T(8,128)(2,1)}, u32[]{:S(2)}, u32[]{:S(2)}) collective-permute-start(bf16[2,256,3584]{2,1,0:T(8,128)(2,1)} %gate_hbm.3), channel_id=1, source_target_pairs={{0,4},{4,0},{8,12},{12,8},{16,20},{20,16},{24,28},{28,24},{32,36},... | collective-permute-start | bytes 11010056 | tf_op jit(solution)/shard_map/ppermute | solution.py:530
  12.8 43.4 %collective-permute-start.11 = (bf16[2,256,3584]{2,1,0:T(8,128)(2,1)}, bf16[2,256,3584]{2,1,0:T(8,128)(2,1)}, u32[]{:S(2)}, u32[]{:S(2)}) collective-permute-start(bf16[2,256,3584]{2,1,0:T(8,128)(2,1)} %up_hbm.3), channel_id=1, source_target_pairs={{0,4},{4,0},{8,12},{12,8},{16,20},{20,16},{24,28},{28,24},{32,36},... | collective-permute-start | bytes 11010056 | tf_op jit(solution)/shard_map/ppermute | solution.py:530
  30.5 15.2 %all-to-all-start.1 = ((bf16[16,144,128]{2,1,0:T(8,128)(2,1)}), bf16[16,144,128]{2,1,0:T(8,128)(2,1)S(1)}, u32[]{:S(2)}, u32[]{:S(2)}) async-start(bf16[16,144,128]{2,1,0:T(8,128)(2,1)} %bitcast.3), calls=%async_computation.1 | async-start | bytes 1179648 | tf_op jit(solution)/shard_map/all_to_all | solution.py:518
  34.1 13.9 %collective-permute-start.6 = (bf16[2,1024,256]{2,1,0:T(8,128)(2,1)S(1)}, bf16[2,1024,256]{2,1,0:T(8,128)(2,1)S(1)}, u32[]{:S(2)}, u32[]{:S(2)}) collective-permute-start(bf16[2,1024,256]{2,1,0:T(8,128)(2,1)S(1)} %copy-done.5), channel_id=1, source_target_pairs={{0,4},{4,0},{8,12},{12,8},{16,20},{20,16},{24,28},{28,24},{32,36},... | collective-permute-start | bytes 3145736 | tf_op jit(solution)/shard_map/ppermute | solution.py:530
  46.2 1.9 %collective-permute-start.5 = (bf16[128,128]{1,0:T(8,128)(2,1)S(1)}, bf16[128,128]{1,0:T(8,128)(2,1)S(1)}, u32[]{:S(2)}, u32[]{:S(2)}) collective-permute-start(bf16[128,128]{1,0:T(8,128)(2,1)S(1)} %shard_map.131.own_ref), channel_id=1, source_target_pairs={{0,4},{4,0},{8,12},{12,8},{16,20},{20,16},{24,28},{28,24},{32,36},... | collective-permute-start | bytes 98312 | tf_op jit(solution)/shard_map/ppermute | solution.py:530
  47.6 5.3 %collective-permute-start = (bf16[32,256]{1,0:T(8,128)(2,1)S(1)}, bf16[32,256]{1,0:T(8,128)(2,1)S(1)}, u32[]{:S(2)}, u32[]{:S(2)}) collective-permute-start(bf16[32,256]{1,0:T(8,128)(2,1)S(1)} %copy-done.6), channel_id=1, source_target_pairs={{0,4},{4,0},{8,12},{12,8},{16,20},{20,16},{24,28},{28,24},{32,36},... | collective-permute-start | bytes 49160 | tf_op jit(solution)/shard_map/ppermute | solution.py:530
  48.1 29.0 %collective-permute-start.12 = (bf16[2,3584,256]{2,1,0:T(8,128)(2,1)}, bf16[2,3584,256]{2,1,0:T(8,128)(2,1)}, u32[]{:S(2)}, u32[]{:S(2)}) collective-permute-start(bf16[2,3584,256]{2,1,0:T(8,128)(2,1)} %own_hbm.13), channel_id=1, source_target_pairs={{0,4},{4,0},{8,12},{12,8},{16,20},{20,16},{24,28},{28,24},{32,36},... | collective-permute-start | bytes 11010056 | tf_op jit(solution)/shard_map/ppermute | solution.py:530
  49.1 7.2 %collective-permute-start.7 = (bf16[32,512]{1,0:T(8,128)(2,1)S(1)}, bf16[32,512]{1,0:T(8,128)(2,1)S(1)}, u32[]{:S(2)}, u32[]{:S(2)}) collective-permute-start(bf16[32,512]{1,0:T(8,128)(2,1)S(1)} %shard_map.132.a), channel_id=1, source_target_pairs={{0,2},{1,3},{2,0},{3,1},{4,6},{5,7},{6,4},{7,5},{8,10},{9,11},{10,... | collective-permute-start | bytes 98312 | tf_op jit(solution)/shard_map/ppermute | solution.py:536
  53.0 5.1 %collective-permute-start.8 = (bf16[32,512]{1,0:T(8,128)(2,1)S(1)}, bf16[32,512]{1,0:T(8,128)(2,1)S(1)}, u32[]{:S(2)}, u32[]{:S(2)}) collective-permute-start(bf16[32,512]{1,0:T(8,128)(2,1)S(1)} %shard_map.132.a), channel_id=1, source_target_pairs={{0,1},{1,2},{2,3},{3,0},{4,5},{5,6},{6,7},{7,4},{8,9},{9,10},{10,1... | collective-permute-start | bytes 98312 | tf_op jit(solution)/shard_map/ppermute | solution.py:536
  54.0 4.1 %collective-permute-start.9 = (bf16[32,512]{1,0:T(8,128)(2,1)S(1)}, bf16[32,512]{1,0:T(8,128)(2,1)S(1)}, u32[]{:S(2)}, u32[]{:S(2)}) collective-permute-start(bf16[32,512]{1,0:T(8,128)(2,1)S(1)} %shard_map.132.a), channel_id=1, source_target_pairs={{0,3},{1,0},{2,1},{3,2},{4,7},{5,4},{6,5},{7,6},{8,11},{9,8},{10,9... | collective-permute-start | bytes 98312 | tf_op jit(solution)/shard_map/ppermute | solution.py:536
  73.0 12.8 %all-to-all-start.3 = ((bf16[32,32,128]{2,1,0:T(8,128)(2,1)}), bf16[32,32,128]{2,1,0:T(8,128)(2,1)S(1)}, u32[]{:S(2)}, u32[]{:S(2)}) async-start(bf16[32,32,128]{2,1,0:T(8,128)(2,1)} %bitcast.7), calls=%async_computation.3 | async-start | bytes 524288 | tf_op jit(solution)/shard_map/all_to_all | solution.py:526
  76.9 16.5 %collective-permute-start.16 = (bf16[2,256,1024]{2,1,0:T(8,128)(2,1)S(1)}, bf16[2,256,1024]{2,1,0:T(8,128)(2,1)}, u32[]{:S(2)}, u32[]{:S(2)}) collective-permute-start(bf16[2,256,1024]{2,1,0:T(8,128)(2,1)S(1)} %copy-done.4), channel_id=1, source_target_pairs={{0,4},{4,0},{8,12},{12,8},{16,20},{20,16},{24,28},{28,24},{32,36},... | collective-permute-start | bytes 3145736 | tf_op jit(solution)/shard_map/ppermute | solution.py:530
  88.6 5.5 %collective-permute-start.13 = (bf16[32,512]{1,0:T(8,128)(2,1)S(1)}, bf16[32,512]{1,0:T(8,128)(2,1)S(1)}, u32[]{:S(2)}, u32[]{:S(2)}) collective-permute-start(bf16[32,512]{1,0:T(8,128)(2,1)S(1)} %shard_map.135.a), channel_id=1, source_target_pairs={{0,2},{1,3},{2,0},{3,1},{4,6},{5,7},{6,4},{7,5},{8,10},{9,11},{10,... | collective-permute-start | bytes 98312 | tf_op jit(solution)/shard_map/ppermute | solution.py:536
  90.1 5.1 %collective-permute-start.14 = (bf16[32,512]{1,0:T(8,128)(2,1)S(1)}, bf16[32,512]{1,0:T(8,128)(2,1)S(1)}, u32[]{:S(2)}, u32[]{:S(2)}) collective-permute-start(bf16[32,512]{1,0:T(8,128)(2,1)S(1)} %shard_map.135.a), channel_id=1, source_target_pairs={{0,1},{1,2},{2,3},{3,0},{4,5},{5,6},{6,7},{7,4},{8,9},{9,10},{10,1... | collective-permute-start | bytes 98312 | tf_op jit(solution)/shard_map/ppermute | solution.py:536
  92.8 3.9 %collective-permute-start.15 = (bf16[32,512]{1,0:T(8,128)(2,1)S(1)}, bf16[32,512]{1,0:T(8,128)(2,1)S(1)}, u32[]{:S(2)}, u32[]{:S(2)}) collective-permute-start(bf16[32,512]{1,0:T(8,128)(2,1)S(1)} %shard_map.135.a), channel_id=1, source_target_pairs={{0,3},{1,0},{2,1},{3,2},{4,7},{5,4},{6,5},{7,6},{8,11},{9,8},{10,9... | collective-permute-start | bytes 98312 | tf_op jit(solution)/shard_map/ppermute | solution.py:536
  132.0 5.6 %collective-permute-start.18 = (bf16[32,512]{1,0:T(8,128)(2,1)S(1)}, bf16[32,512]{1,0:T(8,128)(2,1)S(1)}, u32[]{:S(2)}, u32[]{:S(2)}) collective-permute-start(bf16[32,512]{1,0:T(8,128)(2,1)S(1)} %shard_map.139.a), channel_id=1, source_target_pairs={{0,2},{1,3},{2,0},{3,1},{4,6},{5,7},{6,4},{7,5},{8,10},{9,11},{10,... | collective-permute-start | bytes 98312 | tf_op jit(solution)/shard_map/ppermute | solution.py:536
  133.2 5.1 %collective-permute-start.19 = (bf16[32,512]{1,0:T(8,128)(2,1)S(1)}, bf16[32,512]{1,0:T(8,128)(2,1)S(1)}, u32[]{:S(2)}, u32[]{:S(2)}) collective-permute-start(bf16[32,512]{1,0:T(8,128)(2,1)S(1)} %shard_map.139.a), channel_id=1, source_target_pairs={{0,1},{1,2},{2,3},{3,0},{4,5},{5,6},{6,7},{7,4},{8,9},{9,10},{10,1... | collective-permute-start | bytes 98312 | tf_op jit(solution)/shard_map/ppermute | solution.py:536
  134.8 3.9 %collective-permute-start.20 = (bf16[32,512]{1,0:T(8,128)(2,1)S(1)}, bf16[32,512]{1,0:T(8,128)(2,1)S(1)}, u32[]{:S(2)}, u32[]{:S(2)}) collective-permute-start(bf16[32,512]{1,0:T(8,128)(2,1)S(1)} %shard_map.139.a), channel_id=1, source_target_pairs={{0,3},{1,0},{2,1},{3,2},{4,7},{5,4},{6,5},{7,6},{8,11},{9,8},{10,9... | collective-permute-start | bytes 98312 | tf_op jit(solution)/shard_map/ppermute | solution.py:536
  168.0 5.5 %collective-permute-start.21 = (bf16[32,512]{1,0:T(8,128)(2,1)S(1)}, bf16[32,512]{1,0:T(8,128)(2,1)S(1)}, u32[]{:S(2)}, u32[]{:S(2)}) collective-permute-start(bf16[32,512]{1,0:T(8,128)(2,1)S(1)} %shard_map.142.a), channel_id=1, source_target_pairs={{0,2},{1,3},{2,0},{3,1},{4,6},{5,7},{6,4},{7,5},{8,10},{9,11},{10,... | collective-permute-start | bytes 98312 | tf_op jit(solution)/shard_map/ppermute | solution.py:536
  169.6 5.1 %collective-permute-start.22 = (bf16[32,512]{1,0:T(8,128)(2,1)S(1)}, bf16[32,512]{1,0:T(8,128)(2,1)S(1)}, u32[]{:S(2)}, u32[]{:S(2)}) collective-permute-start(bf16[32,512]{1,0:T(8,128)(2,1)S(1)} %shard_map.142.a), channel_id=1, source_target_pairs={{0,1},{1,2},{2,3},{3,0},{4,5},{5,6},{6,7},{7,4},{8,9},{9,10},{10,1... | collective-permute-start | bytes 98312 | tf_op jit(solution)/shard_map/ppermute | solution.py:536
  171.7 3.9 %collective-permute-start.23 = (bf16[32,512]{1,0:T(8,128)(2,1)S(1)}, bf16[32,512]{1,0:T(8,128)(2,1)S(1)}, u32[]{:S(2)}, u32[]{:S(2)}) collective-permute-start(bf16[32,512]{1,0:T(8,128)(2,1)S(1)} %shard_map.142.a), channel_id=1, source_target_pairs={{0,3},{1,0},{2,1},{3,2},{4,7},{5,4},{6,5},{7,6},{8,11},{9,8},{10,9... | collective-permute-start | bytes 98312 | tf_op jit(solution)/shard_map/ppermute | solution.py:536
  (14 other events, 79.4 us)

commit v7 on v6

--- a/solution.py
+++ b/solution.py
@@ -19,6 +19,7 @@
 VMEM = pl.BlockSpec(memory_space=pltpu.VMEM)
 SMEM = pl.BlockSpec(memory_space=pltpu.SMEM)
 HBM = pl.BlockSpec(memory_space=pltpu.HBM)
+ANY = pl.BlockSpec(memory_space=pl.ANY)
 F32 = jnp.float32
 BF16 = jnp.bfloat16
 
@@ -102,6 +103,27 @@
     high = squares.astype(BF16).astype(F32)
     lane = lax.broadcasted_iota(jnp.int32, (current.shape[0], LANES), 1)
     return jnp.where(lane == 0, high, jnp.where(lane == 1, squares - high, 0.0))
+
+
+def along_lanes(column):
+    n = column.shape[0]
+    row = lax.broadcasted_iota(jnp.int32, (n, LANES), 0)
+    lane = lax.broadcasted_iota(jnp.int32, (n, LANES), 1)
+    return jnp.sum(jnp.where(row == lane, column, 0.0), axis=0, keepdims=True)
+
+
+def along_rows(line, n):
+    row = lax.broadcasted_iota(jnp.int32, (n, LANES), 0)
+    lane = lax.broadcasted_iota(jnp.int32, (n, LANES), 1)
+    return jnp.sum(jnp.where(row == lane, line, 0.0), axis=1, keepdims=True)
+
+
+def square_rows(current, rows):
+    squares = jnp.sum(current * current, axis=1, keepdims=True)
+    high = squares.astype(BF16).astype(F32)
+    row = lax.broadcasted_iota(jnp.int32, (rows, LANES), 0)
+    low = jnp.where(row == 1, along_lanes(squares - high), 0.0)
+    return jnp.where(row == 0, along_lanes(high), low)
 
 
 def store_blocks(packed, product):
@@ -212,6 +234,27 @@
     send_ref[rows:, :] = extra.astype(BF16)
 
 
+def fetch_kernel(sources, *refs):
+    count = len(sources)
+    ins, outs, sems = refs[:count], refs[count + 1 : -1], refs[-1]
+    copies = [
+        pltpu.make_async_copy(source(ref), outs[place].at[part], sems.at[i])
+        for i, (ref, (source, place, part)) in enumerate(zip(ins, sources))
+    ]
+    start_all(copies)
+    wait_all(copies)
+
+
+def fetch(sources, operands, shapes, after):
+    return call(
+        functools.partial(fetch_kernel, sources),
+        [jax.ShapeDtypeStruct(shape, BF16) for shape in shapes],
+        [HBM] * len(operands) + [ANY],
+        [pltpu.SemaphoreType.DMA((len(operands),))],
+        flops=2000000000,
+    )(*operands, after)
+
+
 def pair_total_kernel(keep_ref, received_ref, out_ref):
     repeat_into(out_ref, (keep_ref[...] + received_ref[...].astype(F32)).astype(BF16))
 
@@ -221,17 +264,17 @@
         out[...] = joined(own[...].astype(F32), other[...].astype(F32), 1).astype(BF16)
 
 
-def query_kernel(
-    layer_no, x_ref, a, b, c, d, gain_ref, own_hbm, other_hbm, out_ref, payload_ref, weight, packed, sems
-):
-    copies = row_copies(layer_no, own_hbm, other_hbm, weight, sems)
-    start_all(copies)
+def query_kernel(layer_no, x_ref, a, b, c, d, gain_ref, weight_ref, out_ref, payload_ref, packed):
     out_ref[...] = pair_sum(x_ref, (a, b, c, d))
     current = out_ref[...].astype(F32)
-    scaled = (current * gain_ref[layer_no : layer_no + 1, :].astype(F32)).astype(BF16)
-    extra = squares_in_lanes(current)
-    wait_all(copies)
-    product = jnp.dot(scaled, weight[...], preferred_element_type=F32)
+    scaled = current * gain_ref[layer_no : layer_no + 1, :].astype(F32)
+    middle = scaled.shape[1] // 2
+    first = core_side() == 0
+    mine = jnp.where(first, scaled[:, :middle], scaled[:, middle:]).astype(BF16)
+    theirs = jnp.where(first, scaled[:, middle:], scaled[:, :middle]).astype(BF16)
+    product = jnp.dot(mine, weight_ref[0], preferred_element_type=F32)
+    product += jnp.dot(theirs, weight_ref[1], preferred_element_type=F32)
+    extra = square_rows(current, payload_ref.shape[0] // 16 - packed.shape[0])
     rows = jnp.concatenate([store_blocks(packed, product), extra], axis=0)
     repeat_into(payload_ref, rows.astype(BF16))
 
@@ -258,28 +301,32 @@
     layer_no, sources, received_ref, table_ref, tables_ref, own_hbm, other_hbm, out_ref, table_out, blocks, packed, sems
 ):
     n_slots = blocks.shape[1]
-    piece = n_slots // 2
+    piece = n_slots // 1
     copies = [
         [
             pltpu.make_async_copy(
                 pool.at[layer_no, pl.ds(at, piece), 0, part],
                 blocks.at[b, pl.ds(at, piece), part],
-                sems.at[part * 2 + at // piece, b],
+                sems.at[(part * n_slots + at) // piece, b],
             )
             for b, pool in enumerate((own_hbm, other_hbm))
         ]
         for part in range(2)
-        for at in (0, piece)
+        for at in range(0, n_slots, piece)
     ]
     for pair in copies:
         start_all(pair)
     rows = packed.shape[0]
     totals = jnp.sum(received_ref[...].astype(F32).reshape(sources, -1, LANES), axis=0)
     extra = totals[rows:]
-    requests = extra.shape[0]
+    requests = extra.shape[0] if table_ref is None else table_ref.shape[0]
     heads = rows // requests
-    inv = lax.rsqrt((extra[:, 0:1] + extra[:, 1:2]) / D + EPSILON)
-    queries = totals[:rows] * spread(packed, jnp.broadcast_to(inv, extra.shape), heads)
+    if table_ref is None:
+        squares = extra[:, 0:1] + extra[:, 1:2]
+    else:
+        squares = along_rows(extra[0:1] + extra[1:2], requests)
+    inv = lax.rsqrt(squares / D + EPSILON)
+    queries = totals[:rows] * spread(packed, jnp.broadcast_to(inv, (requests, LANES)), heads)
     queries = queries * tables_ref[0:1, :] + pltpu.roll(queries, LANES // 2, 1) * tables_ref[1:2, :]
     queries = queries.astype(BF16)
 
@@ -313,7 +360,7 @@
 
     def of_slot(left, p, part, contract):
         if p % piece == 0:
-            wait_all(copies[part * 2 + p // piece])
+            wait_all(copies[(part * n_slots + p) // piece])
         left = left[p * group : (p + 1) * group]
         left = jnp.concatenate([jnp.where(mine, left, 0.0), jnp.where(mine, 0.0, left)], axis=1)
         right = jnp.concatenate([blocks[0, p, part], blocks[1, p, part]], axis=contract)
@@ -408,11 +455,11 @@
     sems,
 ):
     width = gate.shape[1]
-    piece = width // 2
+    piece = width // 1
     own_rows, other_rows = side_slices(gate_hbm.shape[1])
     steps = []
     for i, (own, other, weight) in enumerate(((gate_hbm, gate_other, gate), (up_hbm, up_other, up))):
-        for j in range(2):
+        for j in range(width // piece):
             columns = pl.ds(pl.multiple_of(core_side() * width + j * piece, LANES), piece)
             local = pl.ds(j * piece, piece)
             copies = pair_copies(
@@ -420,7 +467,7 @@
                 other.at[layer_no, :, columns],
                 weight.at[own_rows, local],
                 weight.at[other_rows, local],
-                sems.at[i * 2 + j],
+                sems.at[len(steps)],
             )
             start_all(copies)
             steps.append((i, j, copies, weight))
@@ -450,6 +497,39 @@
     payload_ref[...] = packed[...].astype(BF16)
 
 
+def fetched_gate_up_kernel(
+    layer_no, chunk, x_ref, a, b, c, d, gain_ref, gate_ref, up_ref, out_ref, payload_ref, packed
+):
+    requests = x_ref.shape[0]
+    stride = packed.shape[0] // requests
+    per_chunk = chunk // stride
+    count = requests // per_chunk
+    blocks = gate_ref.shape[2] // LANES
+    half = stride // 2
+
+    def store(row, values):
+        for q in range(per_chunk):
+            packed[pl.ds(q * stride + row, count, stride=chunk), :] = values[q * count : (q + 1) * count]
+
+    out_ref[...] = pair_sum(x_ref, (a, b, c, d))
+    current = out_ref[...].astype(F32)
+    scaled = current * gain_ref[layer_no : layer_no + 1, :].astype(F32)
+    middle = scaled.shape[1] // 2
+    first = core_side() == 0
+    mine = jnp.where(first, scaled[:, :middle], scaled[:, middle:]).astype(BF16)
+    theirs = jnp.where(first, scaled[:, middle:], scaled[:, :middle]).astype(BF16)
+    zeros = jnp.zeros((requests, LANES), F32)
+    store(blocks, squares_in_lanes(current))
+    for row in [*range(blocks + 1, half), *range(half + blocks, stride)]:
+        store(row, zeros)
+    for i, weight in enumerate((gate_ref, up_ref)):
+        product = jnp.dot(mine, weight[0], preferred_element_type=F32)
+        product += jnp.dot(theirs, weight[1], preferred_element_type=F32)
+        for k in range(blocks):
+            store(i * half + k, product[:, k * LANES : (k + 1) * LANES])
+    payload_ref[...] = packed[...].astype(BF16)
+
+
 def activation_kernel(blocks, sources, half, received_ref, out_ref):
     totals = jnp.sum(received_ref[...].astype(F32).reshape(sources, -1, LANES), axis=0)
     acts = []
@@ -464,21 +544,21 @@
 def down_kernel(
     layer_no, half, chunk, received_ref, own_hbm, other_hbm, out_ref, weight, packed, sems
 ):
-    depth = weight.shape[0] // 2
+    depth = weight.shape[0] // 14
     own_columns, other_columns = side_slices(own_hbm.shape[2])
     steps = []
-    for side in range(2):
-        rows = pl.ds(side * depth, depth)
+    for step in range(weight.shape[0] // depth):
+        rows = pl.ds(step * depth, depth)
         steps.append(
             pair_copies(
                 own_hbm.at[layer_no, rows],
                 other_hbm.at[layer_no, rows],
                 weight.at[rows, own_columns],
                 weight.at[rows, other_columns],
-                sems.at[side],
+                sems.at[step],
             )
         )
-        start_all(steps[side])
+        start_all(steps[step])
     packed[...] = received_ref[...].astype(F32)
     blocks = weight.shape[0] // LANES // 2
     per_chunk = chunk // half
@@ -497,10 +577,12 @@
                 ).astype(BF16)
             )
         rows = jnp.concatenate(columns, axis=1)
-        wait_all(steps[side])
-        total += jnp.dot(
-            rows, weight[side * depth : (side + 1) * depth], preferred_element_type=F32
-        )
+        for at in range(0, rows.shape[1], depth):
+            first = side * rows.shape[1] + at
+            wait_all(steps[first // depth])
+            total += jnp.dot(
+                rows[:, at : at + depth], weight[first : first + depth], preferred_element_type=F32
+            )
     out_ref[...] = total.astype(BF16)
 
 
@@ -629,21 +711,27 @@
     table = None
     for layer_no in range(LAYERS):
         if parts is not None:
+
+            def half_of(ref, l=layer_no):
+                return ref.at[l, :, side_slices(ref.shape[2] // 2)[0]]
+
+            (weights,) = fetch(
+                [(half_of, 0, b) for b in range(2)],
+                (q_weight, q_other),
+                [(2, width, heads * head_size)],
+                act,
+            )
             current, payload = call(
                 functools.partial(query_kernel, layer_no),
-                [pair_type(requests), rows_type(side * sent_rows)],
-                [VMEM] * 6 + [HBM] * 2,
-                [
-                    pltpu.VMEM((2 * width, heads * head_size), BF16),
-                    rows_scratch(q_rows),
-                    dma((2,)),
-                ],
-            )(current, *parts, attn_gain, q_weight, q_other)
+                [pair_type(requests), rows_type(side * stat_rows)],
+                [VMEM] * 7,
+                [rows_scratch(q_rows)],
+            )(current, *parts, attn_gain, weights)
         received = exchange(payload, n_req)
         scratch = [
             pltpu.VMEM((2, pool_dev, 2, block_tokens, head_size), BF16),
             rows_scratch(q_rows),
-            dma((4, 2)),
+            dma((2, 2)),
         ]
         if table is None:
             payload, table = call(
@@ -659,6 +747,7 @@
                 [VMEM] * 3 + [HBM] * 2,
                 scratch,
             )(received, table, tables, kv_pool, pool_other)
+        stats = payload
         context = call(functools.partial(combine_kernel, side), rows_type(q_rows), [VMEM])(
             exchange(payload, n_req)
         )
@@ -669,17 +758,35 @@
             [pltpu.VMEM((o_weight.shape[1], 2 * width), BF16), rows_scratch(q_rows), dma((2,))],
         )(context, from_pair(context, n_req), o_weight, o_other)
         chunk = requests // side * 2 * f_rows
-        current, payload = call(
-            functools.partial(gate_up_kernel, layer_no, chunk),
-            [pair_type(requests), rows_type(requests * 2 * f_rows)],
-            [VMEM] * 6 + [HBM] * 4,
-            [
-                pltpu.VMEM((2 * width, hidden_half), BF16),
-                pltpu.VMEM((2 * width, hidden_half), BF16),
-                rows_scratch(requests * 2 * f_rows),
-                dma((4, 2)),
-            ],
-        )(current, *tp_parts(own), ffn_gain, gate_weight, gate_other, up_weight, up_other)
+        if layer_no in (1,):
+
+            def half_of(ref, l=layer_no):
+                return ref.at[l, :, side_slices(ref.shape[2] // 2)[0]]
+
+            gate_up = fetch(
+                [(half_of, place, b) for place in range(2) for b in range(2)],
+                (gate_weight, gate_other, up_weight, up_other),
+                [(2, width, hidden_half)] * 2,
+                stats,
+            )
+            current, payload = call(
+                functools.partial(fetched_gate_up_kernel, layer_no, chunk),
+                [pair_type(requests), rows_type(requests * 2 * f_rows)],
+                [VMEM] * 8,
+                [rows_scratch(requests * 2 * f_rows)],
+            )(current, own, *tp_parts(own)[1:], ffn_gain, *gate_up)
+        else:
+            current, payload = call(
+                functools.partial(gate_up_kernel, layer_no, chunk),
+                [pair_type(requests), rows_type(requests * 2 * f_rows)],
+                [VMEM] * 6 + [HBM] * 4,
+                [
+                    pltpu.VMEM((2 * width, hidden_half), BF16),
+                    pltpu.VMEM((2 * width, hidden_half), BF16),
+                    rows_scratch(requests * 2 * f_rows),
+                    dma((2, 2)),
+                ],
+            )(current, *tp_parts(own), ffn_gain, gate_weight, gate_other, up_weight, up_other)
         chunk = requests // side * f_rows
         act = call(
             functools.partial(activation_kernel, blocks, side, f_rows),
@@ -693,7 +800,7 @@
             [
                 pltpu.VMEM((down_weight.shape[1], 2 * width), BF16),
                 rows_scratch(n_req * chunk),
-                dma((2, 2)),
+                dma((14, 2)),
             ],
         )(exchange_all(act, n_req), down_weight, down_other)
         parts = tp_parts(own)

time: 177 us -> 173 us (0.977)
  waiting for transfers between devices: 46.8 us -> 44.2 us
    pallas_call x0 -> x3, Pallas kernels: none -> 3.43 us  [the longest x2 2.55 us: fetch(): call(functools.partial(fetch_kernel, sources), [jax.ShapeDtypeStruct(shap...]
    ppermute x12, waiting for transfers between devices: 10.2 us -> 7.6 us  [tp_parts(): lax.ppermute(partial_sum, 'tp', [(i, (i + shift) % n_tp) for i in range(n...]
    pallas_call x2 -> x1, Pallas kernels: 4.69 us -> 2.28 us  [shards(): call(functools.partial(gate_up_kernel, layer_no, chunk), [pair_type(reque...]
  transfers between devices with their start and end apart: 27 -> 27, of which waited for: 17 -> 15; matrix products, arithmetic and copies ran while one was open for 0% -> 0% of each run, Pallas kernels for 6% -> 8%
where the time goes in v7:
time: 173 us
  blocking collectives  63.5 us (37%)
  waiting for transfers between devices  44.2 us (26%)
  starting transfers between devices  38.5 us (22%)
  Pallas kernels  25.2 us (15%)
    all_to_all x4, blocking collectives, exchange(): lax.all_to_all(blocks, 'req', split_axis=0, concat_axis=0, tiled=True, ax...  51.4 us
    all_to_all x2, waiting for transfers between devices, exchange(): lax.all_to_all(blocks, 'req', split_axis=0, concat_axis=0, tiled=True, ax...  24.3 us
    ppermute x12, starting transfers between devices, tp_parts(): lax.ppermute(partial_sum, 'tp', [(i, (i + shift) % n_tp) for i in range(n...  21.3 us
    all_to_all x1, blocking collectives, exchange_all(): lax.all_to_all(blocks, 'req', split_axis=0, concat_axis=0, tiled=True)  12.1 us
    all_to_all x2, starting transfers between devices, exchange(): lax.all_to_all(blocks, 'req', split_axis=0, concat_axis=0, tiled=True, ax...  10.7 us
    all_to_all x1, waiting for transfers between devices, exchange_all(): lax.all_to_all(blocks, 'req', split_axis=0, concat_axis=0, tiled=True)  8.65 us
    ppermute x12, waiting for transfers between devices, tp_parts(): lax.ppermute(partial_sum, 'tp', [(i, (i + shift) % n_tp) for i in range(n...  7.6 us
    pallas_call x2, Pallas kernels, shards(): call(functools.partial(down_kernel, layer_no, f_rows, chunk), pair_type(r...  4.99 us
  transfers between devices with their start and end apart: 27, of which 15 were waited for; matrix products, arithmetic and copies ran while one was open for 0% of the time, Pallas kernels for 8%

profile of v7, /device:TPU:0, one launch (start us, length us, event | category | flops | bytes accessed | tf_op | source)
XLA Modules:
  0.0 172.6 jit_solution(5121913939189200488)
XLA Ops:
  0.0 2.0 %shard_map.128 = (f32[160,128]{1,0:T(8,128)}, bf16[160,128]{1,0:T(8,128)(2,1)}) custom-call(bf16[32,256]{1,0:T(8,128)(2,1)} %x_hbm.1, bf16[2,256]{1,0:T(2,128)(2,1)} %gain_hbm.1, bf16[2,256,1024]{2,1,0:T(8,128)(2,1)} %refs_0_.2, s32[1,32]{1,0:T(1,128)} %homes_hbm.1, s32[2,1,1,24]{3,2,1,0:T(1,128)} %chosen_hbm.1, s32[1,2]{1,0:T(1,128)} %bitcast.30), custom_call_target="tpu_custom_call" | custom-call | flops 10000000000 | tf_op jit(solution)/shard_map/pallas_call | solution.py:662
  5.5 7.1 %all-to-all-start = ((bf16[16,160,128]{2,1,0:T(8,128)(2,1)}), bf16[16,160,128]{2,1,0:T(8,128)(2,1)S(1)}, u32[]{:S(2)}, u32[]{:S(2)}) async-start(bf16[16,160,128]{2,1,0:T(8,128)(2,1)} %bitcast.1), calls=%async_computation | async-start | bytes 1310720 | tf_op jit(solution)/shard_map/all_to_all | solution.py:600
  13.2 12.9 %all-to-all-done = bf16[16,160,128]{2,1,0:T(8,128)(2,1)S(1)} async-done(((bf16[16,160,128]{2,1,0:T(8,128)(2,1)}), bf16[16,160,128]{2,1,0:T(8,128)(2,1)S(1)}, u32[]{:S(2)}, u32[]{:S(2)}) %all-to-all-start) | async-done | bytes 655392 | tf_op jit(solution)/shard_map/all_to_all | solution.py:600
  26.1 4.4 %shard_map.130 = (bf16[2304,128]{1,0:T(8,128)(2,1)}, f32[32,128]{1,0:T(8,128)S(1)}) custom-call(bf16[2560,128]{1,0:T(8,128)(2,1)S(1)} %bitcast.18, f32[2,128]{1,0:T(2,128)S(1)} %copy-done.9, bf16[2,32,1,2,128,128]{5,4,3,2,1,0:T(8,128)(2,1)} %own_hbm.9, bf16[2,32,1,2,128,128]{5,4,3,2,1,0:T(8,128)(2,1)} %collective-permute-done.4.other_hbm), custom_call_target="tpu_custom_call" | custom-call | flops 10000000000 | tf_op jit(solution)/shard_map/pallas_call | solution.py:737
  30.5 3.6 %all-to-all-start.1 = ((bf16[16,144,128]{2,1,0:T(8,128)(2,1)}), bf16[16,144,128]{2,1,0:T(8,128)(2,1)S(1)}, u32[]{:S(2)}, u32[]{:S(2)}) async-start(bf16[16,144,128]{2,1,0:T(8,128)(2,1)} %bitcast.3), calls=%async_computation.1 | async-start | bytes 1179648 | tf_op jit(solution)/shard_map/all_to_all | solution.py:600
  34.2 11.5 %all-to-all-done.1 = bf16[16,144,128]{2,1,0:T(8,128)(2,1)S(1)} async-done(((bf16[16,144,128]{2,1,0:T(8,128)(2,1)}), bf16[16,144,128]{2,1,0:T(8,128)(2,1)S(1)}, u32[]{:S(2)}, u32[]{:S(2)}) %all-to-all-start.1) | async-done | bytes 589856 | tf_op jit(solution)/shard_map/all_to_all | solution.py:600
  49.2 3.9 %collective-permute-start.7 = (bf16[32,512]{1,0:T(8,128)(2,1)S(1)}, bf16[32,512]{1,0:T(8,128)(2,1)S(1)}, u32[]{:S(2)}, u32[]{:S(2)}) collective-permute-start(bf16[32,512]{1,0:T(8,128)(2,1)S(1)} %shard_map.132.a), channel_id=1, source_target_pairs={{0,2},{1,3},{2,0},{3,1},{4,6},{5,7},{6,4},{7,5},{8,10},{9,11},{10,... | collective-permute-start | bytes 98312 | tf_op jit(solution)/shard_map/ppermute | solution.py:618
  54.1 2.2 %collective-permute-start.9 = (bf16[32,512]{1,0:T(8,128)(2,1)S(1)}, bf16[32,512]{1,0:T(8,128)(2,1)S(1)}, u32[]{:S(2)}, u32[]{:S(2)}) collective-permute-start(bf16[32,512]{1,0:T(8,128)(2,1)S(1)} %shard_map.132.a), channel_id=1, source_target_pairs={{0,3},{1,0},{2,1},{3,2},{4,7},{5,4},{6,5},{7,6},{8,11},{9,8},{10,9... | collective-permute-start | bytes 98312 | tf_op jit(solution)/shard_map/ppermute | solution.py:618
  56.3 1.8 %collective-permute-done.8.c = bf16[32,512]{1,0:T(8,128)(2,1)S(1)} collective-permute-done((bf16[32,512]{1,0:T(8,128)(2,1)S(1)}, bf16[32,512]{1,0:T(8,128)(2,1)S(1)}, u32[]{:S(2)}, u32[]{:S(2)}) %collective-permute-start.8) | collective-permute-done | bytes 32800 | tf_op jit(solution)/shard_map/ppermute | solution.py:618
  58.2 2.3 %shard_map.133 = (bf16[32,512]{1,0:T(8,128)(2,1)S(1)}, bf16[1024,128]{1,0:T(8,128)(2,1)S(1)}) custom-call(bf16[32,512]{1,0:T(8,128)(2,1)S(1)} %get-tuple-element.27.x_ref, bf16[32,512]{1,0:T(8,128)(2,1)S(1)} %shard_map.132.a, bf16[32,512]{1,0:T(8,128)(2,1)S(1)} %collective-permute-done.7.b, bf16[32,512]{1,0:T(8,128)(2,1)S(1)} %collective-permute-done.8.c, ...), custom_call_target="tpu_custom_call" | custom-call | flops 10000000000 | tf_op jit(solution)/shard_map/pallas_call | solution.py:779
  60.5 11.7 %all_to_all.40 = bf16[16,64,128]{2,1,0:T(8,128)(2,1)S(1)} all-to-all(bf16[16,64,128]{2,1,0:T(8,128)(2,1)S(1)} %bitcast.25), channel_id=1, replica_groups={{0,8,16,24,32,40,48,56,64,72,80,88,96,104,112,120},{4,12,20,28,36,44,52..., dimensions={0} | all-to-all | bytes 524288 | tf_op jit(solution)/shard_map/all_to_all | solution.py:600
  73.0 3.9 %all-to-all-start.3 = ((bf16[32,32,128]{2,1,0:T(8,128)(2,1)}), bf16[32,32,128]{2,1,0:T(8,128)(2,1)S(1)}, u32[]{:S(2)}, u32[]{:S(2)}) async-start(bf16[32,32,128]{2,1,0:T(8,128)(2,1)} %bitcast.7), calls=%async_computation.3 | async-start | bytes 524288 | tf_op jit(solution)/shard_map/all_to_all | solution.py:608
  77.1 8.6 %all-to-all-done.3 = bf16[32,32,128]{2,1,0:T(8,128)(2,1)S(1)} async-done(((bf16[32,32,128]{2,1,0:T(8,128)(2,1)}), bf16[32,32,128]{2,1,0:T(8,128)(2,1)S(1)}, u32[]{:S(2)}, u32[]{:S(2)}) %all-to-all-start.3) | async-done | bytes 262176 | tf_op jit(solution)/shard_map/all_to_all | solution.py:608
  85.8 2.5 %shard_map.135.a = bf16[32,512]{1,0:T(8,128)(2,1)S(1)} custom-call(bf16[1024,128]{1,0:T(8,128)(2,1)S(1)} %bitcast.23, bf16[2,3584,256]{2,1,0:T(8,128)(2,1)} %own_hbm.11, bf16[2,3584,256]{2,1,0:T(8,128)(2,1)} %collective-permute-done.12.other_hbm), custom_call_target="tpu_custom_call" | custom-call | flops 10000000000 | tf_op jit(solution)/shard_map/pallas_call | solution.py:796
  89.8 2.6 %collective-permute-start.14 = (bf16[32,512]{1,0:T(8,128)(2,1)S(1)}, bf16[32,512]{1,0:T(8,128)(2,1)S(1)}, u32[]{:S(2)}, u32[]{:S(2)}) collective-permute-start(bf16[32,512]{1,0:T(8,128)(2,1)S(1)} %shard_map.135.a), channel_id=1, source_target_pairs={{0,1},{1,2},{2,3},{3,0},{4,5},{5,6},{6,7},{7,4},{8,9},{9,10},{10,1... | collective-permute-start | bytes 98312 | tf_op jit(solution)/shard_map/ppermute | solution.py:618
  96.6 14.2 %all_to_all.41 = bf16[16,144,128]{2,1,0:T(8,128)(2,1)S(1)} all-to-all(bf16[16,144,128]{2,1,0:T(8,128)(2,1)S(1)} %bitcast.20), channel_id=1, replica_groups={{0,8,16,24,32,40,48,56,64,72,80,88,96,104,112,120},{4,12,20,28,36,44,52..., dimensions={0} | all-to-all | bytes 1179648 | tf_op jit(solution)/shard_map/all_to_all | solution.py:600
  110.8 3.3 %shard_map.138.refs_4_ = bf16[2304,128]{1,0:T(8,128)(2,1)S(1)} custom-call(bf16[2304,128]{1,0:T(8,128)(2,1)S(1)} %bitcast.21, f32[32,128]{1,0:T(8,128)S(1)} %get-tuple-element.44.table_ref, f32[2,128]{1,0:T(2,128)S(1)} %copy-done.9, bf16[2,32,1,2,128,128]{5,4,3,2,1,0:T(8,128)(2,1)} %own_hbm.9, bf16[2,32,1,2,128,128]{5,4,3,2,1,0:T(8,128)(2,1)} %collective-permute-done.4.other_hbm), custom_call_target="tpu_custom_call" | custom-call | flops 10000000000 | tf_op jit(solution)/shard_map/pallas_call | solution.py:744
  114.1 13.7 %all_to_all.42 = bf16[16,144,128]{2,1,0:T(8,128)(2,1)S(1)} all-to-all(bf16[16,144,128]{2,1,0:T(8,128)(2,1)S(1)} %bitcast.17), channel_id=1, replica_groups={{0,8,16,24,32,40,48,56,64,72,80,88,96,104,112,120},{4,12,20,28,36,44,52..., dimensions={0} | all-to-all | bytes 1179648 | tf_op jit(solution)/shard_map/all_to_all | solution.py:600
  132.9 1.7 collective-permute-start.20
  137.7 11.8 %all_to_all.43 = bf16[16,64,128]{2,1,0:T(8,128)(2,1)S(1)} all-to-all(bf16[16,64,128]{2,1,0:T(8,128)(2,1)S(1)} %bitcast.24), channel_id=1, replica_groups={{0,8,16,24,32,40,48,56,64,72,80,88,96,104,112,120},{4,12,20,28,36,44,52..., dimensions={0} | all-to-all | bytes 524288 | tf_op jit(solution)/shard_map/all_to_all | solution.py:600
  149.7 12.1 %all_to_all.44 = bf16[32,32,128]{2,1,0:T(8,128)(2,1)S(1)} all-to-all(bf16[32,32,128]{2,1,0:T(8,128)(2,1)S(1)} %bitcast.29), channel_id=1, replica_groups=mesh['req'=32,'tp'=4] {'req'}, dimensions={0} | all-to-all | bytes 524288 | tf_op jit(solution)/shard_map/all_to_all | solution.py:608
  161.8 2.5 %shard_map.144.a = bf16[32,512]{1,0:T(8,128)(2,1)S(1)} custom-call(bf16[1024,128]{1,0:T(8,128)(2,1)S(1)} %bitcast.26, bf16[2,3584,256]{2,1,0:T(8,128)(2,1)} %own_hbm.11, bf16[2,3584,256]{2,1,0:T(8,128)(2,1)} %collective-permute-done.12.other_hbm), custom_call_target="tpu_custom_call" | custom-call | flops 10000000000 | tf_op jit(solution)/shard_map/pallas_call | solution.py:796
  164.3 1.7 collective-permute-start.21
  165.9 2.1 %collective-permute-start.22 = (bf16[32,512]{1,0:T(8,128)(2,1)S(1)}, bf16[32,512]{1,0:T(8,128)(2,1)S(1)}, u32[]{:S(2)}, u32[]{:S(2)}) collective-permute-start(bf16[32,512]{1,0:T(8,128)(2,1)S(1)} %shard_map.144.a), channel_id=1, source_target_pairs={{0,1},{1,2},{2,3},{3,0},{4,5},{5,6},{6,7},{7,4},{8,9},{9,10},{10,1... | collective-permute-start | bytes 98312 | tf_op jit(solution)/shard_map/ppermute | solution.py:618
  (76 shorter events, 28.2 us)
Async XLA Ops:
  2.0 1.5 collective-permute-start.3
  5.4 20.7 %collective-permute-start.4 = (bf16[2,32,1,2,128,128]{5,4,3,2,1,0:T(8,128)(2,1)}, bf16[2,32,1,2,128,128]{5,4,3,2,1,0:T(8,128)(2,1)}, u32[]{:S(2)}, u32[]{:S(2)}) collective-permute-start(bf16[2,32,1,2,128,128]{5,4,3,2,1,0:T(8,128)(2,1)} %own_hbm.9), channel_id=1, source_target_pairs={{0,4},{4,0},{8,12},{12,8},{16,20},{20,16},{24,28},{28,24},{32,36},... | collective-permute-start | bytes 12582920 | tf_op jit(solution)/shard_map/ppermute | solution.py:612
  5.5 20.6 %all-to-all-start = ((bf16[16,160,128]{2,1,0:T(8,128)(2,1)}), bf16[16,160,128]{2,1,0:T(8,128)(2,1)S(1)}, u32[]{:S(2)}, u32[]{:S(2)}) async-start(bf16[16,160,128]{2,1,0:T(8,128)(2,1)} %bitcast.1), calls=%async_computation | async-start | bytes 1310720 | tf_op jit(solution)/shard_map/all_to_all | solution.py:600
  12.6 41.4 %collective-permute-start.10 = (bf16[2,256,3584]{2,1,0:T(8,128)(2,1)}, bf16[2,256,3584]{2,1,0:T(8,128)(2,1)}, u32[]{:S(2)}, u32[]{:S(2)}) collective-permute-start(bf16[2,256,3584]{2,1,0:T(8,128)(2,1)} %refs_0_.3), channel_id=1, source_target_pairs={{0,4},{4,0},{8,12},{12,8},{16,20},{20,16},{24,28},{28,24},{32,36},... | collective-permute-start | bytes 11010056 | tf_op jit(solution)/shard_map/ppermute | solution.py:612
  12.8 43.5 %collective-permute-start.11 = (bf16[2,256,3584]{2,1,0:T(8,128)(2,1)}, bf16[2,256,3584]{2,1,0:T(8,128)(2,1)}, u32[]{:S(2)}, u32[]{:S(2)}) collective-permute-start(bf16[2,256,3584]{2,1,0:T(8,128)(2,1)} %refs_2_.1), channel_id=1, source_target_pairs={{0,4},{4,0},{8,12},{12,8},{16,20},{20,16},{24,28},{28,24},{32,36},... | collective-permute-start | bytes 11010056 | tf_op jit(solution)/shard_map/ppermute | solution.py:612
  30.5 15.2 %all-to-all-start.1 = ((bf16[16,144,128]{2,1,0:T(8,128)(2,1)}), bf16[16,144,128]{2,1,0:T(8,128)(2,1)S(1)}, u32[]{:S(2)}, u32[]{:S(2)}) async-start(bf16[16,144,128]{2,1,0:T(8,128)(2,1)} %bitcast.3), calls=%async_computation.1 | async-start | bytes 1179648 | tf_op jit(solution)/shard_map/all_to_all | solution.py:600
  34.2 13.9 %collective-permute-start.6 = (bf16[2,1024,256]{2,1,0:T(8,128)(2,1)S(1)}, bf16[2,1024,256]{2,1,0:T(8,128)(2,1)S(1)}, u32[]{:S(2)}, u32[]{:S(2)}) collective-permute-start(bf16[2,1024,256]{2,1,0:T(8,128)(2,1)S(1)} %copy-done.5), channel_id=1, source_target_pairs={{0,4},{4,0},{8,12},{12,8},{16,20},{20,16},{24,28},{28,24},{32,36},... | collective-permute-start | bytes 3145736 | tf_op jit(solution)/shard_map/ppermute | solution.py:612
  46.3 1.9 %collective-permute-start.5 = (bf16[128,128]{1,0:T(8,128)(2,1)S(1)}, bf16[128,128]{1,0:T(8,128)(2,1)S(1)}, u32[]{:S(2)}, u32[]{:S(2)}) collective-permute-start(bf16[128,128]{1,0:T(8,128)(2,1)S(1)} %shard_map.131.own_ref), channel_id=1, source_target_pairs={{0,4},{4,0},{8,12},{12,8},{16,20},{20,16},{24,28},{28,24},{32,36},... | collective-permute-start | bytes 98312 | tf_op jit(solution)/shard_map/ppermute | solution.py:612
  47.7 5.3 %collective-permute-start = (bf16[32,256]{1,0:T(8,128)(2,1)S(1)}, bf16[32,256]{1,0:T(8,128)(2,1)S(1)}, u32[]{:S(2)}, u32[]{:S(2)}) collective-permute-start(bf16[32,256]{1,0:T(8,128)(2,1)S(1)} %copy-done.6), channel_id=1, source_target_pairs={{0,4},{4,0},{8,12},{12,8},{16,20},{20,16},{24,28},{28,24},{32,36},... | collective-permute-start | bytes 49160 | tf_op jit(solution)/shard_map/ppermute | solution.py:612
  48.2 28.9 %collective-permute-start.12 = (bf16[2,3584,256]{2,1,0:T(8,128)(2,1)}, bf16[2,3584,256]{2,1,0:T(8,128)(2,1)}, u32[]{:S(2)}, u32[]{:S(2)}) collective-permute-start(bf16[2,3584,256]{2,1,0:T(8,128)(2,1)} %own_hbm.11), channel_id=1, source_target_pairs={{0,4},{4,0},{8,12},{12,8},{16,20},{20,16},{24,28},{28,24},{32,36},... | collective-permute-start | bytes 11010056 | tf_op jit(solution)/shard_map/ppermute | solution.py:612
  49.2 7.2 %collective-permute-start.7 = (bf16[32,512]{1,0:T(8,128)(2,1)S(1)}, bf16[32,512]{1,0:T(8,128)(2,1)S(1)}, u32[]{:S(2)}, u32[]{:S(2)}) collective-permute-start(bf16[32,512]{1,0:T(8,128)(2,1)S(1)} %shard_map.132.a), channel_id=1, source_target_pairs={{0,2},{1,3},{2,0},{3,1},{4,6},{5,7},{6,4},{7,5},{8,10},{9,11},{10,... | collective-permute-start | bytes 98312 | tf_op jit(solution)/shard_map/ppermute | solution.py:618
  53.0 5.1 %collective-permute-start.8 = (bf16[32,512]{1,0:T(8,128)(2,1)S(1)}, bf16[32,512]{1,0:T(8,128)(2,1)S(1)}, u32[]{:S(2)}, u32[]{:S(2)}) collective-permute-start(bf16[32,512]{1,0:T(8,128)(2,1)S(1)} %shard_map.132.a), channel_id=1, source_target_pairs={{0,1},{1,2},{2,3},{3,0},{4,5},{5,6},{6,7},{7,4},{8,9},{9,10},{10,1... | collective-permute-start | bytes 98312 | tf_op jit(solution)/shard_map/ppermute | solution.py:618
  54.1 4.1 %collective-permute-start.9 = (bf16[32,512]{1,0:T(8,128)(2,1)S(1)}, bf16[32,512]{1,0:T(8,128)(2,1)S(1)}, u32[]{:S(2)}, u32[]{:S(2)}) collective-permute-start(bf16[32,512]{1,0:T(8,128)(2,1)S(1)} %shard_map.132.a), channel_id=1, source_target_pairs={{0,3},{1,0},{2,1},{3,2},{4,7},{5,4},{6,5},{7,6},{8,11},{9,8},{10,9... | collective-permute-start | bytes 98312 | tf_op jit(solution)/shard_map/ppermute | solution.py:618
  73.0 12.8 %all-to-all-start.3 = ((bf16[32,32,128]{2,1,0:T(8,128)(2,1)}), bf16[32,32,128]{2,1,0:T(8,128)(2,1)S(1)}, u32[]{:S(2)}, u32[]{:S(2)}) async-start(bf16[32,32,128]{2,1,0:T(8,128)(2,1)} %bitcast.7), calls=%async_computation.3 | async-start | bytes 524288 | tf_op jit(solution)/shard_map/all_to_all | solution.py:608
  76.9 16.2 %collective-permute-start.16 = (bf16[2,256,1024]{2,1,0:T(8,128)(2,1)S(1)}, bf16[2,256,1024]{2,1,0:T(8,128)(2,1)}, u32[]{:S(2)}, u32[]{:S(2)}) collective-permute-start(bf16[2,256,1024]{2,1,0:T(8,128)(2,1)S(1)} %copy-done.4), channel_id=1, source_target_pairs={{0,4},{4,0},{8,12},{12,8},{16,20},{20,16},{24,28},{28,24},{32,36},... | collective-permute-start | bytes 3145736 | tf_op jit(solution)/shard_map/ppermute | solution.py:612
  88.3 5.8 %collective-permute-start.13 = (bf16[32,512]{1,0:T(8,128)(2,1)S(1)}, bf16[32,512]{1,0:T(8,128)(2,1)S(1)}, u32[]{:S(2)}, u32[]{:S(2)}) collective-permute-start(bf16[32,512]{1,0:T(8,128)(2,1)S(1)} %shard_map.135.a), channel_id=1, source_target_pairs={{0,2},{1,3},{2,0},{3,1},{4,6},{5,7},{6,4},{7,5},{8,10},{9,11},{10,... | collective-permute-start | bytes 98312 | tf_op jit(solution)/shard_map/ppermute | solution.py:618
  89.8 5.1 %collective-permute-start.14 = (bf16[32,512]{1,0:T(8,128)(2,1)S(1)}, bf16[32,512]{1,0:T(8,128)(2,1)S(1)}, u32[]{:S(2)}, u32[]{:S(2)}) collective-permute-start(bf16[32,512]{1,0:T(8,128)(2,1)S(1)} %shard_map.135.a), channel_id=1, source_target_pairs={{0,1},{1,2},{2,3},{3,0},{4,5},{5,6},{6,7},{7,4},{8,9},{9,10},{10,1... | collective-permute-start | bytes 98312 | tf_op jit(solution)/shard_map/ppermute | solution.py:618
  92.4 3.9 %collective-permute-start.15 = (bf16[32,512]{1,0:T(8,128)(2,1)S(1)}, bf16[32,512]{1,0:T(8,128)(2,1)S(1)}, u32[]{:S(2)}, u32[]{:S(2)}) collective-permute-start(bf16[32,512]{1,0:T(8,128)(2,1)S(1)} %shard_map.135.a), channel_id=1, source_target_pairs={{0,3},{1,0},{2,1},{3,2},{4,7},{5,4},{6,5},{7,6},{8,11},{9,8},{10,9... | collective-permute-start | bytes 98312 | tf_op jit(solution)/shard_map/ppermute | solution.py:618
  130.0 6.1 %collective-permute-start.18 = (bf16[32,512]{1,0:T(8,128)(2,1)S(1)}, bf16[32,512]{1,0:T(8,128)(2,1)S(1)}, u32[]{:S(2)}, u32[]{:S(2)}) collective-permute-start(bf16[32,512]{1,0:T(8,128)(2,1)S(1)} %shard_map.140.a), channel_id=1, source_target_pairs={{0,2},{1,3},{2,0},{3,1},{4,6},{5,7},{6,4},{7,5},{8,10},{9,11},{10,... | collective-permute-start | bytes 98312 | tf_op jit(solution)/shard_map/ppermute | solution.py:618
  131.4 5.1 %collective-permute-start.19 = (bf16[32,512]{1,0:T(8,128)(2,1)S(1)}, bf16[32,512]{1,0:T(8,128)(2,1)S(1)}, u32[]{:S(2)}, u32[]{:S(2)}) collective-permute-start(bf16[32,512]{1,0:T(8,128)(2,1)S(1)} %shard_map.140.a), channel_id=1, source_target_pairs={{0,1},{1,2},{2,3},{3,0},{4,5},{5,6},{6,7},{7,4},{8,9},{9,10},{10,1... | collective-permute-start | bytes 98312 | tf_op jit(solution)/shard_map/ppermute | solution.py:618
  132.9 3.9 %collective-permute-start.20 = (bf16[32,512]{1,0:T(8,128)(2,1)S(1)}, bf16[32,512]{1,0:T(8,128)(2,1)S(1)}, u32[]{:S(2)}, u32[]{:S(2)}) collective-permute-start(bf16[32,512]{1,0:T(8,128)(2,1)S(1)} %shard_map.140.a), channel_id=1, source_target_pairs={{0,3},{1,0},{2,1},{3,2},{4,7},{5,4},{6,5},{7,6},{8,11},{9,8},{10,9... | collective-permute-start | bytes 98312 | tf_op jit(solution)/shard_map/ppermute | solution.py:618
  164.3 5.5 %collective-permute-start.21 = (bf16[32,512]{1,0:T(8,128)(2,1)S(1)}, bf16[32,512]{1,0:T(8,128)(2,1)S(1)}, u32[]{:S(2)}, u32[]{:S(2)}) collective-permute-start(bf16[32,512]{1,0:T(8,128)(2,1)S(1)} %shard_map.144.a), channel_id=1, source_target_pairs={{0,2},{1,3},{2,0},{3,1},{4,6},{5,7},{6,4},{7,5},{8,10},{9,11},{10,... | collective-permute-start | bytes 98312 | tf_op jit(solution)/shard_map/ppermute | solution.py:618
  165.9 5.1 %collective-permute-start.22 = (bf16[32,512]{1,0:T(8,128)(2,1)S(1)}, bf16[32,512]{1,0:T(8,128)(2,1)S(1)}, u32[]{:S(2)}, u32[]{:S(2)}) collective-permute-start(bf16[32,512]{1,0:T(8,128)(2,1)S(1)} %shard_map.144.a), channel_id=1, source_target_pairs={{0,1},{1,2},{2,3},{3,0},{4,5},{5,6},{6,7},{7,4},{8,9},{9,10},{10,1... | collective-permute-start | bytes 98312 | tf_op jit(solution)/shard_map/ppermute | solution.py:618
  168.1 3.9 %collective-permute-start.23 = (bf16[32,512]{1,0:T(8,128)(2,1)S(1)}, bf16[32,512]{1,0:T(8,128)(2,1)S(1)}, u32[]{:S(2)}, u32[]{:S(2)}) collective-permute-start(bf16[32,512]{1,0:T(8,128)(2,1)S(1)} %shard_map.144.a), channel_id=1, source_target_pairs={{0,3},{1,0},{2,1},{3,2},{4,7},{5,4},{6,5},{7,6},{8,11},{9,8},{10,9... | collective-permute-start | bytes 98312 | tf_op jit(solution)/shard_map/ppermute | solution.py:618
  (14 other events, 74.9 us)

commit v8 on v7

--- a/solution.py
+++ b/solution.py
@@ -391,7 +391,10 @@
     repeat_into(out_ref, jnp.concatenate([acc, stats[:extra]], axis=0).astype(BF16))
 
 
-def first_block_kernel(sources, received_ref, tables_ref, own_hbm, other_hbm, out_ref, table_out, *scratch):
+def first_block_kernel(
+    sources, received_ref, tables_ref, own_hbm, other_hbm, fetched_before, out_ref, table_out, *scratch
+):
+    del fetched_before
     block_kernel(
         0, sources, received_ref, None, tables_ref, own_hbm, other_hbm, out_ref, table_out, *scratch
     )
@@ -737,9 +740,9 @@
             payload, table = call(
                 functools.partial(first_block_kernel, side),
                 [rows_type(side * stat_rows), rows_type(requests, F32)],
-                [VMEM] * 2 + [HBM] * 2,
+                [VMEM] * 2 + [HBM] * 2 + [ANY],
                 scratch,
-            )(received, tables, kv_pool, pool_other)
+            )(received, tables, kv_pool, pool_other, o_other)
         else:
             payload = call(
                 functools.partial(later_block_kernel, layer_no, side),

time: 173 us -> 173 us (level)
  blocking collectives: 63.5 us -> 78.5 us
  waiting for transfers between devices: 44.2 us -> 32.7 us
  starting transfers between devices: 38.5 us -> 34.7 us
    all_to_all x4 -> x5, blocking collectives: 51.4 us -> 66.4 us  [exchange(): lax.all_to_all(blocks, 'req', split_axis=0, concat_axis=0, tiled=True, ax...]
    all_to_all x2 -> x1, waiting for transfers between devices: 24.3 us -> 12.9 us  [exchange(): lax.all_to_all(blocks, 'req', split_axis=0, concat_axis=0, tiled=True, ax...]
    all_to_all x2 -> x1, starting transfers between devices: 10.7 us -> 7.12 us  [exchange(): lax.all_to_all(blocks, 'req', split_axis=0, concat_axis=0, tiled=True, ax...]
  transfers between devices with their start and end apart: 27 -> 26, of which waited for: 15 -> 14; matrix products, arithmetic and copies ran while one was open for 0% -> 0% of each run, Pallas kernels for 8% -> 7%
where the time goes in v8:
time: 173 us; the launch traced here: 172 us
  blocking collectives  78.5 us (45%)
  starting transfers between devices  34.7 us (20%)
  waiting for transfers between devices  32.7 us (19%)
  Pallas kernels  24.3 us (14%)
    all_to_all x5, blocking collectives, exchange(): lax.all_to_all(blocks, 'req', split_axis=0, concat_axis=0, tiled=True, ax...  66.4 us
    ppermute x12, starting transfers between devices, tp_parts(): lax.ppermute(partial_sum, 'tp', [(i, (i + shift) % n_tp) for i in range(n...  21.3 us
    all_to_all x1, waiting for transfers between devices, exchange(): lax.all_to_all(blocks, 'req', split_axis=0, concat_axis=0, tiled=True, ax...  12.9 us
    all_to_all x1, blocking collectives, exchange_all(): lax.all_to_all(blocks, 'req', split_axis=0, concat_axis=0, tiled=True)  12.1 us
    all_to_all x1, waiting for transfers between devices, exchange_all(): lax.all_to_all(blocks, 'req', split_axis=0, concat_axis=0, tiled=True)  8.65 us
    ppermute x12, waiting for transfers between devices, tp_parts(): lax.ppermute(partial_sum, 'tp', [(i, (i + shift) % n_tp) for i in range(n...  7.65 us
    all_to_all x1, starting transfers between devices, exchange(): lax.all_to_all(blocks, 'req', split_axis=0, concat_axis=0, tiled=True, ax...  7.12 us
    pallas_call x2, Pallas kernels, shards(): call(functools.partial(down_kernel, layer_no, f_rows, chunk), pair_type(r...  4.99 us
  transfers between devices with their start and end apart: 26, of which 14 were waited for; matrix products, arithmetic and copies ran while one was open for 0% of the time, Pallas kernels for 7%

profile of v8, /device:TPU:0, one launch (start us, length us, event | category | flops | bytes accessed | tf_op | source)
XLA Modules:
  0.0 171.8 jit_solution(6204936323206313932)
XLA Ops:
  0.0 2.0 %shard_map.128 = (f32[160,128]{1,0:T(8,128)}, bf16[160,128]{1,0:T(8,128)(2,1)}) custom-call(bf16[32,256]{1,0:T(8,128)(2,1)} %x_hbm.1, bf16[2,256]{1,0:T(2,128)(2,1)} %gain_hbm.1, bf16[2,256,1024]{2,1,0:T(8,128)(2,1)} %refs_0_.2, s32[1,32]{1,0:T(1,128)} %homes_hbm.1, s32[2,1,1,24]{3,2,1,0:T(1,128)} %chosen_hbm.1, s32[1,2]{1,0:T(1,128)} %bitcast.31), custom_call_target="tpu_custom_call" | custom-call | flops 10000000000 | tf_op jit(solution)/shard_map/pallas_call | solution.py:665
  6.1 7.1 %all-to-all-start = ((bf16[16,160,128]{2,1,0:T(8,128)(2,1)}), bf16[16,160,128]{2,1,0:T(8,128)(2,1)S(1)}, u32[]{:S(2)}, u32[]{:S(2)}) async-start(bf16[16,160,128]{2,1,0:T(8,128)(2,1)} %bitcast.1), calls=%async_computation | async-start | bytes 1310720 | tf_op jit(solution)/shard_map/all_to_all | solution.py:603
  13.8 12.9 %all-to-all-done = bf16[16,160,128]{2,1,0:T(8,128)(2,1)S(1)} async-done(((bf16[16,160,128]{2,1,0:T(8,128)(2,1)}), bf16[16,160,128]{2,1,0:T(8,128)(2,1)S(1)}, u32[]{:S(2)}, u32[]{:S(2)}) %all-to-all-start) | async-done | bytes 655392 | tf_op jit(solution)/shard_map/all_to_all | solution.py:603
  26.6 3.6 %shard_map.130 = (bf16[2304,128]{1,0:T(8,128)(2,1)S(1)}, f32[32,128]{1,0:T(8,128)S(1)}) custom-call(bf16[2560,128]{1,0:T(8,128)(2,1)S(1)} %bitcast.18, f32[2,128]{1,0:T(2,128)S(1)} %copy-done.9, bf16[2,32,1,2,128,128]{5,4,3,2,1,0:T(8,128)(2,1)} %own_hbm.9, bf16[2,32,1,2,128,128]{5,4,3,2,1,0:T(8,128)(2,1)} %collective-permute-done.4.other_hbm, ...), custom_call_target="tpu_custom_call" | custom-call | flops 10000000000 | tf_op jit(solution)/shard_map/pallas_call | solution.py:740
  30.2 14.9 %all_to_all.40 = bf16[16,144,128]{2,1,0:T(8,128)(2,1)S(1)} all-to-all(bf16[16,144,128]{2,1,0:T(8,128)(2,1)S(1)} %bitcast.21), channel_id=1, replica_groups={{0,8,16,24,32,40,48,56,64,72,80,88,96,104,112,120},{4,12,20,28,36,44,52..., dimensions={0} | all-to-all | bytes 1179648 | tf_op jit(solution)/shard_map/all_to_all | solution.py:603
  48.2 3.9 %collective-permute-start.7 = (bf16[32,512]{1,0:T(8,128)(2,1)S(1)}, bf16[32,512]{1,0:T(8,128)(2,1)S(1)}, u32[]{:S(2)}, u32[]{:S(2)}) collective-permute-start(bf16[32,512]{1,0:T(8,128)(2,1)S(1)} %shard_map.132.a), channel_id=1, source_target_pairs={{0,2},{1,3},{2,0},{3,1},{4,6},{5,7},{6,4},{7,5},{8,10},{9,11},{10,... | collective-permute-start | bytes 98312 | tf_op jit(solution)/shard_map/ppermute | solution.py:621
  53.1 2.2 %collective-permute-start.9 = (bf16[32,512]{1,0:T(8,128)(2,1)S(1)}, bf16[32,512]{1,0:T(8,128)(2,1)S(1)}, u32[]{:S(2)}, u32[]{:S(2)}) collective-permute-start(bf16[32,512]{1,0:T(8,128)(2,1)S(1)} %shard_map.132.a), channel_id=1, source_target_pairs={{0,3},{1,0},{2,1},{3,2},{4,7},{5,4},{6,5},{7,6},{8,11},{9,8},{10,9... | collective-permute-start | bytes 98312 | tf_op jit(solution)/shard_map/ppermute | solution.py:621
  55.4 1.8 %collective-permute-done.8.c = bf16[32,512]{1,0:T(8,128)(2,1)S(1)} collective-permute-done((bf16[32,512]{1,0:T(8,128)(2,1)S(1)}, bf16[32,512]{1,0:T(8,128)(2,1)S(1)}, u32[]{:S(2)}, u32[]{:S(2)}) %collective-permute-start.8) | collective-permute-done | bytes 32800 | tf_op jit(solution)/shard_map/ppermute | solution.py:621
  57.2 2.3 %shard_map.133 = (bf16[32,512]{1,0:T(8,128)(2,1)S(1)}, bf16[1024,128]{1,0:T(8,128)(2,1)S(1)}) custom-call(bf16[32,512]{1,0:T(8,128)(2,1)S(1)} %get-tuple-element.27.x_ref, bf16[32,512]{1,0:T(8,128)(2,1)S(1)} %shard_map.132.a, bf16[32,512]{1,0:T(8,128)(2,1)S(1)} %collective-permute-done.7.b, bf16[32,512]{1,0:T(8,128)(2,1)S(1)} %collective-permute-done.8.c, ...), custom_call_target="tpu_custom_call" | custom-call | flops 10000000000 | tf_op jit(solution)/shard_map/pallas_call | solution.py:782
  59.5 11.8 %all_to_all.41 = bf16[16,64,128]{2,1,0:T(8,128)(2,1)S(1)} all-to-all(bf16[16,64,128]{2,1,0:T(8,128)(2,1)S(1)} %bitcast.26), channel_id=1, replica_groups={{0,8,16,24,32,40,48,56,64,72,80,88,96,104,112,120},{4,12,20,28,36,44,52..., dimensions={0} | all-to-all | bytes 524288 | tf_op jit(solution)/shard_map/all_to_all | solution.py:603
  72.2 3.9 %all-to-all-start.3 = ((bf16[32,32,128]{2,1,0:T(8,128)(2,1)}), bf16[32,32,128]{2,1,0:T(8,128)(2,1)S(1)}, u32[]{:S(2)}, u32[]{:S(2)}) async-start(bf16[32,32,128]{2,1,0:T(8,128)(2,1)} %bitcast.7), calls=%async_computation.3 | async-start | bytes 524288 | tf_op jit(solution)/shard_map/all_to_all | solution.py:611
  76.3 8.6 %all-to-all-done.3 = bf16[32,32,128]{2,1,0:T(8,128)(2,1)S(1)} async-done(((bf16[32,32,128]{2,1,0:T(8,128)(2,1)}), bf16[32,32,128]{2,1,0:T(8,128)(2,1)S(1)}, u32[]{:S(2)}, u32[]{:S(2)}) %all-to-all-start.3) | async-done | bytes 262176 | tf_op jit(solution)/shard_map/all_to_all | solution.py:611
  85.0 2.5 %shard_map.135.a = bf16[32,512]{1,0:T(8,128)(2,1)S(1)} custom-call(bf16[1024,128]{1,0:T(8,128)(2,1)S(1)} %bitcast.24, bf16[2,3584,256]{2,1,0:T(8,128)(2,1)} %own_hbm.11, bf16[2,3584,256]{2,1,0:T(8,128)(2,1)} %collective-permute-done.12.other_hbm), custom_call_target="tpu_custom_call" | custom-call | flops 10000000000 | tf_op jit(solution)/shard_map/pallas_call | solution.py:799
  89.0 2.6 %collective-permute-start.14 = (bf16[32,512]{1,0:T(8,128)(2,1)S(1)}, bf16[32,512]{1,0:T(8,128)(2,1)S(1)}, u32[]{:S(2)}, u32[]{:S(2)}) collective-permute-start(bf16[32,512]{1,0:T(8,128)(2,1)S(1)} %shard_map.135.a), channel_id=1, source_target_pairs={{0,1},{1,2},{2,3},{3,0},{4,5},{5,6},{6,7},{7,4},{8,9},{9,10},{10,1... | collective-permute-start | bytes 98312 | tf_op jit(solution)/shard_map/ppermute | solution.py:621
  95.8 14.2 %all_to_all.42 = bf16[16,144,128]{2,1,0:T(8,128)(2,1)S(1)} all-to-all(bf16[16,144,128]{2,1,0:T(8,128)(2,1)S(1)} %bitcast.19), channel_id=1, replica_groups={{0,8,16,24,32,40,48,56,64,72,80,88,96,104,112,120},{4,12,20,28,36,44,52..., dimensions={0} | all-to-all | bytes 1179648 | tf_op jit(solution)/shard_map/all_to_all | solution.py:603
  110.0 3.3 %shard_map.138.refs_4_ = bf16[2304,128]{1,0:T(8,128)(2,1)S(1)} custom-call(bf16[2304,128]{1,0:T(8,128)(2,1)S(1)} %bitcast.20, f32[32,128]{1,0:T(8,128)S(1)} %get-tuple-element.44.table_ref, f32[2,128]{1,0:T(2,128)S(1)} %copy-done.9, bf16[2,32,1,2,128,128]{5,4,3,2,1,0:T(8,128)(2,1)} %own_hbm.9, bf16[2,32,1,2,128,128]{5,4,3,2,1,0:T(8,128)(2,1)} %collective-permute-done.4.other_hbm), custom_call_target="tpu_custom_call" | custom-call | flops 10000000000 | tf_op jit(solution)/shard_map/pallas_call | solution.py:747
  113.3 13.7 %all_to_all.43 = bf16[16,144,128]{2,1,0:T(8,128)(2,1)S(1)} all-to-all(bf16[16,144,128]{2,1,0:T(8,128)(2,1)S(1)} %bitcast.17), channel_id=1, replica_groups={{0,8,16,24,32,40,48,56,64,72,80,88,96,104,112,120},{4,12,20,28,36,44,52..., dimensions={0} | all-to-all | bytes 1179648 | tf_op jit(solution)/shard_map/all_to_all | solution.py:603
  130.5 1.6 collective-permute-start.19
  132.1 1.7 collective-permute-start.20
  136.9 11.8 %all_to_all.44 = bf16[16,64,128]{2,1,0:T(8,128)(2,1)S(1)} all-to-all(bf16[16,64,128]{2,1,0:T(8,128)(2,1)S(1)} %bitcast.25), channel_id=1, replica_groups={{0,8,16,24,32,40,48,56,64,72,80,88,96,104,112,120},{4,12,20,28,36,44,52..., dimensions={0} | all-to-all | bytes 524288 | tf_op jit(solution)/shard_map/all_to_all | solution.py:603
  148.9 12.1 %all_to_all.45 = bf16[32,32,128]{2,1,0:T(8,128)(2,1)S(1)} all-to-all(bf16[32,32,128]{2,1,0:T(8,128)(2,1)S(1)} %bitcast.30), channel_id=1, replica_groups=mesh['req'=32,'tp'=4] {'req'}, dimensions={0} | all-to-all | bytes 524288 | tf_op jit(solution)/shard_map/all_to_all | solution.py:611
  161.0 2.5 %shard_map.144.a = bf16[32,512]{1,0:T(8,128)(2,1)S(1)} custom-call(bf16[1024,128]{1,0:T(8,128)(2,1)S(1)} %bitcast.27, bf16[2,3584,256]{2,1,0:T(8,128)(2,1)} %own_hbm.11, bf16[2,3584,256]{2,1,0:T(8,128)(2,1)} %collective-permute-done.12.other_hbm), custom_call_target="tpu_custom_call" | custom-call | flops 10000000000 | tf_op jit(solution)/shard_map/pallas_call | solution.py:799
  163.5 1.6 collective-permute-start.21
  165.2 2.1 %collective-permute-start.22 = (bf16[32,512]{1,0:T(8,128)(2,1)S(1)}, bf16[32,512]{1,0:T(8,128)(2,1)S(1)}, u32[]{:S(2)}, u32[]{:S(2)}) collective-permute-start(bf16[32,512]{1,0:T(8,128)(2,1)S(1)} %shard_map.144.a), channel_id=1, source_target_pairs={{0,1},{1,2},{2,3},{3,0},{4,5},{5,6},{6,7},{7,4},{8,9},{9,10},{10,1... | collective-permute-start | bytes 98312 | tf_op jit(solution)/shard_map/ppermute | solution.py:621
  (75 shorter events, 26.8 us)
Async XLA Ops:
  2.0 1.5 collective-permute-start.3
  5.3 21.3 %collective-permute-start.4 = (bf16[2,32,1,2,128,128]{5,4,3,2,1,0:T(8,128)(2,1)}, bf16[2,32,1,2,128,128]{5,4,3,2,1,0:T(8,128)(2,1)}, u32[]{:S(2)}, u32[]{:S(2)}) collective-permute-start(bf16[2,32,1,2,128,128]{5,4,3,2,1,0:T(8,128)(2,1)} %own_hbm.9), channel_id=1, source_target_pairs={{0,4},{4,0},{8,12},{12,8},{16,20},{20,16},{24,28},{28,24},{32,36},... | collective-permute-start | bytes 12582920 | tf_op jit(solution)/shard_map/ppermute | solution.py:615
  5.9 20.7 %collective-permute-start.5 = (bf16[2,1024,256]{2,1,0:T(8,128)(2,1)S(1)}, bf16[2,1024,256]{2,1,0:T(8,128)(2,1)S(1)}, u32[]{:S(2)}, u32[]{:S(2)}) collective-permute-start(bf16[2,1024,256]{2,1,0:T(8,128)(2,1)S(1)} %copy-done.5), channel_id=1, source_target_pairs={{0,4},{4,0},{8,12},{12,8},{16,20},{20,16},{24,28},{28,24},{32,36},... | collective-permute-start | bytes 3145736 | tf_op jit(solution)/shard_map/ppermute | solution.py:615
  6.1 20.6 %all-to-all-start = ((bf16[16,160,128]{2,1,0:T(8,128)(2,1)}), bf16[16,160,128]{2,1,0:T(8,128)(2,1)S(1)}, u32[]{:S(2)}, u32[]{:S(2)}) async-start(bf16[16,160,128]{2,1,0:T(8,128)(2,1)} %bitcast.1), calls=%async_computation | async-start | bytes 1310720 | tf_op jit(solution)/shard_map/all_to_all | solution.py:603
  13.2 39.9 %collective-permute-start.10 = (bf16[2,256,3584]{2,1,0:T(8,128)(2,1)}, bf16[2,256,3584]{2,1,0:T(8,128)(2,1)}, u32[]{:S(2)}, u32[]{:S(2)}) collective-permute-start(bf16[2,256,3584]{2,1,0:T(8,128)(2,1)} %refs_0_.3), channel_id=1, source_target_pairs={{0,4},{4,0},{8,12},{12,8},{16,20},{20,16},{24,28},{28,24},{32,36},... | collective-permute-start | bytes 11010056 | tf_op jit(solution)/shard_map/ppermute | solution.py:615
  13.3 42.0 %collective-permute-start.11 = (bf16[2,256,3584]{2,1,0:T(8,128)(2,1)}, bf16[2,256,3584]{2,1,0:T(8,128)(2,1)}, u32[]{:S(2)}, u32[]{:S(2)}) collective-permute-start(bf16[2,256,3584]{2,1,0:T(8,128)(2,1)} %refs_2_.1), channel_id=1, source_target_pairs={{0,4},{4,0},{8,12},{12,8},{16,20},{20,16},{24,28},{28,24},{32,36},... | collective-permute-start | bytes 11010056 | tf_op jit(solution)/shard_map/ppermute | solution.py:615
  45.7 1.7 %collective-permute-start.6 = (bf16[128,128]{1,0:T(8,128)(2,1)S(1)}, bf16[128,128]{1,0:T(8,128)(2,1)S(1)}, u32[]{:S(2)}, u32[]{:S(2)}) collective-permute-start(bf16[128,128]{1,0:T(8,128)(2,1)S(1)} %shard_map.131.own_ref), channel_id=1, source_target_pairs={{0,4},{4,0},{8,12},{12,8},{16,20},{20,16},{24,28},{28,24},{32,36},... | collective-permute-start | bytes 98312 | tf_op jit(solution)/shard_map/ppermute | solution.py:615
  46.3 5.8 %collective-permute-start = (bf16[32,256]{1,0:T(8,128)(2,1)S(1)}, bf16[32,256]{1,0:T(8,128)(2,1)S(1)}, u32[]{:S(2)}, u32[]{:S(2)}) collective-permute-start(bf16[32,256]{1,0:T(8,128)(2,1)S(1)} %copy-done.6), channel_id=1, source_target_pairs={{0,4},{4,0},{8,12},{12,8},{16,20},{20,16},{24,28},{28,24},{32,36},... | collective-permute-start | bytes 49160 | tf_op jit(solution)/shard_map/ppermute | solution.py:615
  47.4 28.9 %collective-permute-start.12 = (bf16[2,3584,256]{2,1,0:T(8,128)(2,1)}, bf16[2,3584,256]{2,1,0:T(8,128)(2,1)}, u32[]{:S(2)}, u32[]{:S(2)}) collective-permute-start(bf16[2,3584,256]{2,1,0:T(8,128)(2,1)} %own_hbm.11), channel_id=1, source_target_pairs={{0,4},{4,0},{8,12},{12,8},{16,20},{20,16},{24,28},{28,24},{32,36},... | collective-permute-start | bytes 11010056 | tf_op jit(solution)/shard_map/ppermute | solution.py:615
  48.2 7.2 %collective-permute-start.7 = (bf16[32,512]{1,0:T(8,128)(2,1)S(1)}, bf16[32,512]{1,0:T(8,128)(2,1)S(1)}, u32[]{:S(2)}, u32[]{:S(2)}) collective-permute-start(bf16[32,512]{1,0:T(8,128)(2,1)S(1)} %shard_map.132.a), channel_id=1, source_target_pairs={{0,2},{1,3},{2,0},{3,1},{4,6},{5,7},{6,4},{7,5},{8,10},{9,11},{10,... | collective-permute-start | bytes 98312 | tf_op jit(solution)/shard_map/ppermute | solution.py:621
  52.1 5.1 %collective-permute-start.8 = (bf16[32,512]{1,0:T(8,128)(2,1)S(1)}, bf16[32,512]{1,0:T(8,128)(2,1)S(1)}, u32[]{:S(2)}, u32[]{:S(2)}) collective-permute-start(bf16[32,512]{1,0:T(8,128)(2,1)S(1)} %shard_map.132.a), channel_id=1, source_target_pairs={{0,1},{1,2},{2,3},{3,0},{4,5},{5,6},{6,7},{7,4},{8,9},{9,10},{10,1... | collective-permute-start | bytes 98312 | tf_op jit(solution)/shard_map/ppermute | solution.py:621
  53.1 4.1 %collective-permute-start.9 = (bf16[32,512]{1,0:T(8,128)(2,1)S(1)}, bf16[32,512]{1,0:T(8,128)(2,1)S(1)}, u32[]{:S(2)}, u32[]{:S(2)}) collective-permute-start(bf16[32,512]{1,0:T(8,128)(2,1)S(1)} %shard_map.132.a), channel_id=1, source_target_pairs={{0,3},{1,0},{2,1},{3,2},{4,7},{5,4},{6,5},{7,6},{8,11},{9,8},{10,9... | collective-permute-start | bytes 98312 | tf_op jit(solution)/shard_map/ppermute | solution.py:621
  72.2 12.8 %all-to-all-start.3 = ((bf16[32,32,128]{2,1,0:T(8,128)(2,1)}), bf16[32,32,128]{2,1,0:T(8,128)(2,1)S(1)}, u32[]{:S(2)}, u32[]{:S(2)}) async-start(bf16[32,32,128]{2,1,0:T(8,128)(2,1)} %bitcast.7), calls=%async_computation.3 | async-start | bytes 524288 | tf_op jit(solution)/shard_map/all_to_all | solution.py:611
  76.1 16.2 %collective-permute-start.16 = (bf16[2,256,1024]{2,1,0:T(8,128)(2,1)S(1)}, bf16[2,256,1024]{2,1,0:T(8,128)(2,1)}, u32[]{:S(2)}, u32[]{:S(2)}) collective-permute-start(bf16[2,256,1024]{2,1,0:T(8,128)(2,1)S(1)} %copy-done.4), channel_id=1, source_target_pairs={{0,4},{4,0},{8,12},{12,8},{16,20},{20,16},{24,28},{28,24},{32,36},... | collective-permute-start | bytes 3145736 | tf_op jit(solution)/shard_map/ppermute | solution.py:615
  87.5 5.8 %collective-permute-start.13 = (bf16[32,512]{1,0:T(8,128)(2,1)S(1)}, bf16[32,512]{1,0:T(8,128)(2,1)S(1)}, u32[]{:S(2)}, u32[]{:S(2)}) collective-permute-start(bf16[32,512]{1,0:T(8,128)(2,1)S(1)} %shard_map.135.a), channel_id=1, source_target_pairs={{0,2},{1,3},{2,0},{3,1},{4,6},{5,7},{6,4},{7,5},{8,10},{9,11},{10,... | collective-permute-start | bytes 98312 | tf_op jit(solution)/shard_map/ppermute | solution.py:621
  89.0 5.1 %collective-permute-start.14 = (bf16[32,512]{1,0:T(8,128)(2,1)S(1)}, bf16[32,512]{1,0:T(8,128)(2,1)S(1)}, u32[]{:S(2)}, u32[]{:S(2)}) collective-permute-start(bf16[32,512]{1,0:T(8,128)(2,1)S(1)} %shard_map.135.a), channel_id=1, source_target_pairs={{0,1},{1,2},{2,3},{3,0},{4,5},{5,6},{6,7},{7,4},{8,9},{9,10},{10,1... | collective-permute-start | bytes 98312 | tf_op jit(solution)/shard_map/ppermute | solution.py:621
  91.6 3.9 %collective-permute-start.15 = (bf16[32,512]{1,0:T(8,128)(2,1)S(1)}, bf16[32,512]{1,0:T(8,128)(2,1)S(1)}, u32[]{:S(2)}, u32[]{:S(2)}) collective-permute-start(bf16[32,512]{1,0:T(8,128)(2,1)S(1)} %shard_map.135.a), channel_id=1, source_target_pairs={{0,3},{1,0},{2,1},{3,2},{4,7},{5,4},{6,5},{7,6},{8,11},{9,8},{10,9... | collective-permute-start | bytes 98312 | tf_op jit(solution)/shard_map/ppermute | solution.py:621
  127.6 1.3 collective-permute-start.17
  129.3 6.1 %collective-permute-start.18 = (bf16[32,512]{1,0:T(8,128)(2,1)S(1)}, bf16[32,512]{1,0:T(8,128)(2,1)S(1)}, u32[]{:S(2)}, u32[]{:S(2)}) collective-permute-start(bf16[32,512]{1,0:T(8,128)(2,1)S(1)} %shard_map.140.a), channel_id=1, source_target_pairs={{0,2},{1,3},{2,0},{3,1},{4,6},{5,7},{6,4},{7,5},{8,10},{9,11},{10,... | collective-permute-start | bytes 98312 | tf_op jit(solution)/shard_map/ppermute | solution.py:621
  130.5 5.1 %collective-permute-start.19 = (bf16[32,512]{1,0:T(8,128)(2,1)S(1)}, bf16[32,512]{1,0:T(8,128)(2,1)S(1)}, u32[]{:S(2)}, u32[]{:S(2)}) collective-permute-start(bf16[32,512]{1,0:T(8,128)(2,1)S(1)} %shard_map.140.a), channel_id=1, source_target_pairs={{0,1},{1,2},{2,3},{3,0},{4,5},{5,6},{6,7},{7,4},{8,9},{9,10},{10,1... | collective-permute-start | bytes 98312 | tf_op jit(solution)/shard_map/ppermute | solution.py:621
  132.1 3.9 %collective-permute-start.20 = (bf16[32,512]{1,0:T(8,128)(2,1)S(1)}, bf16[32,512]{1,0:T(8,128)(2,1)S(1)}, u32[]{:S(2)}, u32[]{:S(2)}) collective-permute-start(bf16[32,512]{1,0:T(8,128)(2,1)S(1)} %shard_map.140.a), channel_id=1, source_target_pairs={{0,3},{1,0},{2,1},{3,2},{4,7},{5,4},{6,5},{7,6},{8,11},{9,8},{10,9... | collective-permute-start | bytes 98312 | tf_op jit(solution)/shard_map/ppermute | solution.py:621
  163.5 5.5 %collective-permute-start.21 = (bf16[32,512]{1,0:T(8,128)(2,1)S(1)}, bf16[32,512]{1,0:T(8,128)(2,1)S(1)}, u32[]{:S(2)}, u32[]{:S(2)}) collective-permute-start(bf16[32,512]{1,0:T(8,128)(2,1)S(1)} %shard_map.144.a), channel_id=1, source_target_pairs={{0,2},{1,3},{2,0},{3,1},{4,6},{5,7},{6,4},{7,5},{8,10},{9,11},{10,... | collective-permute-start | bytes 98312 | tf_op jit(solution)/shard_map/ppermute | solution.py:621
  165.2 5.1 %collective-permute-start.22 = (bf16[32,512]{1,0:T(8,128)(2,1)S(1)}, bf16[32,512]{1,0:T(8,128)(2,1)S(1)}, u32[]{:S(2)}, u32[]{:S(2)}) collective-permute-start(bf16[32,512]{1,0:T(8,128)(2,1)S(1)} %shard_map.144.a), channel_id=1, source_target_pairs={{0,1},{1,2},{2,3},{3,0},{4,5},{5,6},{6,7},{7,4},{8,9},{9,10},{10,1... | collective-permute-start | bytes 98312 | tf_op jit(solution)/shard_map/ppermute | solution.py:621
  167.3 3.9 %collective-permute-start.23 = (bf16[32,512]{1,0:T(8,128)(2,1)S(1)}, bf16[32,512]{1,0:T(8,128)(2,1)S(1)}, u32[]{:S(2)}, u32[]{:S(2)}) collective-permute-start(bf16[32,512]{1,0:T(8,128)(2,1)S(1)} %shard_map.144.a), channel_id=1, source_target_pairs={{0,3},{1,0},{2,1},{3,2},{4,7},{5,4},{6,5},{7,6},{8,11},{9,8},{10,9... | collective-permute-start | bytes 98312 | tf_op jit(solution)/shard_map/ppermute | solution.py:621
  (13 other events, 66.4 us)

commit v9 on v8

--- a/solution.py
+++ b/solution.py
@@ -688,15 +688,14 @@
     payload = call(pair_total_kernel, rows_type(side * sent_rows), [VMEM] * 2)(
         keep, from_pair(send, n_req)
     )
-    payload, kv_later, o_later, gate_later, up_later, down_later, q_later = lax.optimization_barrier(
-        (payload, kv_pool, o_weight, gate_weight, up_weight, down_weight, q_weight)
+    payload, kv_later, o_later, gate_later, up_later, down_later = lax.optimization_barrier(
+        (payload, kv_pool, o_weight, gate_weight, up_weight, down_weight)
     )
     pool_other = from_pair(kv_later, n_req)
     o_other = from_pair(o_later, n_req)
     gate_other = from_pair(gate_later, n_req)
     up_other = from_pair(up_later, n_req)
     down_other = from_pair(down_later, n_req)
-    q_other = from_pair(q_later, n_req)
     current, attn_gain, ffn_gain = call(
         pair_state_kernel,
         [pair_type(requests), pair_type(LAYERS), pair_type(LAYERS)],
@@ -796,6 +795,10 @@
             rows_type(n_req * chunk),
             [VMEM],
         )(exchange(payload, n_req))
+        acts = exchange_all(act, n_req)
+        if layer_no == 0:
+            acts, q_later = lax.optimization_barrier((acts, q_weight))
+            q_other = from_pair(q_later, n_req)
         own = call(
             functools.partial(down_kernel, layer_no, f_rows, chunk),
             pair_type(requests),
@@ -805,7 +808,7 @@
                 rows_scratch(n_req * chunk),
                 dma((14, 2)),
             ],
-        )(exchange_all(act, n_req), down_weight, down_other)
+        )(acts, down_weight, down_other)
         parts = tp_parts(own)
     return call(last_kernel, jax.ShapeDtypeStruct(hidden.shape, BF16), [VMEM] * 5)(current, *parts)
 

time: 173 us -> 170 us (0.983)
  blocking collectives: 78.5 us -> 90.7 us
  waiting for transfers between devices: 32.7 us -> 25.1 us
  starting transfers between devices: 34.7 us -> 30.9 us
  Pallas kernels: 24.3 us -> 21 us
    all_to_all x1 -> x2, blocking collectives: 12.1 us -> 24.3 us  [exchange_all(): lax.all_to_all(blocks, 'req', split_axis=0, concat_axis=0, tiled=True)]
    all_to_all x1 -> x0, waiting for transfers between devices: 8.65 us -> none  [exchange_all(): lax.all_to_all(blocks, 'req', split_axis=0, concat_axis=0, tiled=True)]
    all_to_all x1 -> x0, starting transfers between devices: 3.87 us -> none  [exchange_all(): lax.all_to_all(blocks, 'req', split_axis=0, concat_axis=0, tiled=True)]
  transfers between devices with their start and end apart: 26 -> 25, of which waited for: 14 -> 14; matrix products, arithmetic and copies ran while one was open for 0% -> 0% of each run, Pallas kernels for 7% -> 6%
where the time goes in v9:
time: 170 us; the launch traced here: 169 us
  blocking collectives  90.7 us (53%)
  starting transfers between devices  30.9 us (18%)
  waiting for transfers between devices  25.1 us (15%)
  Pallas kernels  21 us (12%)
    all_to_all x5, blocking collectives, exchange(): lax.all_to_all(blocks, 'req', split_axis=0, concat_axis=0, tiled=True, ax...  66.4 us
    all_to_all x2, blocking collectives, exchange_all(): lax.all_to_all(blocks, 'req', split_axis=0, concat_axis=0, tiled=True)  24.3 us
    ppermute x12, starting transfers between devices, tp_parts(): lax.ppermute(partial_sum, 'tp', [(i, (i + shift) % n_tp) for i in range(n...  21.3 us
    all_to_all x1, waiting for transfers between devices, exchange(): lax.all_to_all(blocks, 'req', split_axis=0, concat_axis=0, tiled=True, ax...  12.9 us
    ppermute x12, waiting for transfers between devices, tp_parts(): lax.ppermute(partial_sum, 'tp', [(i, (i + shift) % n_tp) for i in range(n...  8.68 us
    all_to_all x1, starting transfers between devices, exchange(): lax.all_to_all(blocks, 'req', split_axis=0, concat_axis=0, tiled=True, ax...  7.12 us
    pallas_call x1, Pallas kernels, shards(): call(functools.partial(first_block_kernel, side), [rows_type(side * stat_...  3.57 us
    ppermute x12, waiting for transfers between devices, from_pair(): return lax.ppermute(array, 'req', [(i, i ^ 1) for i in range(n_req)])  3.52 us
  transfers between devices with their start and end apart: 25, of which 14 were waited for; matrix products, arithmetic and copies ran while one was open for 0% of the time, Pallas kernels for 6%

profile of v9, /device:TPU:0, one launch (start us, length us, event | category | flops | bytes accessed | tf_op | source)
XLA Modules:
  0.0 169.3 jit_solution(7753123306629261962)
XLA Ops:
  0.0 2.0 %shard_map.128 = (f32[160,128]{1,0:T(8,128)}, bf16[160,128]{1,0:T(8,128)(2,1)}) custom-call(bf16[32,256]{1,0:T(8,128)(2,1)} %x_hbm.1, bf16[2,256]{1,0:T(2,128)(2,1)} %gain_hbm.1, bf16[2,256,1024]{2,1,0:T(8,128)(2,1)} %refs_0_.2, s32[1,32]{1,0:T(1,128)} %homes_hbm.1, s32[2,1,1,24]{3,2,1,0:T(1,128)} %chosen_hbm.1, s32[1,2]{1,0:T(1,128)} %bitcast.32), custom_call_target="tpu_custom_call" | custom-call | flops 10000000000 | tf_op jit(solution)/shard_map/pallas_call | solution.py:665
  6.1 7.1 %all-to-all-start = ((bf16[16,160,128]{2,1,0:T(8,128)(2,1)}), bf16[16,160,128]{2,1,0:T(8,128)(2,1)S(1)}, u32[]{:S(2)}, u32[]{:S(2)}) async-start(bf16[16,160,128]{2,1,0:T(8,128)(2,1)} %bitcast.1), calls=%async_computation | async-start | bytes 1310720 | tf_op jit(solution)/shard_map/all_to_all | solution.py:603
  13.8 12.9 %all-to-all-done = bf16[16,160,128]{2,1,0:T(8,128)(2,1)S(1)} async-done(((bf16[16,160,128]{2,1,0:T(8,128)(2,1)}), bf16[16,160,128]{2,1,0:T(8,128)(2,1)S(1)}, u32[]{:S(2)}, u32[]{:S(2)}) %all-to-all-start) | async-done | bytes 655392 | tf_op jit(solution)/shard_map/all_to_all | solution.py:603
  26.6 3.6 %shard_map.130 = (bf16[2304,128]{1,0:T(8,128)(2,1)S(1)}, f32[32,128]{1,0:T(8,128)S(1)}) custom-call(bf16[2560,128]{1,0:T(8,128)(2,1)S(1)} %bitcast.18, f32[2,128]{1,0:T(2,128)S(1)} %copy-done.8, bf16[2,32,1,2,128,128]{5,4,3,2,1,0:T(8,128)(2,1)} %own_hbm.9, bf16[2,32,1,2,128,128]{5,4,3,2,1,0:T(8,128)(2,1)} %collective-permute-done.4.other_hbm, ...), custom_call_target="tpu_custom_call" | custom-call | flops 10000000000 | tf_op jit(solution)/shard_map/pallas_call | solution.py:739
  30.2 14.9 %all_to_all.40 = bf16[16,144,128]{2,1,0:T(8,128)(2,1)S(1)} all-to-all(bf16[16,144,128]{2,1,0:T(8,128)(2,1)S(1)} %bitcast.21), channel_id=1, replica_groups={{0,8,16,24,32,40,48,56,64,72,80,88,96,104,112,120},{4,12,20,28,36,44,52..., dimensions={0} | all-to-all | bytes 1179648 | tf_op jit(solution)/shard_map/all_to_all | solution.py:603
  48.2 3.9 %collective-permute-start.7 = (bf16[32,512]{1,0:T(8,128)(2,1)S(1)}, bf16[32,512]{1,0:T(8,128)(2,1)S(1)}, u32[]{:S(2)}, u32[]{:S(2)}) collective-permute-start(bf16[32,512]{1,0:T(8,128)(2,1)S(1)} %shard_map.132.a), channel_id=1, source_target_pairs={{0,2},{1,3},{2,0},{3,1},{4,6},{5,7},{6,4},{7,5},{8,10},{9,11},{10,... | collective-permute-start | bytes 98312 | tf_op jit(solution)/shard_map/ppermute | solution.py:621
  53.1 2.2 %collective-permute-start.9 = (bf16[32,512]{1,0:T(8,128)(2,1)S(1)}, bf16[32,512]{1,0:T(8,128)(2,1)S(1)}, u32[]{:S(2)}, u32[]{:S(2)}) collective-permute-start(bf16[32,512]{1,0:T(8,128)(2,1)S(1)} %shard_map.132.a), channel_id=1, source_target_pairs={{0,3},{1,0},{2,1},{3,2},{4,7},{5,4},{6,5},{7,6},{8,11},{9,8},{10,9... | collective-permute-start | bytes 98312 | tf_op jit(solution)/shard_map/ppermute | solution.py:621
  55.4 1.8 %collective-permute-done.8.c = bf16[32,512]{1,0:T(8,128)(2,1)S(1)} collective-permute-done((bf16[32,512]{1,0:T(8,128)(2,1)S(1)}, bf16[32,512]{1,0:T(8,128)(2,1)S(1)}, u32[]{:S(2)}, u32[]{:S(2)}) %collective-permute-start.8) | collective-permute-done | bytes 32800 | tf_op jit(solution)/shard_map/ppermute | solution.py:621
  57.2 2.3 %shard_map.133 = (bf16[32,512]{1,0:T(8,128)(2,1)S(1)}, bf16[1024,128]{1,0:T(8,128)(2,1)S(1)}) custom-call(bf16[32,512]{1,0:T(8,128)(2,1)S(1)} %get-tuple-element.28.x_ref, bf16[32,512]{1,0:T(8,128)(2,1)S(1)} %shard_map.132.a, bf16[32,512]{1,0:T(8,128)(2,1)S(1)} %collective-permute-done.7.b, bf16[32,512]{1,0:T(8,128)(2,1)S(1)} %collective-permute-done.8.c, ...), custom_call_target="tpu_custom_call" | custom-call | flops 10000000000 | tf_op jit(solution)/shard_map/pallas_call | solution.py:781
  59.5 11.8 %all_to_all.41 = bf16[16,64,128]{2,1,0:T(8,128)(2,1)S(1)} all-to-all(bf16[16,64,128]{2,1,0:T(8,128)(2,1)S(1)} %bitcast.26), channel_id=1, replica_groups={{0,8,16,24,32,40,48,56,64,72,80,88,96,104,112,120},{4,12,20,28,36,44,52..., dimensions={0} | all-to-all | bytes 524288 | tf_op jit(solution)/shard_map/all_to_all | solution.py:603
  71.5 12.2 %all_to_all.42 = bf16[32,32,128]{2,1,0:T(8,128)(2,1)S(1)} all-to-all(bf16[32,32,128]{2,1,0:T(8,128)(2,1)S(1)} %bitcast.24), channel_id=1, replica_groups=mesh['req'=32,'tp'=4] {'req'}, dimensions={0} | all-to-all | bytes 524288 | tf_op jit(solution)/shard_map/all_to_all | solution.py:611
  84.0 1.7 shard_map.135.a
  87.2 2.6 %collective-permute-start.14 = (bf16[32,512]{1,0:T(8,128)(2,1)S(1)}, bf16[32,512]{1,0:T(8,128)(2,1)S(1)}, u32[]{:S(2)}, u32[]{:S(2)}) collective-permute-start(bf16[32,512]{1,0:T(8,128)(2,1)S(1)} %shard_map.135.a), channel_id=1, source_target_pairs={{0,1},{1,2},{2,3},{3,0},{4,5},{5,6},{6,7},{7,4},{8,9},{9,10},{10,1... | collective-permute-start | bytes 98312 | tf_op jit(solution)/shard_map/ppermute | solution.py:621
  94.0 14.2 %all_to_all.43 = bf16[16,144,128]{2,1,0:T(8,128)(2,1)S(1)} all-to-all(bf16[16,144,128]{2,1,0:T(8,128)(2,1)S(1)} %bitcast.19), channel_id=1, replica_groups={{0,8,16,24,32,40,48,56,64,72,80,88,96,104,112,120},{4,12,20,28,36,44,52..., dimensions={0} | all-to-all | bytes 1179648 | tf_op jit(solution)/shard_map/all_to_all | solution.py:603
  108.2 3.3 %shard_map.138.refs_4_ = bf16[2304,128]{1,0:T(8,128)(2,1)S(1)} custom-call(bf16[2304,128]{1,0:T(8,128)(2,1)S(1)} %bitcast.20, f32[32,128]{1,0:T(8,128)S(1)} %get-tuple-element.46.table_ref, f32[2,128]{1,0:T(2,128)S(1)} %copy-done.8, bf16[2,32,1,2,128,128]{5,4,3,2,1,0:T(8,128)(2,1)} %own_hbm.9, bf16[2,32,1,2,128,128]{5,4,3,2,1,0:T(8,128)(2,1)} %collective-permute-done.4.other_hbm), custom_call_target="tpu_custom_call" | custom-call | flops 10000000000 | tf_op jit(solution)/shard_map/pallas_call | solution.py:746
  111.6 13.7 %all_to_all.44 = bf16[16,144,128]{2,1,0:T(8,128)(2,1)S(1)} all-to-all(bf16[16,144,128]{2,1,0:T(8,128)(2,1)S(1)} %bitcast.17), channel_id=1, replica_groups={{0,8,16,24,32,40,48,56,64,72,80,88,96,104,112,120},{4,12,20,28,36,44,52..., dimensions={0} | all-to-all | bytes 1179648 | tf_op jit(solution)/shard_map/all_to_all | solution.py:603
  128.8 1.7 collective-permute-start.19
  130.5 1.6 collective-permute-start.20
  132.0 1.6 shard_map.141
  135.3 11.8 %all_to_all.45 = bf16[16,64,128]{2,1,0:T(8,128)(2,1)S(1)} all-to-all(bf16[16,64,128]{2,1,0:T(8,128)(2,1)S(1)} %bitcast.25), channel_id=1, replica_groups={{0,8,16,24,32,40,48,56,64,72,80,88,96,104,112,120},{4,12,20,28,36,44,52..., dimensions={0} | all-to-all | bytes 524288 | tf_op jit(solution)/shard_map/all_to_all | solution.py:603
  147.2 12.1 %all_to_all.46 = bf16[32,32,128]{2,1,0:T(8,128)(2,1)S(1)} all-to-all(bf16[32,32,128]{2,1,0:T(8,128)(2,1)S(1)} %bitcast.31), channel_id=1, replica_groups=mesh['req'=32,'tp'=4] {'req'}, dimensions={0} | all-to-all | bytes 524288 | tf_op jit(solution)/shard_map/all_to_all | solution.py:611
  159.3 1.7 shard_map.144.a
  161.0 1.6 collective-permute-start.21
  162.6 2.1 %collective-permute-start.22 = (bf16[32,512]{1,0:T(8,128)(2,1)S(1)}, bf16[32,512]{1,0:T(8,128)(2,1)S(1)}, u32[]{:S(2)}, u32[]{:S(2)}) collective-permute-start(bf16[32,512]{1,0:T(8,128)(2,1)S(1)} %shard_map.144.a), channel_id=1, source_target_pairs={{0,1},{1,2},{2,3},{3,0},{4,5},{5,6},{6,7},{7,4},{8,9},{9,10},{10,1... | collective-permute-start | bytes 98312 | tf_op jit(solution)/shard_map/ppermute | solution.py:621
  (72 shorter events, 24.7 us)
Async XLA Ops:
  2.0 1.5 collective-permute-start.3
  5.3 21.3 %collective-permute-start.4 = (bf16[2,32,1,2,128,128]{5,4,3,2,1,0:T(8,128)(2,1)}, bf16[2,32,1,2,128,128]{5,4,3,2,1,0:T(8,128)(2,1)}, u32[]{:S(2)}, u32[]{:S(2)}) collective-permute-start(bf16[2,32,1,2,128,128]{5,4,3,2,1,0:T(8,128)(2,1)} %own_hbm.9), channel_id=1, source_target_pairs={{0,4},{4,0},{8,12},{12,8},{16,20},{20,16},{24,28},{28,24},{32,36},... | collective-permute-start | bytes 12582920 | tf_op jit(solution)/shard_map/ppermute | solution.py:615
  5.9 20.7 %collective-permute-start.5 = (bf16[2,1024,256]{2,1,0:T(8,128)(2,1)S(1)}, bf16[2,1024,256]{2,1,0:T(8,128)(2,1)S(1)}, u32[]{:S(2)}, u32[]{:S(2)}) collective-permute-start(bf16[2,1024,256]{2,1,0:T(8,128)(2,1)S(1)} %copy-done.4), channel_id=1, source_target_pairs={{0,4},{4,0},{8,12},{12,8},{16,20},{20,16},{24,28},{28,24},{32,36},... | collective-permute-start | bytes 3145736 | tf_op jit(solution)/shard_map/ppermute | solution.py:615
  6.1 20.6 %all-to-all-start = ((bf16[16,160,128]{2,1,0:T(8,128)(2,1)}), bf16[16,160,128]{2,1,0:T(8,128)(2,1)S(1)}, u32[]{:S(2)}, u32[]{:S(2)}) async-start(bf16[16,160,128]{2,1,0:T(8,128)(2,1)} %bitcast.1), calls=%async_computation | async-start | bytes 1310720 | tf_op jit(solution)/shard_map/all_to_all | solution.py:603
  13.2 39.9 %collective-permute-start.10 = (bf16[2,256,3584]{2,1,0:T(8,128)(2,1)}, bf16[2,256,3584]{2,1,0:T(8,128)(2,1)}, u32[]{:S(2)}, u32[]{:S(2)}) collective-permute-start(bf16[2,256,3584]{2,1,0:T(8,128)(2,1)} %refs_0_.3), channel_id=1, source_target_pairs={{0,4},{4,0},{8,12},{12,8},{16,20},{20,16},{24,28},{28,24},{32,36},... | collective-permute-start | bytes 11010056 | tf_op jit(solution)/shard_map/ppermute | solution.py:615
  13.3 42.0 %collective-permute-start.11 = (bf16[2,256,3584]{2,1,0:T(8,128)(2,1)}, bf16[2,256,3584]{2,1,0:T(8,128)(2,1)}, u32[]{:S(2)}, u32[]{:S(2)}) collective-permute-start(bf16[2,256,3584]{2,1,0:T(8,128)(2,1)} %refs_2_.1), channel_id=1, source_target_pairs={{0,4},{4,0},{8,12},{12,8},{16,20},{20,16},{24,28},{28,24},{32,36},... | collective-permute-start | bytes 11010056 | tf_op jit(solution)/shard_map/ppermute | solution.py:615
  45.7 1.7 %collective-permute-start.6 = (bf16[128,128]{1,0:T(8,128)(2,1)S(1)}, bf16[128,128]{1,0:T(8,128)(2,1)S(1)}, u32[]{:S(2)}, u32[]{:S(2)}) collective-permute-start(bf16[128,128]{1,0:T(8,128)(2,1)S(1)} %shard_map.131.own_ref), channel_id=1, source_target_pairs={{0,4},{4,0},{8,12},{12,8},{16,20},{20,16},{24,28},{28,24},{32,36},... | collective-permute-start | bytes 98312 | tf_op jit(solution)/shard_map/ppermute | solution.py:615
  45.8 1.3 collective-permute-start.1
  46.3 5.8 %collective-permute-start = (bf16[32,256]{1,0:T(8,128)(2,1)S(1)}, bf16[32,256]{1,0:T(8,128)(2,1)S(1)}, u32[]{:S(2)}, u32[]{:S(2)}) collective-permute-start(bf16[32,256]{1,0:T(8,128)(2,1)S(1)} %copy-done.5), channel_id=1, source_target_pairs={{0,4},{4,0},{8,12},{12,8},{16,20},{20,16},{24,28},{28,24},{32,36},... | collective-permute-start | bytes 49160 | tf_op jit(solution)/shard_map/ppermute | solution.py:615
  47.4 36.6 %collective-permute-start.12 = (bf16[2,3584,256]{2,1,0:T(8,128)(2,1)S(1)}, bf16[2,3584,256]{2,1,0:T(8,128)(2,1)S(1)}, u32[]{:S(2)}, u32[]{:S(2)}) collective-permute-start(bf16[2,3584,256]{2,1,0:T(8,128)(2,1)S(1)} %copy-done.2), channel_id=1, source_target_pairs={{0,4},{4,0},{8,12},{12,8},{16,20},{20,16},{24,28},{28,24},{32,36},... | collective-permute-start | bytes 11010056 | tf_op jit(solution)/shard_map/ppermute | solution.py:615
  48.2 7.2 %collective-permute-start.7 = (bf16[32,512]{1,0:T(8,128)(2,1)S(1)}, bf16[32,512]{1,0:T(8,128)(2,1)S(1)}, u32[]{:S(2)}, u32[]{:S(2)}) collective-permute-start(bf16[32,512]{1,0:T(8,128)(2,1)S(1)} %shard_map.132.a), channel_id=1, source_target_pairs={{0,2},{1,3},{2,0},{3,1},{4,6},{5,7},{6,4},{7,5},{8,10},{9,11},{10,... | collective-permute-start | bytes 98312 | tf_op jit(solution)/shard_map/ppermute | solution.py:621
  52.1 5.1 %collective-permute-start.8 = (bf16[32,512]{1,0:T(8,128)(2,1)S(1)}, bf16[32,512]{1,0:T(8,128)(2,1)S(1)}, u32[]{:S(2)}, u32[]{:S(2)}) collective-permute-start(bf16[32,512]{1,0:T(8,128)(2,1)S(1)} %shard_map.132.a), channel_id=1, source_target_pairs={{0,1},{1,2},{2,3},{3,0},{4,5},{5,6},{6,7},{7,4},{8,9},{9,10},{10,1... | collective-permute-start | bytes 98312 | tf_op jit(solution)/shard_map/ppermute | solution.py:621
  53.1 4.1 %collective-permute-start.9 = (bf16[32,512]{1,0:T(8,128)(2,1)S(1)}, bf16[32,512]{1,0:T(8,128)(2,1)S(1)}, u32[]{:S(2)}, u32[]{:S(2)}) collective-permute-start(bf16[32,512]{1,0:T(8,128)(2,1)S(1)} %shard_map.132.a), channel_id=1, source_target_pairs={{0,3},{1,0},{2,1},{3,2},{4,7},{5,4},{6,5},{7,6},{8,11},{9,8},{10,9... | collective-permute-start | bytes 98312 | tf_op jit(solution)/shard_map/ppermute | solution.py:621
  83.7 6.7 %collective-permute-start.16 = (bf16[2,256,1024]{2,1,0:T(8,128)(2,1)S(1)}, bf16[2,256,1024]{2,1,0:T(8,128)(2,1)S(1)}, u32[]{:S(2)}, u32[]{:S(2)}) collective-permute-start(bf16[2,256,1024]{2,1,0:T(8,128)(2,1)S(1)} %copy-done.3), channel_id=1, source_target_pairs={{0,4},{4,0},{8,12},{12,8},{16,20},{20,16},{24,28},{28,24},{32,36},... | collective-permute-start | bytes 3145736 | tf_op jit(solution)/shard_map/ppermute | solution.py:615
  85.7 5.5 %collective-permute-start.13 = (bf16[32,512]{1,0:T(8,128)(2,1)S(1)}, bf16[32,512]{1,0:T(8,128)(2,1)S(1)}, u32[]{:S(2)}, u32[]{:S(2)}) collective-permute-start(bf16[32,512]{1,0:T(8,128)(2,1)S(1)} %shard_map.135.a), channel_id=1, source_target_pairs={{0,2},{1,3},{2,0},{3,1},{4,6},{5,7},{6,4},{7,5},{8,10},{9,11},{10,... | collective-permute-start | bytes 98312 | tf_op jit(solution)/shard_map/ppermute | solution.py:621
  87.2 5.1 %collective-permute-start.14 = (bf16[32,512]{1,0:T(8,128)(2,1)S(1)}, bf16[32,512]{1,0:T(8,128)(2,1)S(1)}, u32[]{:S(2)}, u32[]{:S(2)}) collective-permute-start(bf16[32,512]{1,0:T(8,128)(2,1)S(1)} %shard_map.135.a), channel_id=1, source_target_pairs={{0,1},{1,2},{2,3},{3,0},{4,5},{5,6},{6,7},{7,4},{8,9},{9,10},{10,1... | collective-permute-start | bytes 98312 | tf_op jit(solution)/shard_map/ppermute | solution.py:621
  89.8 3.9 %collective-permute-start.15 = (bf16[32,512]{1,0:T(8,128)(2,1)S(1)}, bf16[32,512]{1,0:T(8,128)(2,1)S(1)}, u32[]{:S(2)}, u32[]{:S(2)}) collective-permute-start(bf16[32,512]{1,0:T(8,128)(2,1)S(1)} %shard_map.135.a), channel_id=1, source_target_pairs={{0,3},{1,0},{2,1},{3,2},{4,7},{5,4},{6,5},{7,6},{8,11},{9,8},{10,9... | collective-permute-start | bytes 98312 | tf_op jit(solution)/shard_map/ppermute | solution.py:621
  125.8 1.3 collective-permute-start.17
  127.5 6.1 %collective-permute-start.18 = (bf16[32,512]{1,0:T(8,128)(2,1)S(1)}, bf16[32,512]{1,0:T(8,128)(2,1)S(1)}, u32[]{:S(2)}, u32[]{:S(2)}) collective-permute-start(bf16[32,512]{1,0:T(8,128)(2,1)S(1)} %shard_map.140.a), channel_id=1, source_target_pairs={{0,2},{1,3},{2,0},{3,1},{4,6},{5,7},{6,4},{7,5},{8,10},{9,11},{10,... | collective-permute-start | bytes 98312 | tf_op jit(solution)/shard_map/ppermute | solution.py:621
  128.8 5.1 %collective-permute-start.19 = (bf16[32,512]{1,0:T(8,128)(2,1)S(1)}, bf16[32,512]{1,0:T(8,128)(2,1)S(1)}, u32[]{:S(2)}, u32[]{:S(2)}) collective-permute-start(bf16[32,512]{1,0:T(8,128)(2,1)S(1)} %shard_map.140.a), channel_id=1, source_target_pairs={{0,1},{1,2},{2,3},{3,0},{4,5},{5,6},{6,7},{7,4},{8,9},{9,10},{10,1... | collective-permute-start | bytes 98312 | tf_op jit(solution)/shard_map/ppermute | solution.py:621
  130.5 3.9 %collective-permute-start.20 = (bf16[32,512]{1,0:T(8,128)(2,1)S(1)}, bf16[32,512]{1,0:T(8,128)(2,1)S(1)}, u32[]{:S(2)}, u32[]{:S(2)}) collective-permute-start(bf16[32,512]{1,0:T(8,128)(2,1)S(1)} %shard_map.140.a), channel_id=1, source_target_pairs={{0,3},{1,0},{2,1},{3,2},{4,7},{5,4},{6,5},{7,6},{8,11},{9,8},{10,9... | collective-permute-start | bytes 98312 | tf_op jit(solution)/shard_map/ppermute | solution.py:621
  161.0 5.6 %collective-permute-start.21 = (bf16[32,512]{1,0:T(8,128)(2,1)S(1)}, bf16[32,512]{1,0:T(8,128)(2,1)S(1)}, u32[]{:S(2)}, u32[]{:S(2)}) collective-permute-start(bf16[32,512]{1,0:T(8,128)(2,1)S(1)} %shard_map.144.a), channel_id=1, source_target_pairs={{0,2},{1,3},{2,0},{3,1},{4,6},{5,7},{6,4},{7,5},{8,10},{9,11},{10,... | collective-permute-start | bytes 98312 | tf_op jit(solution)/shard_map/ppermute | solution.py:621
  162.6 5.1 %collective-permute-start.22 = (bf16[32,512]{1,0:T(8,128)(2,1)S(1)}, bf16[32,512]{1,0:T(8,128)(2,1)S(1)}, u32[]{:S(2)}, u32[]{:S(2)}) collective-permute-start(bf16[32,512]{1,0:T(8,128)(2,1)S(1)} %shard_map.144.a), channel_id=1, source_target_pairs={{0,1},{1,2},{2,3},{3,0},{4,5},{5,6},{6,7},{7,4},{8,9},{9,10},{10,1... | collective-permute-start | bytes 98312 | tf_op jit(solution)/shard_map/ppermute | solution.py:621
  164.7 3.9 %collective-permute-start.23 = (bf16[32,512]{1,0:T(8,128)(2,1)S(1)}, bf16[32,512]{1,0:T(8,128)(2,1)S(1)}, u32[]{:S(2)}, u32[]{:S(2)}) collective-permute-start(bf16[32,512]{1,0:T(8,128)(2,1)S(1)} %shard_map.144.a), channel_id=1, source_target_pairs={{0,3},{1,0},{2,1},{3,2},{4,7},{5,4},{6,5},{7,6},{8,11},{9,8},{10,9... | collective-permute-start | bytes 98312 | tf_op jit(solution)/shard_map/ppermute | solution.py:621
  (11 other events, 62.6 us)
